TPU v7x, 32 devices: a whole 2x2x4 slice. The times are simulated.
32 devices in a mesh: dp: 8 (over z, y), tensor: 4 (over x, core).
Axes of the slice: x: 2, y: 2, z: 4, core: 2. Of those that a mesh axis runs over, the one named last changes fastest.
Arguments:
- cotangent: bfloat16 [4096, 4608], P(('dp', 'tensor')), may hold values from -6 to 6
- attn_saved: bfloat16 [4096, 2048], P('dp', 'tensor'), may hold values from -6 to 6
- attn_next: bfloat16 [4096, 2048], P('dp', 'tensor'), may hold values from -6 to 6
- weight: bfloat16 [4608, 2048], P('dp', 'tensor'), may hold values from -0.125 to 0.125
- moment1: float32 [4608, 2048], P('dp', 'tensor'), may hold values from -6 to 6
- moment2: float32 [4608, 2048], P('dp', 'tensor'), may hold values from 0.1 to 10
Outputs:
- grad_attn: bfloat16 [4096, 2048], P('dp', 'tensor')
- new_weight: bfloat16 [4608, 2048], P('dp', 'tensor')
- new_moment1: float32 [4608, 2048], P('dp', 'tensor')
- new_moment2: float32 [4608, 2048], P('dp', 'tensor')
- next_out: bfloat16 [4096, 4608], P(('dp', 'tensor'))
All inputs are finite; a program needn't handle non-finite values.
Results may differ from a plain program's by a relative error of at most 0.013.
Values may be sent and summed in bfloat16 or wider, within the bound.
No kernel may reach another device: no remote copies, remote signals or barrier semaphores. Data moves between devices by JAX's collectives and lax.ppermute only.
A program may use at most 128 MiB of HBM per device.

v0:
```python
import math

import jax
import jax.numpy as jnp
from jax import lax
from jax.sharding import PartitionSpec as P

first_decay = 0.9
second_decay = 0.95
first_fix = 1.0 - 0.9**10
second_fix = 1.0 - 0.95**10
learning_rate = 0.002
weight_decay = 0.1
epsilon = 1e-08


def adamw_step(gradient, weight, moment1, moment2):
    new_moment1 = first_decay * moment1 + (1.0 - first_decay) * gradient
    new_moment2 = second_decay * moment2 + (1.0 - second_decay) * gradient * gradient
    update = new_moment1 / first_fix / (jnp.sqrt(new_moment2 / second_fix) + epsilon)
    new_weight = (
        weight.astype(jnp.float32) * (1.0 - learning_rate * weight_decay) - learning_rate * update
    ).astype(jnp.bfloat16)
    return (new_weight, new_moment1, new_moment2)


def local(cotangent, attn_saved, attn_next, weight, moment1, moment2):
    gathered = lax.all_gather(cotangent, "tensor", axis=0, tiled=True)
    tok_rows = gathered.shape[0]
    scale = 1.0 / math.sqrt(tok_rows * lax.axis_size("dp"))
    columns = gathered
    grad_attn = jnp.dot(
        columns,
        lax.all_gather(weight, "dp", axis=0, tiled=True),
        preferred_element_type=jnp.float32,
    ).astype(jnp.bfloat16)
    columns = gathered
    product = lax.dot_general(
        columns, attn_saved, (((0,), (0,)), ((), ())), preferred_element_type=jnp.float32
    )
    gradient = lax.psum_scatter(product * scale, "dp", scatter_dimension=0, tiled=True)
    new_weight, new_moment1, new_moment2 = adamw_step(gradient, weight, moment1, moment2)
    partial_out = lax.dot_general(
        attn_next,
        lax.all_gather(new_weight, "dp", axis=0, tiled=True),
        (((1,), (1,)), ((), ())),
        preferred_element_type=jnp.float32,
    )
    next_out = lax.psum_scatter(
        partial_out.astype(jnp.bfloat16), "tensor", scatter_dimension=0, tiled=True
    )
    return (grad_attn, new_weight, new_moment1, new_moment2, next_out)


def solution(mesh):
    return jax.shard_map(
        local,
        mesh=mesh,
        in_specs=(
            P(("dp", "tensor"), None),
            P("dp", "tensor"),
            P("dp", "tensor"),
            P("dp", "tensor"),
            P("dp", "tensor"),
            P("dp", "tensor"),
        ),
        out_specs=(
            P("dp", "tensor"),
            P("dp", "tensor"),
            P("dp", "tensor"),
            P("dp", "tensor"),
            P(("dp", "tensor"), None),
        ),
        check_vma=False,
    )
```

profile of v0, /device:TPU:0, one launch (start us, length us, event | category | flops | bytes accessed | tf_op | source)
XLA Modules:
  0.0 439.3 jit_solution(9607447278694332474)
XLA Ops:
  7.2 0.0 copy-start
  7.2 0.0 all-gather.4.cloned.1.call-start
  7.2 0.7 all-gather.4.cloned.1.call-update
  7.9 0.0 reduce-scatter.5.cloned.1.call-start
  8.0 41.8 %all-gather.4.cloned.1.call-done = bf16[512,4608]{1,0:T(8,128)(2,1)} async-done(((bf16[128,4608]{1,0:T(8,128)(2,1)}), bf16[512,4608]{1,0:T(8,128)(2,1)}) %all-gather.4.cloned.1.call-update) | async-done | bytes 4718608 | tf_op jit(solution)/shard_map/all_gather | solution.py:28
  49.8 0.0 copy-done
  49.8 7.5 %convolution_multiply_fusion = f32[4608,512]{1,0:T(8,128)} fusion(bf16[512,4608]{1,0:T(8,128)(2,1)} %all-gather.4.cloned.1.call-done, bf16[512,512]{1,0:T(8,128)(2,1)S(1)} %copy-done), kind=kOutput, calls=%fused_computation | convolution fusion | flops 2418278400 | bytes 14680064 | tf_op jit(solution)/shard_map/dot_general | solution.py:38
  57.3 0.0 copy-start.1
  57.3 0.0 copy-start.2
  57.3 0.0 copy-start.3
  57.3 0.0 reduce-scatter.5.cloned.1.call-update
  57.3 0.0 all-gather.8.cloned.1.call-start
  57.4 163.5 %reduce-scatter.5.cloned.1.call-done = f32[576,512]{1,0:T(8,128)} async-done(((f32[4608,512]{1,0:T(8,128)}), f32[576,512]{1,0:T(8,128)}) %reduce-scatter.5.cloned.1.call-update) | async-done | bytes 1179664 | tf_op jit(solution)/shard_map/reduce_scatter | solution.py:41
  220.9 0.0 copy-done.1
  220.9 0.0 copy-done.2
  220.9 0.0 copy-done.3
  220.9 3.6 subtract_convert_fusion
  224.5 0.0 copy-start.4
  224.5 0.0 all-gather.8.cloned.1.call-update
  224.5 0.0 all-gather.6.cloned.1.call-start
  224.6 0.5 all-gather.6.cloned.1.call-update
  225.1 0.0 reduce-scatter.7.cloned.1.call-start
  225.1 78.5 %all-gather.8.cloned.1.call-done = bf16[4608,512]{1,0:T(8,128)(2,1)} async-done(((bf16[576,512]{1,0:T(8,128)(2,1)}), bf16[4608,512]{1,0:T(8,128)(2,1)}) %all-gather.8.cloned.1.call-update) | async-done | bytes 4718608 | tf_op jit(solution)/shard_map/all_gather | solution.py:45
  303.7 0.0 copy-done.4
  303.7 6.7 %fusion = bf16[512,4608]{0,1:T(8,128)(2,1)} fusion(bf16[4608,512]{1,0:T(8,128)(2,1)} %all-gather.8.cloned.1.call-done, bf16[512,512]{1,0:T(8,128)(2,1)S(1)} %copy-done.4), kind=kOutput, calls=%fused_computation.2 | convolution fusion | flops 2418278400 | bytes 9961472 | tf_op jit(solution)/shard_map/dot_general | solution.py:43
  310.3 6.9 %copy.13 = bf16[512,4608]{1,0:T(8,128)(2,1)} copy(bf16[512,4608]{0,1:T(8,128)(2,1)} %fusion) | data formatting | bytes 9437184
  317.2 0.0 reduce-scatter.7.cloned.1.call-update
  317.2 66.5 %all-gather.6.cloned.1.call-done = bf16[4608,512]{1,0:T(8,128)(2,1)} async-done(((bf16[576,512]{1,0:T(8,128)(2,1)}), bf16[4608,512]{1,0:T(8,128)(2,1)}) %all-gather.6.cloned.1.call-update) | async-done | bytes 4718608 | tf_op jit(solution)/shard_map/all_gather | solution.py:34
  383.8 7.2 %convolution_convert_fusion.1 = bf16[512,512]{1,0:T(8,128)(2,1)} fusion(bf16[512,4608]{1,0:T(8,128)(2,1)} %all-gather.4.cloned.1.call-done, bf16[4608,512]{1,0:T(8,128)(2,1)} %all-gather.6.cloned.1.call-done), kind=kOutput, calls=%fused_computation.4 | convolution fusion | flops 2416181248 | bytes 9961472 | tf_op jit(solution)/shard_map/dot_general | solution.py:32
  390.9 41.8 %reduce-scatter.7.cloned.1.call-done = bf16[128,4608]{1,0:T(8,128)(2,1)} async-done(((bf16[512,4608]{1,0:T(8,128)(2,1)}), bf16[128,4608]{1,0:T(8,128)(2,1)}) %reduce-scatter.7.cloned.1.call-update) | async-done | bytes 1179664
Async XLA Ops:
  7.2 42.6 %copy-start = (bf16[512,512]{1,0:T(8,128)(2,1)S(1)}, bf16[512,512]{1,0:T(8,128)(2,1)}, u32[]{:S(2)}) copy-start(bf16[512,512]{1,0:T(8,128)(2,1)} %param.7) | copy-start | bytes 1572868
  7.2 42.6 %all-gather.4.cloned.1.call-start = ((), (), s32[]{:S(2)}) async-start(), calls=%async_computation.2 | async-start | bytes 5898240 | tf_op jit(solution)/shard_map/all_gather | solution.py:28
  7.9 213.0 %reduce-scatter.5.cloned.1.call-start = ((), (), s32[]{:S(2)}) async-start(), calls=%async_computation.4 | async-start | bytes 10616832 | tf_op jit(solution)/shard_map/reduce_scatter | solution.py:41
  57.3 163.6 %copy-start.1 = (bf16[576,512]{1,0:T(8,128)(2,1)S(1)}, bf16[576,512]{1,0:T(8,128)(2,1)}, u32[]{:S(2)}) copy-start(bf16[576,512]{1,0:T(8,128)(2,1)} %param.9) | copy-start | bytes 1769476
  57.3 163.6 %copy-start.2 = (f32[576,512]{1,0:T(8,128)S(1)}, f32[576,512]{1,0:T(8,128)}, u32[]{:S(2)}) copy-start(f32[576,512]{1,0:T(8,128)} %param.10) | copy-start | bytes 3538948
  57.3 163.6 %copy-start.3 = (f32[576,512]{1,0:T(8,128)S(1)}, f32[576,512]{1,0:T(8,128)}, u32[]{:S(2)}) copy-start(f32[576,512]{1,0:T(8,128)} %param.11) | copy-start | bytes 3538948
  57.3 246.3 %all-gather.8.cloned.1.call-start = ((), (), s32[]{:S(2)}) async-start(), calls=%async_computation.5 | async-start | bytes 5308416 | tf_op jit(solution)/shard_map/all_gather | solution.py:45
  224.5 79.2 %copy-start.4 = (bf16[512,512]{1,0:T(8,128)(2,1)S(1)}, bf16[512,512]{1,0:T(8,128)(2,1)}, u32[]{:S(2)}) copy-start(bf16[512,512]{1,0:T(8,128)(2,1)} %param.8) | copy-start | bytes 1572868
  224.5 159.2 %all-gather.6.cloned.1.call-start = ((), (), s32[]{:S(2)}) async-start(), calls=%async_computation.3 | async-start | bytes 5308416 | tf_op jit(solution)/shard_map/all_gather | solution.py:34
  225.1 207.6 %reduce-scatter.7.cloned.1.call-start = ((), (), s32[]{:S(2)}) async-start(), calls=%async_computation.6 | async-start | bytes 5898240
Sparse Core Ops, SparseCore 0:
  9.6 40.1 all-gather.3
  57.4 163.4 reduce-scatter.4
  224.6 78.9 all-gather.7
  305.7 78.0 all-gather.5
  386.7 45.9 reduce-scatter.6
where the time goes:
time: 440 us; the launch traced here: 439 us
  waiting for transfers between devices  393 us (89%)
  matrix products  21.3 us (5%)
  between operations  13.8 us (3%)
  local copies, waits for them, and re-layouts  6.89 us (2%)
    reduce_scatter x1, waiting for transfers between devices, local(): lax.psum_scatter(product * scale, 'dp', scatter_dimension=0, tiled=True)  164 us
    all_gather x1, waiting for transfers between devices, local(): lax.all_gather(new_weight, 'dp', axis=0, tiled=True)  78.5 us
    all_gather x1, waiting for transfers between devices, local(): lax.all_gather(weight, 'dp', axis=0, tiled=True)  66.5 us
    unnamed x6, waiting for transfers between devices  43.1 us
    all_gather x1, waiting for transfers between devices, local(): gathered = lax.all_gather(cotangent, 'tensor', axis=0, tiled=True)  41.8 us
  transfers between devices with their start and end apart: 5, of which 5 were waited for; matrix products, arithmetic and copies ran while one was open for 5% of the time, Pallas kernels for 0%

commit v1 on v0

v1 whole, which is shorter than its diff:
```python
import functools
import math

import jax
import jax.numpy as jnp
from jax import lax
from jax.experimental import pallas as pl
from jax.experimental.pallas import tpu as pltpu
from jax.sharding import PartitionSpec as P

first_decay = 0.9
second_decay = 0.95
first_fix = 1.0 - 0.9**10
second_fix = 1.0 - 0.95**10
learning_rate = 0.002
weight_decay = 0.1
epsilon = 1e-08
bf16 = jnp.bfloat16
f32 = jnp.float32
VMEM_LIMIT = 48 * 2**20


def adamw_step(gradient, weight, moment1, moment2):
    new_moment1 = first_decay * moment1 + (1.0 - first_decay) * gradient
    new_moment2 = second_decay * moment2 + (1.0 - second_decay) * gradient * gradient
    update = new_moment1 / first_fix / (jnp.sqrt(new_moment2 / second_fix) + epsilon)
    new_weight = (
        weight.astype(f32) * (1.0 - learning_rate * weight_decay) - learning_rate * update
    ).astype(bf16)
    return (new_weight, new_moment1, new_moment2)


def flip(value, axis, bit):
    return lax.ppermute(value, axis, [(i, i ^ bit) for i in range(lax.axis_size(axis))])


def to_partner(value):
    return flip(value, "dp", 1)


def to_chip(value):
    return flip(value, "tensor", 2)


def to_core(value):
    return flip(value, "tensor", 1)


def up(value, step, n):
    pairs = [(2 * z + y, 2 * z + 2 + y) for z in range(n - 1) for y in range(2) if step(z)]
    return lax.ppermute(value, "dp", pairs)


def down(value, step, n):
    pairs = [(2 * z + 2 + y, 2 * z + y) for z in range(n - 1) for y in range(2) if step(n - 2 - z)]
    return lax.ppermute(value, "dp", pairs)


def stage(*values):
    return lax.optimization_barrier(values)


def arrivals(n):
    table = []
    for z in range(n):
        steps = [(d, s) for s in range(1, n) for d in (1, -1) if 0 <= z - d * s < n]
        table.append(steps)
    return table


def pick(z, choices):
    result, seen = choices[-1], [choices[-1]]
    for value in reversed(choices):
        if not any(value is other for other in seen):
            seen.append(value)
            hit = functools.reduce(jnp.logical_or, [z == j for j, v in enumerate(choices) if v is value])
            result = jnp.where(hit, value, result)
    return result


def relative(rows, x, c):
    block = rows.shape[0] // 4
    rows = rows.reshape(2, 2, block, rows.shape[1])
    rows = jnp.where(x == 1, rows[::-1], rows)
    rows = jnp.where(c == 1, rows[:, ::-1], rows)
    return rows.transpose(1, 0, 2, 3).reshape(4 * block, -1)


def absolute(rows, x, c):
    block = rows.shape[0] // 4
    rows = rows.reshape(2, 2, block, -1).transpose(1, 0, 2, 3)
    rows = jnp.where(c == 1, rows[:, ::-1], rows)
    rows = jnp.where(x == 1, rows[::-1], rows)
    return rows.reshape(4 * block, -1)


def params():
    return pltpu.CompilerParams(vmem_limit_bytes=VMEM_LIMIT)


def cost(flops, bytes_accessed):
    return pl.CostEstimate(flops=flops, bytes_accessed=bytes_accessed, transcendentals=0)


def gradient_kernel(scale, *refs):
    pieces, (saved0, saved1, out) = refs[:8], refs[8:]
    rows = saved0.shape[0]
    left = jnp.concatenate([ref[0] for ref in pieces], axis=1)
    total = jnp.dot(left[:, :rows], saved0[...], preferred_element_type=f32)
    total += jnp.dot(left[:, rows:], saved1[...], preferred_element_type=f32)
    out[0] = (total * scale).astype(bf16)


def gradient_part(pieces, saved0, saved1, first, count, scale):
    _, own, tok = pieces[0].shape
    rows, wide = saved0.shape
    whole = pl.BlockSpec((rows, wide), lambda i: (0, 0))
    return pl.pallas_call(
        functools.partial(gradient_kernel, scale),
        grid=(count,),
        in_specs=[pl.BlockSpec((1, own, tok), lambda i: (i + first, 0, 0))] * 8 + [whole] * 2,
        out_specs=pl.BlockSpec((1, own, wide), lambda i: (i, 0, 0)),
        out_shape=jax.ShapeDtypeStruct((count, own, wide), bf16),
        compiler_params=params(),
        cost_estimate=cost(2 * count * own * 2 * rows * wide, 2 * count * own * (2 * rows + wide) + 4 * rows * wide),
        name="gradient_part",
    )(*pieces, saved0, saved1)


def attn_kernel(*refs):
    pieces, (weights, kept, sent, total) = refs[:8], refs[8:]
    step = pl.program_id(0)
    rows = kept.shape[0]
    left = jnp.concatenate([ref[0] for ref in pieces], axis=1)
    product = lax.dot_general(left, weights[0], (((0,), (0,)), ((), ())), preferred_element_type=f32)

    @pl.when(step == 0)
    def _():
        total[...] = product

    @pl.when(step > 0)
    def _():
        total[...] += product

    @pl.when(step == pl.num_programs(0) - 1)
    def _():
        kept[...] = total[:rows]
        sent[...] = total[rows:].astype(bf16)


def attn_part(pieces, weights):
    n, own, tok = pieces[0].shape
    wide = weights.shape[2]
    rows = 4 * tok
    whole = pl.BlockSpec((rows, wide), lambda i: (0, 0))
    return pl.pallas_call(
        attn_kernel,
        grid=(n,),
        in_specs=[pl.BlockSpec((1, own, tok), lambda i: (i, 0, 0))] * 8
        + [pl.BlockSpec((1, own, wide), lambda i: (i, 0, 0))],
        out_specs=[whole, whole],
        out_shape=[jax.ShapeDtypeStruct((rows, wide), f32), jax.ShapeDtypeStruct((rows, wide), bf16)],
        scratch_shapes=[pltpu.VMEM((2 * rows, wide), f32)],
        compiler_params=params(),
        cost_estimate=cost(4 * n * own * rows * wide, 2 * n * own * (2 * rows + wide) + 6 * rows * wide),
        name="attn_part",
    )(*pieces, weights)


def outward_kernel(block, next0, next1, kept, sent):
    tok = kept.shape[3]
    for y, following in enumerate((next0, next1)):
        out = lax.dot_general(
            block[...], following[...], (((1,), (1,)), ((), ())), preferred_element_type=f32
        ).astype(bf16)
        for chip in range(2):
            kept[chip, y] = out[:, chip * tok : (chip + 1) * tok]
            sent[chip, y] = out[:, (2 + chip) * tok : (3 + chip) * tok]


def outward_part(block, next0, next1):
    own, wide = block.shape
    rows = next0.shape[0]
    shape = jax.ShapeDtypeStruct((2, 2, own, rows // 4), bf16)
    return pl.pallas_call(
        outward_kernel,
        out_shape=[shape, shape],
        compiler_params=params(),
        cost_estimate=cost(4 * own * rows * wide, 2 * (own * wide + 2 * rows * wide + 2 * own * rows)),
        name="outward_part",
    )(block, next0, next1)


def add(a, b):
    return (a.astype(f32) + b.astype(f32)).astype(bf16)


def local(cotangent, attn_saved, attn_next, weight, moment1, moment2):
    dp, t = lax.axis_index("dp"), lax.axis_index("tensor")
    n = lax.axis_size("dp") // 2
    z, y, x, c = dp // 2, dp % 2, t // 2, t % 2
    own, wide = weight.shape
    tok = cotangent.shape[0]
    scale = 1.0 / math.sqrt(4 * tok * lax.axis_size("dp"))
    order = [r for k in range(1, n // 2 + 1) for r in dict.fromkeys((k, n - k))] + [0]
    half = n // 2

    blocks = cotangent.T.reshape(n, 2, own, tok)
    blocks = jnp.take(blocks, (z + jnp.array(order)) % n, axis=0)
    mine = jnp.where(y == 0, blocks[:, 0], blocks[:, 1])
    other = jnp.where(y == 0, blocks[:, 1], blocks[:, 0])
    saved0 = relative(attn_saved, x, c)

    weights = {(1, 0): weight, (-1, 0): weight}

    def weight_step(s):
        weights[1, s] = up(weights[1, s - 1], lambda a: a >= s - 1, n)
        weights[-1, s] = down(weights[-1, s - 1], lambda a: a >= s - 1, n)

    other, mine, weight0 = stage(other, mine, weight)
    weights[1, 0] = weights[-1, 0] = weight0
    partner = to_partner(other)
    mine_x = to_chip(mine)
    mine_c = to_core(mine)
    weight_step(1)
    partner, mine_x, mine_c, weights[1, 1], weights[-1, 1], saved0 = stage(
        partner, mine_x, mine_c, weights[1, 1], weights[-1, 1], saved0
    )
    saved1 = to_partner(saved0)
    partner_x = to_chip(partner)
    partner_c = to_core(partner)
    mine_xc = to_core(mine_x)
    if n > 2:
        weight_step(2)
    else:
        weights[1, 2] = weights[-1, 2] = weight
    saved1, partner_x, partner_c, mine_xc, weights[1, 2], weights[-1, 2] = stage(
        saved1, partner_x, partner_c, mine_xc, weights[1, 2], weights[-1, 2]
    )
    partner_xc = to_core(partner_x)
    pieces = [mine, mine_x, mine_c, mine_xc, partner, partner_x, partner_c, partner_xc]

    first = gradient_part(pieces, saved0, saved1, 0, half, scale)
    parts = {r: first[j] for j, r in enumerate(order[:half])}
    next0 = relative(attn_next, x, c)

    rising, falling = parts[n - 1], parts[1]
    for s in range(1, n):
        rising = up(rising, lambda a: a <= s - 1, n)
        falling = down(falling, lambda a: a <= s - 1, n)
        if s == 1:
            next1 = to_partner(next0)
            second = gradient_part(pieces, saved0, saved1, half, n - half, scale)
            rising, falling, next1, second = stage(rising, falling, next1, second)
            parts.update({r: second[j] for j, r in enumerate(order[half:])})
        if s + 2 < n:
            weight_step(s + 2)
            rising, falling, weights[1, s + 2], weights[-1, s + 2] = stage(
                rising, falling, weights[1, s + 2], weights[-1, s + 2]
            )
        if s == n - 2:
            gathered = jnp.stack(
                [jnp.where(z >= n - r, weights[1, n - r], weights[-1, r]) if r else weight for r in order]
            )
            kept, sent = attn_part(pieces, gathered)
            rising, falling, kept, sent = stage(rising, falling, kept, sent)
        if s < n - 1:
            rising = add(rising, parts[n - s - 1])
            falling = add(falling, parts[s + 1])
    sent = to_partner(sent)
    rising, falling, sent = stage(rising, falling, sent)
    gradient = parts[0].astype(f32) + rising.astype(f32) + falling.astype(f32)
    new_weight, new_moment1, new_moment2 = adamw_step(gradient, weight, moment1, moment2)
    grad_attn = absolute((kept + sent.astype(f32)).astype(bf16), x, c)

    table = arrivals(n)
    news = {(1, 0): new_weight, (-1, 0): new_weight}
    block, results, pending = new_weight, [], None
    for s in range(1, n + 1):
        if s < n:
            news[1, s] = up(news[1, s - 1], lambda a: a >= s - 1, n)
            news[-1, s] = down(news[-1, s - 1], lambda a: a >= s - 1, n)
        kept, sent = outward_part(block, next0, next1)
        half_sum = add(kept, to_core(sent))
        sums = add(half_sum[0], to_chip(half_sum[1]))
        if pending is not None:
            results.append((pending[0], to_partner(pending[1])))
        if s < n:
            sums, news[1, s], news[-1, s] = stage(sums, news[1, s], news[-1, s])
            block = pick(z, [news[steps[s - 1]] for steps in table])
        pending = sums
    results.append((pending[0], to_partner(pending[1])))

    mine = jnp.stack([m for m, _ in results])
    other = jnp.stack([o for _, o in results])
    halves = jnp.stack([jnp.where(y == 0, mine, other), jnp.where(y == 0, other, mine)], axis=1)
    slots = [[0] * n for _ in range(n)]
    for plane in range(n):
        for k, (d, s) in enumerate(table[plane]):
            slots[plane][plane - d * s] = k + 1
    next_out = jnp.take(halves, jnp.array(slots)[z], axis=0).reshape(2 * n * own, tok).T
    return (grad_attn, new_weight, new_moment1, new_moment2, next_out)


def solution(mesh):
    return jax.shard_map(
        local,
        mesh=mesh,
        in_specs=(
            P(("dp", "tensor"), None),
            P("dp", "tensor"),
            P("dp", "tensor"),
            P("dp", "tensor"),
            P("dp", "tensor"),
            P("dp", "tensor"),
        ),
        out_specs=(
            P("dp", "tensor"),
            P("dp", "tensor"),
            P("dp", "tensor"),
            P("dp", "tensor"),
            P(("dp", "tensor"), None),
        ),
        check_vma=False,
    )
```

time: 440 us -> 218 us (0.50)
  waiting for transfers between devices: 393 us -> 106 us
  starting transfers between devices: 0.2 us -> 60.8 us
  matrix products: 21.3 us -> 0 us
  Pallas kernels: 0 us -> 20.2 us
  other arithmetic: 3.58 us -> 17.5 us
  between operations: 13.8 us -> 1.33 us
  local copies, waits for them, and re-layouts: 6.89 us -> 11.3 us
    all_gather x3 -> x0, waiting for transfers between devices: 187 us -> none  [the longest x1 78.5 us: local(): lax.all_gather(new_weight, 'dp', axis=0, tiled=True)]
    reduce_scatter x1 -> x0, waiting for transfers between devices: 164 us -> none  [local(): lax.psum_scatter(product * scale, 'dp', scatter_dimension=0, tiled=True)]
    ppermute x0 -> x40, waiting for transfers between devices: none -> 106 us  [the longest x22 73.5 us: flip(): lax.ppermute(value, axis, [(i, i ^ bit) for i in range(lax.axis_size(axis...]
    ppermute x0 -> x40, starting transfers between devices: none -> 60.8 us  [the longest x9 36.2 us: up(): return lax.ppermute(value, 'dp', pairs)]
    unnamed x6 -> x0, waiting for transfers between devices: 43.1 us -> none
    dot_general x3 -> x0, matrix products: 21.3 us -> none  [the longest x1 7.53 us: local(): lax.dot_general(columns, attn_saved, (((0,), (0,)), ((), ())), preferred_...]
    pallas_call x0 -> x7, Pallas kernels: none -> 20.2 us  [the longest x4 8.35 us: outward_part(): pl.pallas_call(outward_kernel, out_shape=[shape, shape], compiler_params=...]
    another operation x0 -> x5, other arithmetic: none -> 5.39 us  [the longest x4 5.28 us: local(): jnp.stack([jnp.where(z >= n - r, weights[1, n - r], weights[-1, r]) if r...]
  transfers between devices with their start and end apart: 5 -> 40, of which waited for: 5 -> 20; matrix products, arithmetic and copies ran while one was open for 5% -> 6% of each run, Pallas kernels for 0% -> 5%
where the time goes in v1:
time: 218 us
  waiting for transfers between devices  106 us (49%)
  starting transfers between devices  60.8 us (28%)
  Pallas kernels  20.2 us (9%)
  other arithmetic  17.5 us (8%)
  local copies, waits for them, and re-layouts  11.3 us (5%)
    ppermute x22, waiting for transfers between devices, flip(): lax.ppermute(value, axis, [(i, i ^ bit) for i in range(lax.axis_size(axis...  73.5 us
    ppermute x9, starting transfers between devices, up(): return lax.ppermute(value, 'dp', pairs)  36.2 us
    ppermute x9, waiting for transfers between devices, down(): return lax.ppermute(value, 'dp', pairs)  26.6 us
    ppermute x22, starting transfers between devices, flip(): lax.ppermute(value, axis, [(i, i ^ bit) for i in range(lax.axis_size(axis...  13.2 us
    ppermute x9, starting transfers between devices, down(): return lax.ppermute(value, 'dp', pairs)  11.4 us
    pallas_call x4, Pallas kernels, outward_part(): pl.pallas_call(outward_kernel, out_shape=[shape, shape], compiler_params=...  8.35 us
    pallas_call x1, Pallas kernels, attn_part(): pl.pallas_call(attn_kernel, grid=(n,), in_specs=[pl.BlockSpec((1, own, to...  7.04 us
    ppermute x9, waiting for transfers between devices, up(): return lax.ppermute(value, 'dp', pairs)  6.41 us
  transfers between devices with their start and end apart: 40, of which 20 were waited for; matrix products, arithmetic and copies ran while one was open for 6% of the time, Pallas kernels for 5%

profile of v1, /device:TPU:0, one launch (start us, length us, event | category | flops | bytes accessed | tf_op | source)
XLA Modules:
  0.0 217.5 jit_solution(885574326200595138)
XLA Ops:
  1.3 1.7 copy.19
  4.9 3.0 %collective-permute-start = (bf16[4,576,128]{2,1,0:T(8,128)(2,1)}, bf16[4,576,128]{2,1,0:T(8,128)(2,1)S(1)}, u32[]{:S(2)}, u32[]{:S(2)}) collective-permute-start(bf16[4,576,128]{2,1,0:T(8,128)(2,1)} %get-tuple-element.56), channel_id=1, source_target_pairs={{0,4},{4,0},{8,12},{12,8},{16,20},{20,16},{24,28},{28,24},{1,5},{5... | collective-permute-start | bytes 1769480 | tf_op jit(solution)/shard_map/ppermute | solution.py:34
  9.4 4.3 %collective-permute-start.3 = (bf16[576,512]{1,0:T(8,128)(2,1)S(1)}, bf16[576,512]{1,0:T(8,128)(2,1)}, u32[]{:S(2)}, u32[]{:S(2)}) collective-permute-start(bf16[576,512]{1,0:T(8,128)(2,1)S(1)} %copy-done.11), channel_id=1, source_target_pairs={{0,8},{4,12},{8,16},{12,20},{16,24},{20,28},{1,9},{5,13},{9,17},{1... | collective-permute-start | bytes 1769480 | tf_op jit(solution)/shard_map/ppermute | solution.py:51
  16.4 5.0 %collective-permute-done.refs_4_ = bf16[4,576,128]{2,1,0:T(8,128)(2,1)S(1)} collective-permute-done((bf16[4,576,128]{2,1,0:T(8,128)(2,1)}, bf16[4,576,128]{2,1,0:T(8,128)(2,1)S(1)}, u32[]{:S(2)}, u32[]{:S(2)}) %collective-permute-start) | collective-permute-done | bytes 589856 | tf_op jit(solution)/shard_map/ppermute | solution.py:34
  22.7 3.4 %collective-permute-done.3 = bf16[576,512]{1,0:T(8,128)(2,1)} collective-permute-done((bf16[576,512]{1,0:T(8,128)(2,1)S(1)}, bf16[576,512]{1,0:T(8,128)(2,1)}, u32[]{:S(2)}, u32[]{:S(2)}) %collective-permute-start.3) | collective-permute-done | bytes 589856 | tf_op jit(solution)/shard_map/ppermute | solution.py:51
  26.1 5.1 %collective-permute-done.4 = bf16[576,512]{1,0:T(8,128)(2,1)} collective-permute-done((bf16[576,512]{1,0:T(8,128)(2,1)S(1)}, bf16[576,512]{1,0:T(8,128)(2,1)}, u32[]{:S(2)}, u32[]{:S(2)}) %collective-permute-start.4) | collective-permute-done | bytes 589856 | tf_op jit(solution)/shard_map/ppermute | solution.py:56
  34.1 10.3 %collective-permute-done.5.refs_9_ = bf16[512,512]{1,0:T(8,128)(2,1)S(1)} collective-permute-done((bf16[512,512]{1,0:T(8,128)(2,1)S(1)}, bf16[512,512]{1,0:T(8,128)(2,1)S(1)}, u32[]{:S(2)}, u32[]{:S(2)}) %collective-permute-start.5) | collective-permute-done | bytes 524320 | tf_op jit(solution)/shard_map/ppermute | solution.py:34
  45.9 4.3 %collective-permute-done.10 = bf16[576,512]{1,0:T(8,128)(2,1)} collective-permute-done((bf16[576,512]{1,0:T(8,128)(2,1)}, bf16[576,512]{1,0:T(8,128)(2,1)}, u32[]{:S(2)}, u32[]{:S(2)}) %collective-permute-start.10) | collective-permute-done | bytes 589856 | tf_op jit(solution)/shard_map/ppermute | solution.py:56
  53.1 2.4 %gradient_part.2 = bf16[2,576,512]{2,1,0:T(8,128)(2,1)} custom-call(bf16[4,576,128]{2,1,0:T(8,128)(2,1)S(1)} %get-tuple-element.55.refs_0_, bf16[4,576,128]{2,1,0:T(8,128)(2,1)S(1)} %collective-permute-done.1.refs_1_, bf16[4,576,128]{2,1,0:T(8,128)(2,1)S(1)} %collective-permute-done.2.refs_2_, bf16[4,576,128]{2,1,0:T(8,128)(2,1)S(1)} %collective-permute-done.8.refs_3_, ...), custom_call_target="tpu_custom_call" | custom-call | flops 1207959552 | bytes 4587520 | tf_op jit(solution)/shard_map/gradient_part/pallas_call | solution.py:118
  55.5 2.4 %slice_bitcast_fusion = (bf16[576,512]{1,0:T(8,128)(2,1)}, bf16[576,512]{1,0:T(8,128)(2,1)}) fusion(bf16[2,576,512]{2,1,0:T(8,128)(2,1)} %gradient_part.2), kind=kLoop, calls=%fused_computation.29 | loop fusion | bytes 2359296 | tf_op jit(solution)/shard_map/squeeze | solution.py:244
  57.9 13.4 %collective-permute-start.12 = (bf16[576,512]{1,0:T(8,128)(2,1)}, bf16[576,512]{1,0:T(8,128)(2,1)}, u32[]{:S(2)}, u32[]{:S(2)}) collective-permute-start(bf16[576,512]{1,0:T(8,128)(2,1)} %get-tuple-element.118), channel_id=1, source_target_pairs={{0,8},{4,12},{1,9},{5,13},{2,10},{6,14},{3,11},{7,15}} | collective-permute-start | bytes 1769480 | tf_op jit(solution)/shard_map/ppermute | solution.py:51
  76.8 2.4 %gradient_part.3 = bf16[2,576,512]{2,1,0:T(8,128)(2,1)} custom-call(bf16[4,576,128]{2,1,0:T(8,128)(2,1)S(1)} %get-tuple-element.55.refs_0_, bf16[4,576,128]{2,1,0:T(8,128)(2,1)S(1)} %collective-permute-done.1.refs_1_, bf16[4,576,128]{2,1,0:T(8,128)(2,1)S(1)} %collective-permute-done.2.refs_2_, bf16[4,576,128]{2,1,0:T(8,128)(2,1)S(1)} %copy-done.3, ...), custom_call_target="tpu_custom_call" | custom-call | flops 1207959552 | bytes 4587520 | tf_op jit(solution)/shard_map/gradient_part/pallas_call | solution.py:118
  79.2 8.9 %collective-permute-done.14.next1 = bf16[512,512]{1,0:T(8,128)(2,1)} collective-permute-done((bf16[512,512]{1,0:T(8,128)(2,1)}, bf16[512,512]{1,0:T(8,128)(2,1)}, u32[]{:S(2)}, u32[]{:S(2)}) %collective-permute-start.14) | collective-permute-done | bytes 524320 | tf_op jit(solution)/shard_map/ppermute | solution.py:34
  88.0 1.7 fusion.1
  95.9 7.0 %attn_part.1 = (f32[512,512]{1,0:T(8,128)}, bf16[512,512]{1,0:T(8,128)(2,1)S(1)}) custom-call(bf16[4,576,128]{2,1,0:T(8,128)(2,1)S(1)} %get-tuple-element.55.refs_0_, bf16[4,576,128]{2,1,0:T(8,128)(2,1)S(1)} %collective-permute-done.1.refs_1_, bf16[4,576,128]{2,1,0:T(8,128)(2,1)S(1)} %collective-permute-done.2.refs_2_, bf16[4,576,128]{2,1,0:T(8,128)(2,1)S(1)} %copy-done.3, ...), custom_call_target="tpu_custom_call" | custom-call | flops 2415919104 | bytes 8650752 | tf_op jit(solution)/shard_map/attn_part/pallas_call | solution.py:156
  103.8 9.5 %collective-permute-start.19 = (bf16[576,512]{1,0:T(8,128)(2,1)S(1)}, bf16[576,512]{1,0:T(8,128)(2,1)S(1)}, u32[]{:S(2)}, u32[]{:S(2)}) collective-permute-start(bf16[576,512]{1,0:T(8,128)(2,1)S(1)} %get-tuple-element.114), channel_id=1, source_target_pairs={{0,8},{4,12},{8,16},{12,20},{16,24},{20,28},{1,9},{5,13},{9,17},{1... | collective-permute-start | bytes 1769480 | tf_op jit(solution)/shard_map/ppermute | solution.py:51
  115.2 11.2 %collective-permute-done.21 = bf16[512,512]{1,0:T(8,128)(2,1)S(1)} collective-permute-done((bf16[512,512]{1,0:T(8,128)(2,1)S(1)}, bf16[512,512]{1,0:T(8,128)(2,1)S(1)}, u32[]{:S(2)}, u32[]{:S(2)}) %collective-permute-start.21) | collective-permute-done | bytes 524320 | tf_op jit(solution)/shard_map/ppermute | solution.py:34
  128.4 2.5 %subtract_convert_fusion = (bf16[576,512]{1,0:T(8,128)(2,1)S(1)}, f32[576,512]{1,0:T(8,128)}, f32[576,512]{1,0:T(8,128)}) fusion(bf16[576,512]{1,0:T(8,128)(2,1)S(1)} %copy-done.12, bf16[576,512]{1,0:T(8,128)(2,1)S(1)} %collective-permute-done.20, bf16[576,512]{1,0:T(8,128)(2,1)S(1)} %collective-permute-done.19, bf16[2,576,512]{2,1,0:T(8,128)(2,1)S(1)} %copy-done.10, ...), kind=kLoop, calls=%fused_computation.16 | loop fusion | flops 6193152 | bytes 7667712 | tf_op jit(solution)/shard_map/convert_element_type | solution.py:29
  131.0 2.2 %outward_part.4 = (bf16[2,2,576,128]{3,2,1,0:T(8,128)(2,1)S(1)}, bf16[2,2,576,128]{3,2,1,0:T(8,128)(2,1)S(1)}) custom-call(bf16[576,512]{1,0:T(8,128)(2,1)S(1)} %get-tuple-element.106.block, bf16[512,512]{1,0:T(8,128)(2,1)} %bitcast.11.next0, bf16[512,512]{1,0:T(8,128)(2,1)} %collective-permute-done.14.next1), custom_call_target="tpu_custom_call" | custom-call | flops 603979776 | bytes 2818048 | tf_op jit(solution)/shard_map/outward_part/pallas_call | solution.py:185
  133.3 3.2 %collective-permute-start.24 = (bf16[576,512]{1,0:T(8,128)(2,1)S(1)}, bf16[576,512]{1,0:T(8,128)(2,1)S(1)}, u32[]{:S(2)}, u32[]{:S(2)}) collective-permute-start(bf16[576,512]{1,0:T(8,128)(2,1)S(1)} %get-tuple-element.106.block), channel_id=1, source_target_pairs={{0,8},{4,12},{8,16},{12,20},{16,24},{20,28},{1,9},{5,13},{9,17},{1... | collective-permute-start | bytes 1769480 | tf_op jit(solution)/shard_map/ppermute | solution.py:51
  138.6 8.6 %collective-permute-done.23 = bf16[2,576,128]{2,1,0:T(8,128)(2,1)S(1)} collective-permute-done((bf16[2,576,128]{2,1,0:T(8,128)(2,1)S(1)}, bf16[2,576,128]{2,1,0:T(8,128)(2,1)S(1)}, u32[]{:S(2)}, u32[]{:S(2)}) %collective-permute-start.23) | collective-permute-done | bytes 294944 | tf_op jit(solution)/shard_map/ppermute | solution.py:34
  147.2 2.4 %collective-permute-done.24 = bf16[576,512]{1,0:T(8,128)(2,1)S(1)} collective-permute-done((bf16[576,512]{1,0:T(8,128)(2,1)S(1)}, bf16[576,512]{1,0:T(8,128)(2,1)S(1)}, u32[]{:S(2)}, u32[]{:S(2)}) %collective-permute-start.24) | collective-permute-done | bytes 589856 | tf_op jit(solution)/shard_map/ppermute | solution.py:51
  149.6 4.1 %collective-permute-done.25 = bf16[576,512]{1,0:T(8,128)(2,1)S(1)} collective-permute-done((bf16[576,512]{1,0:T(8,128)(2,1)S(1)}, bf16[576,512]{1,0:T(8,128)(2,1)S(1)}, u32[]{:S(2)}, u32[]{:S(2)}) %collective-permute-start.25) | collective-permute-done | bytes 589856 | tf_op jit(solution)/shard_map/ppermute | solution.py:56
  153.9 2.0 outward_part.5
  158.8 9.0 %collective-permute-done.27 = bf16[2,576,128]{2,1,0:T(8,128)(2,1)} collective-permute-done((bf16[2,576,128]{2,1,0:T(8,128)(2,1)S(1)}, bf16[2,576,128]{2,1,0:T(8,128)(2,1)}, u32[]{:S(2)}, u32[]{:S(2)}) %collective-permute-start.27) | collective-permute-done | bytes 294944 | tf_op jit(solution)/shard_map/ppermute | solution.py:34
  168.8 5.5 %collective-permute-done.29 = bf16[576,512]{1,0:T(8,128)(2,1)S(1)} collective-permute-done((bf16[576,512]{1,0:T(8,128)(2,1)S(1)}, bf16[576,512]{1,0:T(8,128)(2,1)S(1)}, u32[]{:S(2)}, u32[]{:S(2)}) %collective-permute-start.29) | collective-permute-done | bytes 589856 | tf_op jit(solution)/shard_map/ppermute | solution.py:56
  174.3 2.0 outward_part.6
  180.1 8.2 %collective-permute-done.31 = bf16[2,576,128]{2,1,0:T(8,128)(2,1)S(1)} collective-permute-done((bf16[2,576,128]{2,1,0:T(8,128)(2,1)S(1)}, bf16[2,576,128]{2,1,0:T(8,128)(2,1)S(1)}, u32[]{:S(2)}, u32[]{:S(2)}) %collective-permute-start.31) | collective-permute-done | bytes 294944 | tf_op jit(solution)/shard_map/ppermute | solution.py:34
  188.4 6.5 %collective-permute-done.33 = bf16[576,512]{1,0:T(8,128)(2,1)} collective-permute-done((bf16[576,512]{1,0:T(8,128)(2,1)S(1)}, bf16[576,512]{1,0:T(8,128)(2,1)}, u32[]{:S(2)}, u32[]{:S(2)}) %collective-permute-start.33) | collective-permute-done | bytes 589856 | tf_op jit(solution)/shard_map/ppermute | solution.py:56
  196.1 2.1 outward_part.7
  203.3 6.3 %collective-permute-done.35 = bf16[2,576,128]{2,1,0:T(8,128)(2,1)S(1)} collective-permute-done((bf16[2,576,128]{2,1,0:T(8,128)(2,1)S(1)}, bf16[2,576,128]{2,1,0:T(8,128)(2,1)S(1)}, u32[]{:S(2)}, u32[]{:S(2)}) %collective-permute-start.35) | collective-permute-done | bytes 294944 | tf_op jit(solution)/shard_map/ppermute | solution.py:34
  211.2 3.7 %collective-permute-done.39 = bf16[576,128]{1,0:T(8,128)(2,1)S(1)} collective-permute-done((bf16[576,128]{1,0:T(8,128)(2,1)S(1)}, bf16[576,128]{1,0:T(8,128)(2,1)S(1)}, u32[]{:S(2)}, u32[]{:S(2)}) %collective-permute-start.39) | collective-permute-done | bytes 147488 | tf_op jit(solution)/shard_map/ppermute | solution.py:34
  (144 shorter events, 52.0 us)
Async XLA Ops:
  4.9 16.5 %collective-permute-start = (bf16[4,576,128]{2,1,0:T(8,128)(2,1)}, bf16[4,576,128]{2,1,0:T(8,128)(2,1)S(1)}, u32[]{:S(2)}, u32[]{:S(2)}) collective-permute-start(bf16[4,576,128]{2,1,0:T(8,128)(2,1)} %get-tuple-element.56), channel_id=1, source_target_pairs={{0,4},{4,0},{8,12},{12,8},{16,20},{20,16},{24,28},{28,24},{1,5},{5... | collective-permute-start | bytes 1769480 | tf_op jit(solution)/shard_map/ppermute | solution.py:34
  7.9 14.8 %collective-permute-start.1 = (bf16[4,576,128]{2,1,0:T(8,128)(2,1)S(1)}, bf16[4,576,128]{2,1,0:T(8,128)(2,1)S(1)}, u32[]{:S(2)}, u32[]{:S(2)}) collective-permute-start(bf16[4,576,128]{2,1,0:T(8,128)(2,1)S(1)} %get-tuple-element.55.refs_0_), channel_id=1, source_target_pairs={{0,2},{1,3},{2,0},{3,1},{4,6},{5,7},{6,4},{7,5},{8,10},{9,11},{10,... | collective-permute-start | bytes 1769480 | tf_op jit(solution)/shard_map/ppermute | solution.py:34
  9.4 13.3 %collective-permute-start.2 = (bf16[4,576,128]{2,1,0:T(8,128)(2,1)S(1)}, bf16[4,576,128]{2,1,0:T(8,128)(2,1)S(1)}, u32[]{:S(2)}, u32[]{:S(2)}) collective-permute-start(bf16[4,576,128]{2,1,0:T(8,128)(2,1)S(1)} %get-tuple-element.55.refs_0_), channel_id=1, source_target_pairs={{0,1},{1,0},{2,3},{3,2},{4,5},{5,4},{6,7},{7,6},{8,9},{9,8},{10,11... | collective-permute-start | bytes 1769480 | tf_op jit(solution)/shard_map/ppermute | solution.py:34
  9.4 16.7 %collective-permute-start.3 = (bf16[576,512]{1,0:T(8,128)(2,1)S(1)}, bf16[576,512]{1,0:T(8,128)(2,1)}, u32[]{:S(2)}, u32[]{:S(2)}) collective-permute-start(bf16[576,512]{1,0:T(8,128)(2,1)S(1)} %copy-done.11), channel_id=1, source_target_pairs={{0,8},{4,12},{8,16},{12,20},{16,24},{20,28},{1,9},{5,13},{9,17},{1... | collective-permute-start | bytes 1769480 | tf_op jit(solution)/shard_map/ppermute | solution.py:51
  13.7 17.4 %collective-permute-start.4 = (bf16[576,512]{1,0:T(8,128)(2,1)S(1)}, bf16[576,512]{1,0:T(8,128)(2,1)}, u32[]{:S(2)}, u32[]{:S(2)}) collective-permute-start(bf16[576,512]{1,0:T(8,128)(2,1)S(1)} %copy-done.11), channel_id=1, source_target_pairs={{8,0},{12,4},{16,8},{20,12},{24,16},{28,20},{9,1},{13,5},{17,9},{2... | collective-permute-start | bytes 1769480 | tf_op jit(solution)/shard_map/ppermute | solution.py:56
  31.2 13.2 %collective-permute-start.5 = (bf16[512,512]{1,0:T(8,128)(2,1)S(1)}, bf16[512,512]{1,0:T(8,128)(2,1)S(1)}, u32[]{:S(2)}, u32[]{:S(2)}) collective-permute-start(bf16[512,512]{1,0:T(8,128)(2,1)S(1)} %bitcast.97), channel_id=1, source_target_pairs={{0,4},{4,0},{8,12},{12,8},{16,20},{20,16},{24,28},{28,24},{1,5},{5... | collective-permute-start | bytes 1572872 | tf_op jit(solution)/shard_map/ppermute | solution.py:34
  31.7 18.5 %collective-permute-start.6 = (bf16[4,576,128]{2,1,0:T(8,128)(2,1)S(1)}, bf16[4,576,128]{2,1,0:T(8,128)(2,1)S(1)}, u32[]{:S(2)}, u32[]{:S(2)}) collective-permute-start(bf16[4,576,128]{2,1,0:T(8,128)(2,1)S(1)} %collective-permute-done.refs_4_), channel_id=1, source_target_pairs={{0,2},{1,3},{2,0},{3,1},{4,6},{5,7},{6,4},{7,5},{8,10},{9,11},{10,... | collective-permute-start | bytes 1769480 | tf_op jit(solution)/shard_map/ppermute | solution.py:34
  32.2 17.9 %collective-permute-start.7 = (bf16[4,576,128]{2,1,0:T(8,128)(2,1)S(1)}, bf16[4,576,128]{2,1,0:T(8,128)(2,1)S(1)}, u32[]{:S(2)}, u32[]{:S(2)}) collective-permute-start(bf16[4,576,128]{2,1,0:T(8,128)(2,1)S(1)} %collective-permute-done.refs_4_), channel_id=1, source_target_pairs={{0,1},{1,0},{2,3},{3,2},{4,5},{5,4},{6,7},{7,6},{8,9},{9,8},{10,11... | collective-permute-start | bytes 1769480 | tf_op jit(solution)/shard_map/ppermute | solution.py:34
  32.2 17.9 %collective-permute-start.10 = (bf16[576,512]{1,0:T(8,128)(2,1)}, bf16[576,512]{1,0:T(8,128)(2,1)}, u32[]{:S(2)}, u32[]{:S(2)}) collective-permute-start(bf16[576,512]{1,0:T(8,128)(2,1)} %collective-permute-done.4), channel_id=1, source_target_pairs={{8,0},{12,4},{16,8},{20,12},{9,1},{13,5},{17,9},{21,13},{10,2},{14... | collective-permute-start | bytes 1769480 | tf_op jit(solution)/shard_map/ppermute | solution.py:56
  33.5 16.7 %collective-permute-start.8 = (bf16[4,576,128]{2,1,0:T(8,128)(2,1)S(1)}, bf16[4,576,128]{2,1,0:T(8,128)(2,1)S(1)}, u32[]{:S(2)}, u32[]{:S(2)}) collective-permute-start(bf16[4,576,128]{2,1,0:T(8,128)(2,1)S(1)} %collective-permute-done.1.refs_1_), channel_id=1, source_target_pairs={{0,1},{1,0},{2,3},{3,2},{4,5},{5,4},{6,7},{7,6},{8,9},{9,8},{10,11... | collective-permute-start | bytes 1769480 | tf_op jit(solution)/shard_map/ppermute | solution.py:34
  50.3 37.7 %collective-permute-start.15 = (bf16[576,512]{1,0:T(8,128)(2,1)}, bf16[576,512]{1,0:T(8,128)(2,1)}, u32[]{:S(2)}, u32[]{:S(2)}) collective-permute-start(bf16[576,512]{1,0:T(8,128)(2,1)} %collective-permute-done.9), channel_id=1, source_target_pairs={{16,24},{20,28},{17,25},{21,29},{18,26},{22,30},{19,27},{23,31}} | collective-permute-start | bytes 1769480 | tf_op jit(solution)/shard_map/ppermute | solution.py:51
  51.8 36.3 %collective-permute-start.16 = (bf16[576,512]{1,0:T(8,128)(2,1)}, bf16[576,512]{1,0:T(8,128)(2,1)}, u32[]{:S(2)}, u32[]{:S(2)}) collective-permute-start(bf16[576,512]{1,0:T(8,128)(2,1)} %collective-permute-done.10), channel_id=1, source_target_pairs={{8,0},{12,4},{9,1},{13,5},{10,2},{14,6},{11,3},{15,7}} | collective-permute-start | bytes 1769480 | tf_op jit(solution)/shard_map/ppermute | solution.py:56
  57.9 30.2 %collective-permute-start.12 = (bf16[576,512]{1,0:T(8,128)(2,1)}, bf16[576,512]{1,0:T(8,128)(2,1)}, u32[]{:S(2)}, u32[]{:S(2)}) collective-permute-start(bf16[576,512]{1,0:T(8,128)(2,1)} %get-tuple-element.118), channel_id=1, source_target_pairs={{0,8},{4,12},{1,9},{5,13},{2,10},{6,14},{3,11},{7,15}} | collective-permute-start | bytes 1769480 | tf_op jit(solution)/shard_map/ppermute | solution.py:51
  71.3 16.8 %collective-permute-start.13 = (bf16[576,512]{1,0:T(8,128)(2,1)}, bf16[576,512]{1,0:T(8,128)(2,1)}, u32[]{:S(2)}, u32[]{:S(2)}) collective-permute-start(bf16[576,512]{1,0:T(8,128)(2,1)} %get-tuple-element.117), channel_id=1, source_target_pairs={{24,16},{28,20},{25,17},{29,21},{26,18},{30,22},{27,19},{31,23}} | collective-permute-start | bytes 1769480 | tf_op jit(solution)/shard_map/ppermute | solution.py:56
  73.6 14.4 %collective-permute-start.14 = (bf16[512,512]{1,0:T(8,128)(2,1)}, bf16[512,512]{1,0:T(8,128)(2,1)}, u32[]{:S(2)}, u32[]{:S(2)}) collective-permute-start(bf16[512,512]{1,0:T(8,128)(2,1)} %bitcast.11.next0), channel_id=1, source_target_pairs={{0,4},{4,0},{8,12},{12,8},{16,20},{20,16},{24,28},{28,24},{1,5},{5... | collective-permute-start | bytes 1572872 | tf_op jit(solution)/shard_map/ppermute | solution.py:34
  89.7 13.7 %collective-permute-start.17 = (bf16[576,512]{1,0:T(8,128)(2,1)S(1)}, bf16[576,512]{1,0:T(8,128)(2,1)S(1)}, u32[]{:S(2)}, u32[]{:S(2)}) collective-permute-start(bf16[576,512]{1,0:T(8,128)(2,1)S(1)} %get-tuple-element.116), channel_id=1, source_target_pairs={{0,8},{4,12},{8,16},{12,20},{1,9},{5,13},{9,17},{13,21},{2,10},{6,... | collective-permute-start | bytes 1769480 | tf_op jit(solution)/shard_map/ppermute | solution.py:51
  91.1 12.4 %collective-permute-start.18 = (bf16[576,512]{1,0:T(8,128)(2,1)S(1)}, bf16[576,512]{1,0:T(8,128)(2,1)S(1)}, u32[]{:S(2)}, u32[]{:S(2)}) collective-permute-start(bf16[576,512]{1,0:T(8,128)(2,1)S(1)} %get-tuple-element.115), channel_id=1, source_target_pairs={{16,8},{20,12},{24,16},{28,20},{17,9},{21,13},{25,17},{29,21},{18,... | collective-permute-start | bytes 1769480 | tf_op jit(solution)/shard_map/ppermute | solution.py:56
  103.8 22.7 %collective-permute-start.19 = (bf16[576,512]{1,0:T(8,128)(2,1)S(1)}, bf16[576,512]{1,0:T(8,128)(2,1)S(1)}, u32[]{:S(2)}, u32[]{:S(2)}) collective-permute-start(bf16[576,512]{1,0:T(8,128)(2,1)S(1)} %get-tuple-element.114), channel_id=1, source_target_pairs={{0,8},{4,12},{8,16},{12,20},{16,24},{20,28},{1,9},{5,13},{9,17},{1... | collective-permute-start | bytes 1769480 | tf_op jit(solution)/shard_map/ppermute | solution.py:51
  113.4 15.1 %collective-permute-start.20 = (bf16[576,512]{1,0:T(8,128)(2,1)S(1)}, bf16[576,512]{1,0:T(8,128)(2,1)S(1)}, u32[]{:S(2)}, u32[]{:S(2)}) collective-permute-start(bf16[576,512]{1,0:T(8,128)(2,1)S(1)} %get-tuple-element.113), channel_id=1, source_target_pairs={{8,0},{12,4},{16,8},{20,12},{24,16},{28,20},{9,1},{13,5},{17,9},{2... | collective-permute-start | bytes 1769480 | tf_op jit(solution)/shard_map/ppermute | solution.py:56
  114.7 11.8 %collective-permute-start.21 = (bf16[512,512]{1,0:T(8,128)(2,1)S(1)}, bf16[512,512]{1,0:T(8,128)(2,1)S(1)}, u32[]{:S(2)}, u32[]{:S(2)}) collective-permute-start(bf16[512,512]{1,0:T(8,128)(2,1)S(1)} %get-tuple-element.82), channel_id=1, source_target_pairs={{0,4},{4,0},{8,12},{12,8},{16,20},{20,16},{24,28},{28,24},{1,5},{5... | collective-permute-start | bytes 1572872 | tf_op jit(solution)/shard_map/ppermute | solution.py:34
  133.3 16.4 %collective-permute-start.24 = (bf16[576,512]{1,0:T(8,128)(2,1)S(1)}, bf16[576,512]{1,0:T(8,128)(2,1)S(1)}, u32[]{:S(2)}, u32[]{:S(2)}) collective-permute-start(bf16[576,512]{1,0:T(8,128)(2,1)S(1)} %get-tuple-element.106.block), channel_id=1, source_target_pairs={{0,8},{4,12},{8,16},{12,20},{16,24},{20,28},{1,9},{5,13},{9,17},{1... | collective-permute-start | bytes 1769480 | tf_op jit(solution)/shard_map/ppermute | solution.py:51
  136.5 17.3 %collective-permute-start.25 = (bf16[576,512]{1,0:T(8,128)(2,1)S(1)}, bf16[576,512]{1,0:T(8,128)(2,1)S(1)}, u32[]{:S(2)}, u32[]{:S(2)}) collective-permute-start(bf16[576,512]{1,0:T(8,128)(2,1)S(1)} %get-tuple-element.106.block), channel_id=1, source_target_pairs={{8,0},{12,4},{16,8},{20,12},{24,16},{28,20},{9,1},{13,5},{17,9},{2... | collective-permute-start | bytes 1769480 | tf_op jit(solution)/shard_map/ppermute | solution.py:56
  138.0 9.2 %collective-permute-start.23 = (bf16[2,576,128]{2,1,0:T(8,128)(2,1)S(1)}, bf16[2,576,128]{2,1,0:T(8,128)(2,1)S(1)}, u32[]{:S(2)}, u32[]{:S(2)}) collective-permute-start(bf16[2,576,128]{2,1,0:T(8,128)(2,1)S(1)} %slice_bitcast_fusion.8), channel_id=1, source_target_pairs={{0,2},{1,3},{2,0},{3,1},{4,6},{5,7},{6,4},{7,5},{8,10},{9,11},{10,... | collective-permute-start | bytes 884744 | tf_op jit(solution)/shard_map/ppermute | solution.py:34
  155.9 12.8 %collective-permute-start.28 = (bf16[576,512]{1,0:T(8,128)(2,1)S(1)}, bf16[576,512]{1,0:T(8,128)(2,1)S(1)}, u32[]{:S(2)}, u32[]{:S(2)}) collective-permute-start(bf16[576,512]{1,0:T(8,128)(2,1)S(1)} %collective-permute-done.24), channel_id=1, source_target_pairs={{8,16},{12,20},{16,24},{20,28},{9,17},{13,21},{17,25},{21,29},{10,... | collective-permute-start | bytes 1769480 | tf_op jit(solution)/shard_map/ppermute | solution.py:51
  156.7 17.6 %collective-permute-start.29 = (bf16[576,512]{1,0:T(8,128)(2,1)S(1)}, bf16[576,512]{1,0:T(8,128)(2,1)S(1)}, u32[]{:S(2)}, u32[]{:S(2)}) collective-permute-start(bf16[576,512]{1,0:T(8,128)(2,1)S(1)} %collective-permute-done.25), channel_id=1, source_target_pairs={{8,0},{12,4},{16,8},{20,12},{9,1},{13,5},{17,9},{21,13},{10,2},{14... | collective-permute-start | bytes 1769480 | tf_op jit(solution)/shard_map/ppermute | solution.py:56
  158.2 9.6 %collective-permute-start.27 = (bf16[2,576,128]{2,1,0:T(8,128)(2,1)S(1)}, bf16[2,576,128]{2,1,0:T(8,128)(2,1)}, u32[]{:S(2)}, u32[]{:S(2)}) collective-permute-start(bf16[2,576,128]{2,1,0:T(8,128)(2,1)S(1)} %slice_bitcast_fusion.6), channel_id=1, source_target_pairs={{0,2},{1,3},{2,0},{3,1},{4,6},{5,7},{6,4},{7,5},{8,10},{9,11},{10,... | collective-permute-start | bytes 884744 | tf_op jit(solution)/shard_map/ppermute | solution.py:34
  176.4 11.9 %collective-permute-start.32 = (bf16[576,512]{1,0:T(8,128)(2,1)S(1)}, bf16[576,512]{1,0:T(8,128)(2,1)S(1)}, u32[]{:S(2)}, u32[]{:S(2)}) collective-permute-start(bf16[576,512]{1,0:T(8,128)(2,1)S(1)} %collective-permute-done.28), channel_id=1, source_target_pairs={{16,24},{20,28},{17,25},{21,29},{18,26},{22,30},{19,27},{23,31}} | collective-permute-start | bytes 1769480 | tf_op jit(solution)/shard_map/ppermute | solution.py:51
  177.1 17.7 %collective-permute-start.33 = (bf16[576,512]{1,0:T(8,128)(2,1)S(1)}, bf16[576,512]{1,0:T(8,128)(2,1)}, u32[]{:S(2)}, u32[]{:S(2)}) collective-permute-start(bf16[576,512]{1,0:T(8,128)(2,1)S(1)} %collective-permute-done.29), channel_id=1, source_target_pairs={{8,0},{12,4},{9,1},{13,5},{10,2},{14,6},{11,3},{15,7}} | collective-permute-start | bytes 1769480 | tf_op jit(solution)/shard_map/ppermute | solution.py:56
  178.8 9.5 %collective-permute-start.31 = (bf16[2,576,128]{2,1,0:T(8,128)(2,1)S(1)}, bf16[2,576,128]{2,1,0:T(8,128)(2,1)S(1)}, u32[]{:S(2)}, u32[]{:S(2)}) collective-permute-start(bf16[2,576,128]{2,1,0:T(8,128)(2,1)S(1)} %slice_bitcast_fusion.4), channel_id=1, source_target_pairs={{0,2},{1,3},{2,0},{3,1},{4,6},{5,7},{6,4},{7,5},{8,10},{9,11},{10,... | collective-permute-start | bytes 884744 | tf_op jit(solution)/shard_map/ppermute | solution.py:34
  198.6 12.6 %collective-permute-start.36 = (bf16[576,128]{1,0:T(8,128)(2,1)S(1)}, bf16[576,128]{1,0:T(8,128)(2,1)S(1)}, u32[]{:S(2)}, u32[]{:S(2)}) collective-permute-start(bf16[576,128]{1,0:T(8,128)(2,1)S(1)} %get-tuple-element.122), channel_id=1, source_target_pairs={{0,4},{4,0},{8,12},{12,8},{16,20},{20,16},{24,28},{28,24},{1,5},{5... | collective-permute-start | bytes 442376 | tf_op jit(solution)/shard_map/ppermute | solution.py:34
  201.1 10.1 %collective-permute-start.37 = (bf16[576,128]{1,0:T(8,128)(2,1)S(1)}, bf16[576,128]{1,0:T(8,128)(2,1)S(1)}, u32[]{:S(2)}, u32[]{:S(2)}) collective-permute-start(bf16[576,128]{1,0:T(8,128)(2,1)S(1)} %get-tuple-element.124), channel_id=1, source_target_pairs={{0,4},{4,0},{8,12},{12,8},{16,20},{20,16},{24,28},{28,24},{1,5},{5... | collective-permute-start | bytes 442376 | tf_op jit(solution)/shard_map/ppermute | solution.py:34
  201.7 9.5 %collective-permute-start.38 = (bf16[576,128]{1,0:T(8,128)(2,1)S(1)}, bf16[576,128]{1,0:T(8,128)(2,1)S(1)}, u32[]{:S(2)}, u32[]{:S(2)}) collective-permute-start(bf16[576,128]{1,0:T(8,128)(2,1)S(1)} %get-tuple-element.126), channel_id=1, source_target_pairs={{0,4},{4,0},{8,12},{12,8},{16,20},{20,16},{24,28},{28,24},{1,5},{5... | collective-permute-start | bytes 442376 | tf_op jit(solution)/shard_map/ppermute | solution.py:34
  (28 other events, 176.8 us)

commit v2 on v1

v2 whole, which is shorter than its diff:
```python
import functools
import math

import jax
import jax.numpy as jnp
from jax import lax
from jax.experimental import pallas as pl
from jax.experimental.pallas import tpu as pltpu
from jax.sharding import PartitionSpec as P

first_decay = 0.9
second_decay = 0.95
first_fix = 1.0 - 0.9**10
second_fix = 1.0 - 0.95**10
learning_rate = 0.002
weight_decay = 0.1
epsilon = 1e-08
bf16 = jnp.bfloat16
f32 = jnp.float32
VMEM_LIMIT = 48 * 2**20


def adamw_step(gradient, weight, moment1, moment2):
    new_moment1 = first_decay * moment1 + (1.0 - first_decay) * gradient
    new_moment2 = second_decay * moment2 + (1.0 - second_decay) * gradient * gradient
    update = new_moment1 / first_fix / (jnp.sqrt(new_moment2 / second_fix) + epsilon)
    new_weight = (
        weight.astype(f32) * (1.0 - learning_rate * weight_decay) - learning_rate * update
    ).astype(bf16)
    return (new_weight, new_moment1, new_moment2)


def flip(value, axis, bit):
    return lax.ppermute(value, axis, [(i, i ^ bit) for i in range(lax.axis_size(axis))])


def to_partner(value):
    return flip(value, "dp", 1)


def to_chip(value):
    return flip(value, "tensor", 2)


def to_core(value):
    return flip(value, "tensor", 1)


def to_plane(value, bit):
    return flip(value, "dp", 2 * bit)


def stage(*values):
    return lax.optimization_barrier(values)


def relative(rows, x, c):
    block = rows.shape[0] // 4
    rows = rows.reshape(2, 2, block, rows.shape[1])
    rows = jnp.where(x == 1, rows[::-1], rows)
    rows = jnp.where(c == 1, rows[:, ::-1], rows)
    return rows.transpose(1, 0, 2, 3).reshape(4 * block, -1)


def absolute(rows, x, c):
    block = rows.shape[0] // 4
    rows = rows.reshape(2, 2, block, -1).transpose(1, 0, 2, 3)
    rows = jnp.where(c == 1, rows[:, ::-1], rows)
    rows = jnp.where(x == 1, rows[::-1], rows)
    return rows.reshape(4 * block, -1)


def params():
    return pltpu.CompilerParams(vmem_limit_bytes=VMEM_LIMIT)


def cost(flops, bytes_accessed):
    return pl.CostEstimate(flops=flops, bytes_accessed=bytes_accessed, transcendentals=0)


def gradient_kernel(scale, *refs):
    pieces, (saved0, saved1, out) = refs[:8], refs[8:]
    rows = saved0.shape[0]
    left = jnp.concatenate([ref[0] for ref in pieces], axis=1)
    total = jnp.dot(left[:, :rows], saved0[...], preferred_element_type=f32)
    total += jnp.dot(left[:, rows:], saved1[...], preferred_element_type=f32)
    out[...] = (total * scale).astype(bf16)


def gradient_part(pieces, saved0, saved1, index, scale):
    _, own, tok = pieces[0].shape
    rows, wide = saved0.shape
    steps = 2 if own % 32 == 0 else 1
    part = own // steps
    whole = pl.BlockSpec((rows, wide), lambda i: (0, 0))
    return pl.pallas_call(
        functools.partial(gradient_kernel, scale),
        grid=(steps,),
        in_specs=[pl.BlockSpec((1, part, tok), lambda i: (index, i, 0))] * 8 + [whole] * 2,
        out_specs=pl.BlockSpec((part, wide), lambda i: (i, 0)),
        out_shape=jax.ShapeDtypeStruct((own, wide), bf16),
        compiler_params=params(),
        cost_estimate=cost(4 * own * rows * wide, 2 * own * (2 * rows + wide) + 4 * rows * wide),
        name="gradient_part",
    )(*pieces, saved0, saved1)


def attn_kernel(*refs):
    pieces, (weights, kept, sent, total) = refs[:8], refs[8:]
    step = pl.program_id(0)
    rows = kept.shape[0]
    left = jnp.concatenate([ref[0] for ref in pieces], axis=1)
    product = lax.dot_general(left, weights[0], (((0,), (0,)), ((), ())), preferred_element_type=f32)

    @pl.when(step == 0)
    def _():
        total[...] = product

    @pl.when(step > 0)
    def _():
        total[...] += product

    @pl.when(step == pl.num_programs(0) - 1)
    def _():
        kept[...] = total[:rows]
        sent[...] = total[rows:].astype(bf16)


def attn_part(pieces, weights):
    n, own, tok = pieces[0].shape
    wide = weights.shape[2]
    rows = 4 * tok
    whole = pl.BlockSpec((rows, wide), lambda i: (0, 0))
    return pl.pallas_call(
        attn_kernel,
        grid=(n,),
        in_specs=[pl.BlockSpec((1, own, tok), lambda i: (i, 0, 0))] * 8
        + [pl.BlockSpec((1, own, wide), lambda i: (i, 0, 0))],
        out_specs=[whole, whole],
        out_shape=[jax.ShapeDtypeStruct((rows, wide), f32), jax.ShapeDtypeStruct((rows, wide), bf16)],
        scratch_shapes=[pltpu.VMEM((2 * rows, wide), f32)],
        compiler_params=params(),
        cost_estimate=cost(4 * n * own * rows * wide, 2 * n * own * (2 * rows + wide) + 6 * rows * wide),
        name="attn_part",
    )(*pieces, weights)


def outward_kernel(block, next0, next1, kept, sent):
    tok = kept.shape[3]
    for y, following in enumerate((next0, next1)):
        out = lax.dot_general(
            block[...], following[...], (((1,), (1,)), ((), ())), preferred_element_type=f32
        ).astype(bf16)
        for chip in range(2):
            kept[chip, y] = out[:, chip * tok : (chip + 1) * tok]
            sent[chip, y] = out[:, (2 + chip) * tok : (3 + chip) * tok]


def outward_part(block, next0, next1):
    own, wide = block.shape
    rows = next0.shape[0]
    shape = jax.ShapeDtypeStruct((2, 2, own, rows // 4), bf16)
    return pl.pallas_call(
        outward_kernel,
        out_shape=[shape, shape],
        compiler_params=params(),
        cost_estimate=cost(4 * own * rows * wide, 2 * (own * wide + 2 * rows * wide + 2 * own * rows)),
        name="outward_part",
    )(block, next0, next1)


def add(a, b):
    return (a.astype(f32) + b.astype(f32)).astype(bf16)


def local(cotangent, attn_saved, attn_next, weight, moment1, moment2):
    dp, t = lax.axis_index("dp"), lax.axis_index("tensor")
    n = lax.axis_size("dp") // 2
    z, y, x, c = dp // 2, dp % 2, t // 2, t % 2
    own, wide = weight.shape
    tok = cotangent.shape[0]
    scale = 1.0 / math.sqrt(4 * tok * lax.axis_size("dp"))
    order = [n - 1] + [r for r in range(1, n - 1)] + [0]
    top = n // 2
    levels = [[r for r in range(n) if r.bit_count() == k] for k in range(n.bit_length())]
    low, multi = levels[1][:-1], [r for level in levels[2:] for r in level]
    halves = 2 if own % 32 == 0 else 1

    weights = {(0, h): part for h, part in enumerate(jnp.split(weight, halves))}

    def fetch(keys):
        for r, h in keys:
            weights[r, h] = to_plane(weights[r & (r - 1), h], r & -r)

    def hold(keys, *others):
        came, *others = stage([weights[k] for k in keys], *others)
        weights.update(zip(keys, came))
        return others

    second = [(r, 1) for r in range(n)] if halves > 1 else []

    blocks = cotangent.T.reshape(n, 2, own, tok)
    blocks = jnp.take(blocks, z ^ jnp.array(order), axis=0)
    mine = jnp.where(y == 0, blocks[:, 0], blocks[:, 1])
    other = jnp.where(y == 0, blocks[:, 1], blocks[:, 0])
    mine, other = stage(mine, other)
    fetch([(top, 0)] + [(r, 0) for r in low])
    partner = to_partner(other)
    mine_x = to_chip(mine)
    mine_c = to_core(mine)
    saved0 = relative(attn_saved, x, c)
    keys = [(r, 0) for r in levels[1]] + second[:1]
    partner, mine_x, mine_c, saved0 = hold(keys, partner, mine_x, mine_c, saved0)

    saved1 = to_partner(saved0)
    partner_x = to_chip(partner)
    partner_c = to_core(partner)
    mine_xc = to_core(mine_x)
    fetch([k for k in second if k[0] == top])
    keys = [(r, 0) for r in levels[1]] + second[:1]
    partner_c, mine_xc = hold(keys, partner_c, mine_xc)
    fetch([(r, 0) for r in multi] + [k for k in second if k[0] in low])
    keys = [(r, 0) for r in multi] + [k for k in second if k[0] in levels[1]]
    saved1, partner_x = hold(keys, saved1, partner_x)
    partner_xc = to_core(partner_x)
    pieces = [mine, mine_x, mine_c, mine_xc, partner, partner_x, partner_c, partner_xc]

    sums = {}
    for j, r in enumerate(order):
        sums[r] = gradient_part(pieces, saved0, saved1, j, scale)
    next0 = relative(attn_next, x, c)
    next1 = to_partner(next0)
    m = 1
    while m < top:
        sends = [r for r in sums if r & m and r != m]
        came = [to_plane(sums.pop(r), m) for r in sends]
        came, sums[m] = stage(came, sums[m])
        for r, value in zip(sends, came):
            sums[r ^ m] = add(sums[r ^ m], value)
        m *= 2
    ends = [1 << k for k in reversed(range(n.bit_length() - 1))]
    (came,) = hold([k for k in second if k[0] in levels[1]], came)
    fetch([k for k in second if k[0] in multi])
    came = [to_plane(sums[m], m) for m in ends]
    gathered = jnp.stack([jnp.concatenate([weights[r, h] for h in range(halves)]) for r in order])
    kept, sent = attn_part(pieces, gathered)
    sent = to_partner(sent)
    came, kept, sent, next1 = stage(came, kept, sent, next1)
    gradient = sums[0].astype(f32) + functools.reduce(jnp.add, [v.astype(f32) for v in came])
    new_weight, new_moment1, new_moment2 = adamw_step(gradient, weight, moment1, moment2)
    grad_attn = absolute((kept + sent.astype(f32)).astype(bf16), x, c)

    held, results = {0: new_weight}, {}
    for k, wave in enumerate(levels):
        later = levels[k + 1] if k + 1 < len(levels) else []
        for r in reversed(later):
            held[r] = to_plane(held[r & (r - 1)], r & -r)
        kept, came = {}, {}
        for r in wave:
            block, sent = outward_part(held[r], next0, next1)
            half = add(block, to_core(sent))
            kept[r], came[r] = half[0], to_chip(half[1])
        if later:
            blocks, kept = stage([held[r] for r in later], kept)
            blocks, came, results = stage(blocks, came, results)
            held.update(zip(later, blocks))
        for r in wave:
            total = add(kept[r], came[r])
            results[r] = (total[0], to_partner(total[1]))

    mine = jnp.stack([results[r][0] for r in range(n)])
    other = jnp.stack([results[r][1] for r in range(n)])
    both = jnp.stack([jnp.where(y == 0, mine, other), jnp.where(y == 0, other, mine)], axis=1)
    next_out = jnp.take(both, z ^ jnp.arange(n), axis=0).reshape(2 * n * own, tok).T
    return (grad_attn, new_weight, new_moment1, new_moment2, next_out)


def solution(mesh):
    return jax.shard_map(
        local,
        mesh=mesh,
        in_specs=(
            P(("dp", "tensor"), None),
            P("dp", "tensor"),
            P("dp", "tensor"),
            P("dp", "tensor"),
            P("dp", "tensor"),
            P("dp", "tensor"),
        ),
        out_specs=(
            P("dp", "tensor"),
            P("dp", "tensor"),
            P("dp", "tensor"),
            P("dp", "tensor"),
            P(("dp", "tensor"), None),
        ),
        check_vma=False,
    )
```

time: 218 us -> 181 us (0.83)
  starting transfers between devices: 60.8 us -> 27.4 us
  waiting for transfers between devices: 106 us -> 112 us
  other arithmetic: 17.5 us -> 12.9 us
  Pallas kernels: 20.2 us -> 17.9 us
    ppermute x18 -> x0, starting transfers between devices: 47.5 us -> none  [the longest x9 36.2 us: up(): return lax.ppermute(value, 'dp', pairs)]
    ppermute x22 -> x34, waiting for transfers between devices: 73.5 us -> 112 us  [flip(): lax.ppermute(value, axis, [(i, i ^ bit) for i in range(lax.axis_size(axis...]
    ppermute x18 -> x0, waiting for transfers between devices: 33 us -> none  [the longest x9 26.6 us: down(): return lax.ppermute(value, 'dp', pairs)]
    ppermute x22 -> x34, starting transfers between devices: 13.2 us -> 27.4 us  [flip(): lax.ppermute(value, axis, [(i, i ^ bit) for i in range(lax.axis_size(axis...]
    pallas_call x4, Pallas kernels: 8.35 us -> 3.23 us  [outward_part(): pl.pallas_call(outward_kernel, out_shape=[shape, shape], compiler_params=...]
    pallas_call x2 -> x4, Pallas kernels: 4.78 us -> 7.72 us  [gradient_part(): pl.pallas_call(functools.partial(gradient_kernel, scale), grid=(steps,),...]
    convert_element_type x10 -> x9, other arithmetic: 3.92 us -> 1.09 us  [add(): return (a.astype(f32) + b.astype(f32)).astype(bf16)]
    unnamed x41 -> x21, local copies, waits for them, and re-layouts: 4.93 us -> 2.56 us
  transfers between devices with their start and end apart: 40 -> 34, of which waited for: 20 -> 22; matrix products, arithmetic and copies ran while one was open for 6% -> 7% of each run, Pallas kernels for 5% -> 8%
where the time goes in v2:
time: 181 us
  waiting for transfers between devices  112 us (62%)
  starting transfers between devices  27.4 us (15%)
  Pallas kernels  17.9 us (10%)
  other arithmetic  12.9 us (7%)
  local copies, waits for them, and re-layouts  9.57 us (5%)
    ppermute x34, waiting for transfers between devices, flip(): lax.ppermute(value, axis, [(i, i ^ bit) for i in range(lax.axis_size(axis...  112 us
    ppermute x34, starting transfers between devices, flip(): lax.ppermute(value, axis, [(i, i ^ bit) for i in range(lax.axis_size(axis...  27.4 us
    pallas_call x4, Pallas kernels, gradient_part(): pl.pallas_call(functools.partial(gradient_kernel, scale), grid=(steps,),...  7.72 us
    pallas_call x1, Pallas kernels, attn_part(): pl.pallas_call(attn_kernel, grid=(n,), in_specs=[pl.BlockSpec((1, own, to...  6.95 us
    another operation x5, other arithmetic, local(): jnp.stack([jnp.concatenate([weights[r, h] for h in range(halves)]) for r...  4.73 us
  transfers between devices with their start and end apart: 34, of which 22 were waited for; matrix products, arithmetic and copies ran while one was open for 7% of the time, Pallas kernels for 8%

profile of v2, /device:TPU:0, one launch (start us, length us, event | category | flops | bytes accessed | tf_op | source)
XLA Modules:
  0.0 180.5 jit_solution(11554395165827478478)
XLA Ops:
  0.7 1.7 copy.18
  4.3 2.9 %collective-permute-start.3 = (bf16[4,576,128]{2,1,0:T(8,128)(2,1)S(1)}, bf16[4,576,128]{2,1,0:T(8,128)(2,1)S(1)}, u32[]{:S(2)}, u32[]{:S(2)}) collective-permute-start(bf16[4,576,128]{2,1,0:T(8,128)(2,1)S(1)} %get-tuple-element.58.refs_0_), channel_id=1, source_target_pairs={{0,2},{1,3},{2,0},{3,1},{4,6},{5,7},{6,4},{7,5},{8,10},{9,11},{10,... | collective-permute-start | bytes 1769480 | tf_op jit(solution)/shard_map/ppermute | solution.py:34
  7.2 1.5 collective-permute-start.2
  9.6 1.6 collective-permute-start
  11.2 2.6 %collective-permute-start.1 = (bf16[288,512]{1,0:T(8,128)(2,1)}, bf16[288,512]{1,0:T(8,128)(2,1)}, u32[]{:S(2)}, u32[]{:S(2)}) collective-permute-start(bf16[288,512]{1,0:T(8,128)(2,1)} %get-tuple-element.126), channel_id=1, source_target_pairs={{0,16},{4,20},{8,24},{12,28},{16,0},{20,4},{24,8},{28,12},{1,17},{... | collective-permute-start | bytes 884744 | tf_op jit(solution)/shard_map/ppermute | solution.py:34
  18.5 6.8 %collective-permute-done = bf16[288,512]{1,0:T(8,128)(2,1)} collective-permute-done((bf16[288,512]{1,0:T(8,128)(2,1)}, bf16[288,512]{1,0:T(8,128)(2,1)}, u32[]{:S(2)}, u32[]{:S(2)}) %collective-permute-start) | collective-permute-done | bytes 294944 | tf_op jit(solution)/shard_map/ppermute | solution.py:34
  25.3 2.4 %collective-permute-done.1 = bf16[288,512]{1,0:T(8,128)(2,1)} collective-permute-done((bf16[288,512]{1,0:T(8,128)(2,1)}, bf16[288,512]{1,0:T(8,128)(2,1)}, u32[]{:S(2)}, u32[]{:S(2)}) %collective-permute-start.1) | collective-permute-done | bytes 294944 | tf_op jit(solution)/shard_map/ppermute | solution.py:34
  30.6 1.7 collective-permute-start.7
  32.6 12.5 %collective-permute-done.9 = bf16[288,512]{1,0:T(8,128)(2,1)S(1)} collective-permute-done((bf16[288,512]{1,0:T(8,128)(2,1)}, bf16[288,512]{1,0:T(8,128)(2,1)S(1)}, u32[]{:S(2)}, u32[]{:S(2)}) %collective-permute-start.9) | collective-permute-done | bytes 294944 | tf_op jit(solution)/shard_map/ppermute | solution.py:34
  45.1 1.7 collective-permute-done.7
  46.9 5.5 %collective-permute-done.8 = bf16[288,512]{1,0:T(8,128)(2,1)S(1)} collective-permute-done((bf16[288,512]{1,0:T(8,128)(2,1)}, bf16[288,512]{1,0:T(8,128)(2,1)S(1)}, u32[]{:S(2)}, u32[]{:S(2)}) %collective-permute-start.8) | collective-permute-done | bytes 294944 | tf_op jit(solution)/shard_map/ppermute | solution.py:34
  52.4 2.0 %collective-permute-done.12.refs_7_ = bf16[4,576,128]{2,1,0:T(8,128)(2,1)S(1)} collective-permute-done((bf16[4,576,128]{2,1,0:T(8,128)(2,1)S(1)}, bf16[4,576,128]{2,1,0:T(8,128)(2,1)S(1)}, u32[]{:S(2)}, u32[]{:S(2)}) %collective-permute-start.12) | collective-permute-done | bytes 589856 | tf_op jit(solution)/shard_map/ppermute | solution.py:34
  55.2 1.9 %gradient_part.5 = bf16[576,512]{1,0:T(8,128)(2,1)S(1)} custom-call(bf16[4,576,128]{2,1,0:T(8,128)(2,1)S(1)} %get-tuple-element.58.refs_0_, bf16[4,576,128]{2,1,0:T(8,128)(2,1)S(1)} %collective-permute-done.3.refs_1_, bf16[4,576,128]{2,1,0:T(8,128)(2,1)S(1)} %collective-permute-done.4.refs_2_, bf16[4,576,128]{2,1,0:T(8,128)(2,1)S(1)} %collective-permute-done.6.refs_3_, ...), custom_call_target="tpu_custom_call" | custom-call | flops 603979776 | bytes 2818048 | tf_op jit(solution)/shard_map/gradient_part/pallas_call | solution.py:96
  59.0 1.9 %gradient_part.6 = bf16[576,512]{1,0:T(8,128)(2,1)S(1)} custom-call(bf16[4,576,128]{2,1,0:T(8,128)(2,1)S(1)} %get-tuple-element.58.refs_0_, bf16[4,576,128]{2,1,0:T(8,128)(2,1)S(1)} %collective-permute-done.3.refs_1_, bf16[4,576,128]{2,1,0:T(8,128)(2,1)S(1)} %collective-permute-done.4.refs_2_, bf16[4,576,128]{2,1,0:T(8,128)(2,1)S(1)} %collective-permute-done.6.refs_3_, ...), custom_call_target="tpu_custom_call" | custom-call | flops 603979776 | bytes 2818048 | tf_op jit(solution)/shard_map/gradient_part/pallas_call | solution.py:96
  60.9 1.9 %gradient_part.4 = bf16[576,512]{1,0:T(8,128)(2,1)S(1)} custom-call(bf16[4,576,128]{2,1,0:T(8,128)(2,1)S(1)} %get-tuple-element.58.refs_0_, bf16[4,576,128]{2,1,0:T(8,128)(2,1)S(1)} %collective-permute-done.3.refs_1_, bf16[4,576,128]{2,1,0:T(8,128)(2,1)S(1)} %collective-permute-done.4.refs_2_, bf16[4,576,128]{2,1,0:T(8,128)(2,1)S(1)} %collective-permute-done.6.refs_3_, ...), custom_call_target="tpu_custom_call" | custom-call | flops 603979776 | bytes 2818048 | tf_op jit(solution)/shard_map/gradient_part/pallas_call | solution.py:96
  62.8 9.7 %collective-permute-done.13 = bf16[576,512]{1,0:T(8,128)(2,1)S(1)} collective-permute-done((bf16[576,512]{1,0:T(8,128)(2,1)S(1)}, bf16[576,512]{1,0:T(8,128)(2,1)S(1)}, u32[]{:S(2)}, u32[]{:S(2)}) %collective-permute-start.13) | collective-permute-done | bytes 589856 | tf_op jit(solution)/shard_map/ppermute | solution.py:34
  73.0 2.8 %collective-permute-start.14 = (bf16[576,512]{1,0:T(8,128)(2,1)S(1)}, bf16[576,512]{1,0:T(8,128)(2,1)S(1)}, u32[]{:S(2)}, u32[]{:S(2)}) collective-permute-start(bf16[576,512]{1,0:T(8,128)(2,1)S(1)} %add_convert_fusion.4), channel_id=1, source_target_pairs={{0,16},{4,20},{8,24},{12,28},{16,0},{20,4},{24,8},{28,12},{1,17},{... | collective-permute-start | bytes 1769480 | tf_op jit(solution)/shard_map/ppermute | solution.py:34
  78.0 10.3 %collective-permute-done.16 = bf16[288,512]{1,0:T(8,128)(2,1)S(1)} collective-permute-done((bf16[288,512]{1,0:T(8,128)(2,1)S(1)}, bf16[288,512]{1,0:T(8,128)(2,1)S(1)}, u32[]{:S(2)}, u32[]{:S(2)}) %collective-permute-start.16) | collective-permute-done | bytes 294944 | tf_op jit(solution)/shard_map/ppermute | solution.py:34
  88.4 1.7 pad_maximum_fusion.refs_8_
  90.1 7.0 %attn_part.1 = (f32[512,512]{1,0:T(8,128)}, bf16[512,512]{1,0:T(8,128)(2,1)S(1)}) custom-call(bf16[4,576,128]{2,1,0:T(8,128)(2,1)S(1)} %get-tuple-element.58.refs_0_, bf16[4,576,128]{2,1,0:T(8,128)(2,1)S(1)} %collective-permute-done.3.refs_1_, bf16[4,576,128]{2,1,0:T(8,128)(2,1)S(1)} %collective-permute-done.4.refs_2_, ...), custom_call_target="tpu_custom_call" | custom-call | flops 2415919104 | bytes 8650752 | tf_op jit(solution)/shard_map/attn_part/pallas_call | solution.py:134
  97.6 2.1 %gradient_part.7 = bf16[576,512]{1,0:T(8,128)(2,1)S(1)} custom-call(bf16[4,576,128]{2,1,0:T(8,128)(2,1)S(1)} %get-tuple-element.58.refs_0_, bf16[4,576,128]{2,1,0:T(8,128)(2,1)S(1)} %collective-permute-done.3.refs_1_, bf16[4,576,128]{2,1,0:T(8,128)(2,1)S(1)} %collective-permute-done.4.refs_2_, bf16[4,576,128]{2,1,0:T(8,128)(2,1)S(1)} %collective-permute-done.6.refs_3_, ...), custom_call_target="tpu_custom_call" | custom-call | flops 603979776 | bytes 2818048 | tf_op jit(solution)/shard_map/gradient_part/pallas_call | solution.py:96
  99.8 1.5 collective-permute-done.14
  101.3 4.7 %collective-permute-done.15 = bf16[576,512]{1,0:T(8,128)(2,1)S(1)} collective-permute-done((bf16[576,512]{1,0:T(8,128)(2,1)S(1)}, bf16[576,512]{1,0:T(8,128)(2,1)S(1)}, u32[]{:S(2)}, u32[]{:S(2)}) %collective-permute-start.15) | collective-permute-done | bytes 589856 | tf_op jit(solution)/shard_map/ppermute | solution.py:34
  106.0 1.7 collective-permute-done.17
  107.8 2.5 %subtract_convert_fusion = (bf16[576,512]{1,0:T(8,128)(2,1)S(1)}, f32[576,512]{1,0:T(8,128)}, f32[576,512]{1,0:T(8,128)}) fusion(bf16[576,512]{1,0:T(8,128)(2,1)S(1)} %copy-done.3, bf16[576,512]{1,0:T(8,128)(2,1)S(1)} %collective-permute-done.15, bf16[576,512]{1,0:T(8,128)(2,1)S(1)} %collective-permute-done.14, bf16[576,512]{1,0:T(8,128)(2,1)S(1)} %gradient_part.7, ...), kind=kLoop, calls=%fused_computation.10 | loop fusion | flops 6193152 | bytes 7667712 | tf_op jit(solution)/shard_map/convert_element_type | solution.py:29
  111.3 1.9 %collective-permute-start.20 = (bf16[576,512]{1,0:T(8,128)(2,1)S(1)}, bf16[576,512]{1,0:T(8,128)(2,1)S(1)}, u32[]{:S(2)}, u32[]{:S(2)}) collective-permute-start(bf16[576,512]{1,0:T(8,128)(2,1)S(1)} %get-tuple-element.110.block), channel_id=1, source_target_pairs={{0,16},{4,20},{8,24},{12,28},{16,0},{20,4},{24,8},{28,12},{1,17},{... | collective-permute-start | bytes 1769480 | tf_op jit(solution)/shard_map/ppermute | solution.py:34
  114.5 23.8 %collective-permute-done.19.block = bf16[576,512]{1,0:T(8,128)(2,1)S(1)} collective-permute-done((bf16[576,512]{1,0:T(8,128)(2,1)S(1)}, bf16[576,512]{1,0:T(8,128)(2,1)S(1)}, u32[]{:S(2)}, u32[]{:S(2)}) %collective-permute-start.19) | collective-permute-done | bytes 589856 | tf_op jit(solution)/shard_map/ppermute | solution.py:34
  138.3 2.2 %collective-permute-done.20.block = bf16[576,512]{1,0:T(8,128)(2,1)S(1)} collective-permute-done((bf16[576,512]{1,0:T(8,128)(2,1)S(1)}, bf16[576,512]{1,0:T(8,128)(2,1)S(1)}, u32[]{:S(2)}, u32[]{:S(2)}) %collective-permute-start.20) | collective-permute-done | bytes 589856 | tf_op jit(solution)/shard_map/ppermute | solution.py:34
  147.7 9.5 %collective-permute-done.23.block = bf16[576,512]{1,0:T(8,128)(2,1)S(1)} collective-permute-done((bf16[576,512]{1,0:T(8,128)(2,1)S(1)}, bf16[576,512]{1,0:T(8,128)(2,1)S(1)}, u32[]{:S(2)}, u32[]{:S(2)}) %collective-permute-start.23) | collective-permute-done | bytes 589856 | tf_op jit(solution)/shard_map/ppermute | solution.py:34
  157.2 3.2 %collective-permute-done.27 = bf16[2,576,128]{2,1,0:T(8,128)(2,1)S(1)} collective-permute-done((bf16[2,576,128]{2,1,0:T(8,128)(2,1)S(1)}, bf16[2,576,128]{2,1,0:T(8,128)(2,1)S(1)}, u32[]{:S(2)}, u32[]{:S(2)}) %collective-permute-start.27) | collective-permute-done | bytes 294944 | tf_op jit(solution)/shard_map/ppermute | solution.py:34
  165.6 7.0 %collective-permute-done.30 = bf16[2,576,128]{2,1,0:T(8,128)(2,1)S(1)} collective-permute-done((bf16[2,576,128]{2,1,0:T(8,128)(2,1)S(1)}, bf16[2,576,128]{2,1,0:T(8,128)(2,1)S(1)}, u32[]{:S(2)}, u32[]{:S(2)}) %collective-permute-start.30) | collective-permute-done | bytes 294944 | tf_op jit(solution)/shard_map/ppermute | solution.py:34
  174.3 3.6 %collective-permute-done.33 = bf16[576,128]{1,0:T(8,128)(2,1)S(1)} collective-permute-done((bf16[576,128]{1,0:T(8,128)(2,1)S(1)}, bf16[576,128]{1,0:T(8,128)(2,1)S(1)}, u32[]{:S(2)}, u32[]{:S(2)}) %collective-permute-start.33) | collective-permute-done | bytes 147488 | tf_op jit(solution)/shard_map/ppermute | solution.py:34
  (111 shorter events, 35.6 us)
Async XLA Ops:
  4.3 23.4 %collective-permute-start.3 = (bf16[4,576,128]{2,1,0:T(8,128)(2,1)S(1)}, bf16[4,576,128]{2,1,0:T(8,128)(2,1)S(1)}, u32[]{:S(2)}, u32[]{:S(2)}) collective-permute-start(bf16[4,576,128]{2,1,0:T(8,128)(2,1)S(1)} %get-tuple-element.58.refs_0_), channel_id=1, source_target_pairs={{0,2},{1,3},{2,0},{3,1},{4,6},{5,7},{6,4},{7,5},{8,10},{9,11},{10,... | collective-permute-start | bytes 1769480 | tf_op jit(solution)/shard_map/ppermute | solution.py:34
  7.2 20.4 %collective-permute-start.4 = (bf16[4,576,128]{2,1,0:T(8,128)(2,1)S(1)}, bf16[4,576,128]{2,1,0:T(8,128)(2,1)S(1)}, u32[]{:S(2)}, u32[]{:S(2)}) collective-permute-start(bf16[4,576,128]{2,1,0:T(8,128)(2,1)S(1)} %get-tuple-element.58.refs_0_), channel_id=1, source_target_pairs={{0,1},{1,0},{2,3},{3,2},{4,5},{5,4},{6,7},{7,6},{8,9},{9,8},{10,11... | collective-permute-start | bytes 1769480 | tf_op jit(solution)/shard_map/ppermute | solution.py:34
  7.2 20.4 %collective-permute-start.2 = (bf16[4,576,128]{2,1,0:T(8,128)(2,1)}, bf16[4,576,128]{2,1,0:T(8,128)(2,1)S(1)}, u32[]{:S(2)}, u32[]{:S(2)}) collective-permute-start(bf16[4,576,128]{2,1,0:T(8,128)(2,1)} %get-tuple-element.59), channel_id=1, source_target_pairs={{0,4},{4,0},{8,12},{12,8},{16,20},{20,16},{24,28},{28,24},{1,5},{5... | collective-permute-start | bytes 1769480 | tf_op jit(solution)/shard_map/ppermute | solution.py:34
  9.6 15.6 %collective-permute-start = (bf16[288,512]{1,0:T(8,128)(2,1)}, bf16[288,512]{1,0:T(8,128)(2,1)}, u32[]{:S(2)}, u32[]{:S(2)}) collective-permute-start(bf16[288,512]{1,0:T(8,128)(2,1)} %get-tuple-element.126), channel_id=1, source_target_pairs={{0,8},{4,12},{8,0},{12,4},{16,24},{20,28},{24,16},{28,20},{1,9},{5... | collective-permute-start | bytes 884744 | tf_op jit(solution)/shard_map/ppermute | solution.py:34
  11.2 16.5 %collective-permute-start.1 = (bf16[288,512]{1,0:T(8,128)(2,1)}, bf16[288,512]{1,0:T(8,128)(2,1)}, u32[]{:S(2)}, u32[]{:S(2)}) collective-permute-start(bf16[288,512]{1,0:T(8,128)(2,1)} %get-tuple-element.126), channel_id=1, source_target_pairs={{0,16},{4,20},{8,24},{12,28},{16,0},{20,4},{24,8},{28,12},{1,17},{... | collective-permute-start | bytes 884744 | tf_op jit(solution)/shard_map/ppermute | solution.py:34
  27.7 2.1 %collective-permute-start.5 = (bf16[4,576,128]{2,1,0:T(8,128)(2,1)S(1)}, bf16[4,576,128]{2,1,0:T(8,128)(2,1)S(1)}, u32[]{:S(2)}, u32[]{:S(2)}) collective-permute-start(bf16[4,576,128]{2,1,0:T(8,128)(2,1)S(1)} %collective-permute-done.2.refs_4_), channel_id=1, source_target_pairs={{0,1},{1,0},{2,3},{3,2},{4,5},{5,4},{6,7},{7,6},{8,9},{9,8},{10,11... | collective-permute-start | bytes 1769480 | tf_op jit(solution)/shard_map/ppermute | solution.py:34
  27.8 2.8 %collective-permute-start.6 = (bf16[4,576,128]{2,1,0:T(8,128)(2,1)S(1)}, bf16[4,576,128]{2,1,0:T(8,128)(2,1)S(1)}, u32[]{:S(2)}, u32[]{:S(2)}) collective-permute-start(bf16[4,576,128]{2,1,0:T(8,128)(2,1)S(1)} %collective-permute-done.3.refs_1_), channel_id=1, source_target_pairs={{0,1},{1,0},{2,3},{3,2},{4,5},{5,4},{6,7},{7,6},{8,9},{9,8},{10,11... | collective-permute-start | bytes 1769480 | tf_op jit(solution)/shard_map/ppermute | solution.py:34
  28.2 16.9 %collective-permute-start.11 = (bf16[4,576,128]{2,1,0:T(8,128)(2,1)S(1)}, bf16[4,576,128]{2,1,0:T(8,128)(2,1)S(1)}, u32[]{:S(2)}, u32[]{:S(2)}) collective-permute-start(bf16[4,576,128]{2,1,0:T(8,128)(2,1)S(1)} %collective-permute-done.2.refs_4_), channel_id=1, source_target_pairs={{0,2},{1,3},{2,0},{3,1},{4,6},{5,7},{6,4},{7,5},{8,10},{9,11},{10,... | collective-permute-start | bytes 1769480 | tf_op jit(solution)/shard_map/ppermute | solution.py:34
  28.8 16.3 %collective-permute-start.10 = (bf16[512,512]{1,0:T(8,128)(2,1)S(1)}, bf16[512,512]{1,0:T(8,128)(2,1)S(1)}, u32[]{:S(2)}, u32[]{:S(2)}) collective-permute-start(bf16[512,512]{1,0:T(8,128)(2,1)S(1)} %bitcast.69), channel_id=1, source_target_pairs={{0,4},{4,0},{8,12},{12,8},{16,20},{20,16},{24,28},{28,24},{1,5},{5... | collective-permute-start | bytes 1572872 | tf_op jit(solution)/shard_map/ppermute | solution.py:34
  29.3 15.8 %collective-permute-start.9 = (bf16[288,512]{1,0:T(8,128)(2,1)}, bf16[288,512]{1,0:T(8,128)(2,1)S(1)}, u32[]{:S(2)}, u32[]{:S(2)}) collective-permute-start(bf16[288,512]{1,0:T(8,128)(2,1)} %get-tuple-element.68), channel_id=1, source_target_pairs={{0,16},{4,20},{8,24},{12,28},{16,0},{20,4},{24,8},{28,12},{1,17},{... | collective-permute-start | bytes 884744 | tf_op jit(solution)/shard_map/ppermute | solution.py:34
  30.6 16.3 %collective-permute-start.7 = (bf16[288,512]{1,0:T(8,128)(2,1)}, bf16[288,512]{1,0:T(8,128)(2,1)S(1)}, u32[]{:S(2)}, u32[]{:S(2)}) collective-permute-start(bf16[288,512]{1,0:T(8,128)(2,1)} %collective-permute-done.1), channel_id=1, source_target_pairs={{0,8},{4,12},{8,0},{12,4},{16,24},{20,28},{24,16},{28,20},{1,9},{5... | collective-permute-start | bytes 884744 | tf_op jit(solution)/shard_map/ppermute | solution.py:34
  32.3 20.1 %collective-permute-start.8 = (bf16[288,512]{1,0:T(8,128)(2,1)}, bf16[288,512]{1,0:T(8,128)(2,1)S(1)}, u32[]{:S(2)}, u32[]{:S(2)}) collective-permute-start(bf16[288,512]{1,0:T(8,128)(2,1)} %get-tuple-element.68), channel_id=1, source_target_pairs={{0,8},{4,12},{8,0},{12,4},{16,24},{20,28},{24,16},{28,20},{1,9},{5... | collective-permute-start | bytes 884744 | tf_op jit(solution)/shard_map/ppermute | solution.py:34
  57.1 15.4 %collective-permute-start.13 = (bf16[576,512]{1,0:T(8,128)(2,1)S(1)}, bf16[576,512]{1,0:T(8,128)(2,1)S(1)}, u32[]{:S(2)}, u32[]{:S(2)}) collective-permute-start(bf16[576,512]{1,0:T(8,128)(2,1)S(1)} %gradient_part.5), channel_id=1, source_target_pairs={{0,8},{4,12},{8,0},{12,4},{16,24},{20,28},{24,16},{28,20},{1,9},{5... | collective-permute-start | bytes 1769480 | tf_op jit(solution)/shard_map/ppermute | solution.py:34
  57.3 42.5 %collective-permute-start.18 = (bf16[512,512]{1,0:T(8,128)(2,1)S(1)}, bf16[512,512]{1,0:T(8,128)(2,1)S(1)}, u32[]{:S(2)}, u32[]{:S(2)}) collective-permute-start(bf16[512,512]{1,0:T(8,128)(2,1)S(1)} %bitcast.74), channel_id=1, source_target_pairs={{0,4},{4,0},{8,12},{12,8},{16,20},{20,16},{24,28},{28,24},{1,5},{5... | collective-permute-start | bytes 1572872 | tf_op jit(solution)/shard_map/ppermute | solution.py:34
  72.5 15.8 %collective-permute-start.16 = (bf16[288,512]{1,0:T(8,128)(2,1)S(1)}, bf16[288,512]{1,0:T(8,128)(2,1)S(1)}, u32[]{:S(2)}, u32[]{:S(2)}) collective-permute-start(bf16[288,512]{1,0:T(8,128)(2,1)S(1)} %collective-permute-done.9), channel_id=1, source_target_pairs={{0,8},{4,12},{8,0},{12,4},{16,24},{20,28},{24,16},{28,20},{1,9},{5... | collective-permute-start | bytes 884744 | tf_op jit(solution)/shard_map/ppermute | solution.py:34
  73.0 28.3 %collective-permute-start.14 = (bf16[576,512]{1,0:T(8,128)(2,1)S(1)}, bf16[576,512]{1,0:T(8,128)(2,1)S(1)}, u32[]{:S(2)}, u32[]{:S(2)}) collective-permute-start(bf16[576,512]{1,0:T(8,128)(2,1)S(1)} %add_convert_fusion.4), channel_id=1, source_target_pairs={{0,16},{4,20},{8,24},{12,28},{16,0},{20,4},{24,8},{28,12},{1,17},{... | collective-permute-start | bytes 1769480 | tf_op jit(solution)/shard_map/ppermute | solution.py:34
  75.8 30.3 %collective-permute-start.15 = (bf16[576,512]{1,0:T(8,128)(2,1)S(1)}, bf16[576,512]{1,0:T(8,128)(2,1)S(1)}, u32[]{:S(2)}, u32[]{:S(2)}) collective-permute-start(bf16[576,512]{1,0:T(8,128)(2,1)S(1)} %gradient_part.6), channel_id=1, source_target_pairs={{0,8},{4,12},{8,0},{12,4},{16,24},{20,28},{24,16},{28,20},{1,9},{5... | collective-permute-start | bytes 1769480 | tf_op jit(solution)/shard_map/ppermute | solution.py:34
  97.0 10.7 %collective-permute-start.17 = (bf16[512,512]{1,0:T(8,128)(2,1)S(1)}, bf16[512,512]{1,0:T(8,128)(2,1)S(1)}, u32[]{:S(2)}, u32[]{:S(2)}) collective-permute-start(bf16[512,512]{1,0:T(8,128)(2,1)S(1)} %get-tuple-element.82), channel_id=1, source_target_pairs={{0,4},{4,0},{8,12},{12,8},{16,20},{20,16},{24,28},{28,24},{1,5},{5... | collective-permute-start | bytes 1572872 | tf_op jit(solution)/shard_map/ppermute | solution.py:34
  111.1 2.1 %collective-permute-start.21 = (bf16[2,2,576,128]{3,2,1,0:T(8,128)(2,1)S(1)}, bf16[2,2,576,128]{3,2,1,0:T(8,128)(2,1)S(1)}, u32[]{:S(2)}, u32[]{:S(2)}) collective-permute-start(bf16[2,2,576,128]{3,2,1,0:T(8,128)(2,1)S(1)} %get-tuple-element.89), channel_id=1, source_target_pairs={{0,1},{1,0},{2,3},{3,2},{4,5},{5,4},{6,7},{7,6},{8,9},{9,8},{10,11... | collective-permute-start | bytes 1769480 | tf_op jit(solution)/shard_map/ppermute | solution.py:34
  111.2 27.2 %collective-permute-start.19 = (bf16[576,512]{1,0:T(8,128)(2,1)S(1)}, bf16[576,512]{1,0:T(8,128)(2,1)S(1)}, u32[]{:S(2)}, u32[]{:S(2)}) collective-permute-start(bf16[576,512]{1,0:T(8,128)(2,1)S(1)} %get-tuple-element.110.block), channel_id=1, source_target_pairs={{0,8},{4,12},{8,0},{12,4},{16,24},{20,28},{24,16},{28,20},{1,9},{5... | collective-permute-start | bytes 1769480 | tf_op jit(solution)/shard_map/ppermute | solution.py:34
  111.3 29.2 %collective-permute-start.20 = (bf16[576,512]{1,0:T(8,128)(2,1)S(1)}, bf16[576,512]{1,0:T(8,128)(2,1)S(1)}, u32[]{:S(2)}, u32[]{:S(2)}) collective-permute-start(bf16[576,512]{1,0:T(8,128)(2,1)S(1)} %get-tuple-element.110.block), channel_id=1, source_target_pairs={{0,16},{4,20},{8,24},{12,28},{16,0},{20,4},{24,8},{28,12},{1,17},{... | collective-permute-start | bytes 1769480 | tf_op jit(solution)/shard_map/ppermute | solution.py:34
  113.4 27.1 %collective-permute-start.22 = (bf16[2,576,128]{2,1,0:T(8,128)(2,1)S(1)}, bf16[2,576,128]{2,1,0:T(8,128)(2,1)S(1)}, u32[]{:S(2)}, u32[]{:S(2)}) collective-permute-start(bf16[2,576,128]{2,1,0:T(8,128)(2,1)S(1)} %get-tuple-element.123), channel_id=1, source_target_pairs={{0,2},{1,3},{2,0},{3,1},{4,6},{5,7},{6,4},{7,5},{8,10},{9,11},{10,... | collective-permute-start | bytes 884744 | tf_op jit(solution)/shard_map/ppermute | solution.py:34
  141.3 2.1 %collective-permute-start.24 = (bf16[2,2,576,128]{3,2,1,0:T(8,128)(2,1)S(1)}, bf16[2,2,576,128]{3,2,1,0:T(8,128)(2,1)S(1)}, u32[]{:S(2)}, u32[]{:S(2)}) collective-permute-start(bf16[2,2,576,128]{3,2,1,0:T(8,128)(2,1)S(1)} %get-tuple-element.95), channel_id=1, source_target_pairs={{0,1},{1,0},{2,3},{3,2},{4,5},{5,4},{6,7},{7,6},{8,9},{9,8},{10,11... | collective-permute-start | bytes 1769480 | tf_op jit(solution)/shard_map/ppermute | solution.py:34
  141.4 15.8 %collective-permute-start.23 = (bf16[576,512]{1,0:T(8,128)(2,1)S(1)}, bf16[576,512]{1,0:T(8,128)(2,1)S(1)}, u32[]{:S(2)}, u32[]{:S(2)}) collective-permute-start(bf16[576,512]{1,0:T(8,128)(2,1)S(1)} %collective-permute-done.20.block), channel_id=1, source_target_pairs={{0,8},{4,12},{8,0},{12,4},{16,24},{20,28},{24,16},{28,20},{1,9},{5... | collective-permute-start | bytes 1769480 | tf_op jit(solution)/shard_map/ppermute | solution.py:34
  142.3 2.2 %collective-permute-start.25 = (bf16[2,2,576,128]{3,2,1,0:T(8,128)(2,1)S(1)}, bf16[2,2,576,128]{3,2,1,0:T(8,128)(2,1)S(1)}, u32[]{:S(2)}, u32[]{:S(2)}) collective-permute-start(bf16[2,2,576,128]{3,2,1,0:T(8,128)(2,1)S(1)} %get-tuple-element.97), channel_id=1, source_target_pairs={{0,1},{1,0},{2,3},{3,2},{4,5},{5,4},{6,7},{7,6},{8,9},{9,8},{10,11... | collective-permute-start | bytes 1769480 | tf_op jit(solution)/shard_map/ppermute | solution.py:34
  144.7 12.5 %collective-permute-start.26 = (bf16[2,576,128]{2,1,0:T(8,128)(2,1)S(1)}, bf16[2,576,128]{2,1,0:T(8,128)(2,1)S(1)}, u32[]{:S(2)}, u32[]{:S(2)}) collective-permute-start(bf16[2,576,128]{2,1,0:T(8,128)(2,1)S(1)} %get-tuple-element.121), channel_id=1, source_target_pairs={{0,2},{1,3},{2,0},{3,1},{4,6},{5,7},{6,4},{7,5},{8,10},{9,11},{10,... | collective-permute-start | bytes 884744 | tf_op jit(solution)/shard_map/ppermute | solution.py:34
  145.4 15.0 %collective-permute-start.27 = (bf16[2,576,128]{2,1,0:T(8,128)(2,1)S(1)}, bf16[2,576,128]{2,1,0:T(8,128)(2,1)S(1)}, u32[]{:S(2)}, u32[]{:S(2)}) collective-permute-start(bf16[2,576,128]{2,1,0:T(8,128)(2,1)S(1)} %get-tuple-element.119), channel_id=1, source_target_pairs={{0,2},{1,3},{2,0},{3,1},{4,6},{5,7},{6,4},{7,5},{8,10},{9,11},{10,... | collective-permute-start | bytes 884744 | tf_op jit(solution)/shard_map/ppermute | solution.py:34
  146.8 10.4 %collective-permute-start.28 = (bf16[576,128]{1,0:T(8,128)(2,1)S(1)}, bf16[576,128]{1,0:T(8,128)(2,1)S(1)}, u32[]{:S(2)}, u32[]{:S(2)}) collective-permute-start(bf16[576,128]{1,0:T(8,128)(2,1)S(1)} %get-tuple-element.133), channel_id=1, source_target_pairs={{0,4},{4,0},{8,12},{12,8},{16,20},{20,16},{24,28},{28,24},{1,5},{5... | collective-permute-start | bytes 442376 | tf_op jit(solution)/shard_map/ppermute | solution.py:34
  161.5 12.8 %collective-permute-start.32 = (bf16[576,128]{1,0:T(8,128)(2,1)S(1)}, bf16[576,128]{1,0:T(8,128)(2,1)S(1)}, u32[]{:S(2)}, u32[]{:S(2)}) collective-permute-start(bf16[576,128]{1,0:T(8,128)(2,1)S(1)} %get-tuple-element.130), channel_id=1, source_target_pairs={{0,4},{4,0},{8,12},{12,8},{16,20},{20,16},{24,28},{28,24},{1,5},{5... | collective-permute-start | bytes 442376 | tf_op jit(solution)/shard_map/ppermute | solution.py:34
  163.4 9.1 %collective-permute-start.30 = (bf16[2,576,128]{2,1,0:T(8,128)(2,1)S(1)}, bf16[2,576,128]{2,1,0:T(8,128)(2,1)S(1)}, u32[]{:S(2)}, u32[]{:S(2)}) collective-permute-start(bf16[2,576,128]{2,1,0:T(8,128)(2,1)S(1)} %slice_bitcast_fusion), channel_id=1, source_target_pairs={{0,2},{1,3},{2,0},{3,1},{4,6},{5,7},{6,4},{7,5},{8,10},{9,11},{10,... | collective-permute-start | bytes 884744 | tf_op jit(solution)/shard_map/ppermute | solution.py:34
  164.2 10.0 %collective-permute-start.31 = (bf16[576,128]{1,0:T(8,128)(2,1)S(1)}, bf16[576,128]{1,0:T(8,128)(2,1)S(1)}, u32[]{:S(2)}, u32[]{:S(2)}) collective-permute-start(bf16[576,128]{1,0:T(8,128)(2,1)S(1)} %get-tuple-element.128), channel_id=1, source_target_pairs={{0,4},{4,0},{8,12},{12,8},{16,20},{20,16},{24,28},{28,24},{1,5},{5... | collective-permute-start | bytes 442376 | tf_op jit(solution)/shard_map/ppermute | solution.py:34
  172.7 5.2 %collective-permute-start.33 = (bf16[576,128]{1,0:T(8,128)(2,1)S(1)}, bf16[576,128]{1,0:T(8,128)(2,1)S(1)}, u32[]{:S(2)}, u32[]{:S(2)}) collective-permute-start(bf16[576,128]{1,0:T(8,128)(2,1)S(1)} %get-tuple-element.132), channel_id=1, source_target_pairs={{0,4},{4,0},{8,12},{12,8},{16,20},{20,16},{24,28},{28,24},{1,5},{5... | collective-permute-start | bytes 442376 | tf_op jit(solution)/shard_map/ppermute | solution.py:34
  (12 other events, 71.6 us)

commit v3 on v2

--- a/solution.py
+++ b/solution.py
@@ -183,45 +183,32 @@
     order = [n - 1] + [r for r in range(1, n - 1)] + [0]
     top = n // 2
     levels = [[r for r in range(n) if r.bit_count() == k] for k in range(n.bit_length())]
-    low, multi = levels[1][:-1], [r for level in levels[2:] for r in level]
-    halves = 2 if own % 32 == 0 else 1
-
-    weights = {(0, h): part for h, part in enumerate(jnp.split(weight, halves))}
-
-    def fetch(keys):
-        for r, h in keys:
-            weights[r, h] = to_plane(weights[r & (r - 1), h], r & -r)
-
-    def hold(keys, *others):
-        came, *others = stage([weights[k] for k in keys], *others)
-        weights.update(zip(keys, came))
-        return others
-
-    second = [(r, 1) for r in range(n)] if halves > 1 else []
+
+    weights = {0: weight}
+    for r in reversed(levels[1]):
+        weights[r] = to_plane(weight, r)
 
     blocks = cotangent.T.reshape(n, 2, own, tok)
     blocks = jnp.take(blocks, z ^ jnp.array(order), axis=0)
     mine = jnp.where(y == 0, blocks[:, 0], blocks[:, 1])
     other = jnp.where(y == 0, blocks[:, 1], blocks[:, 0])
     mine, other = stage(mine, other)
-    fetch([(top, 0)] + [(r, 0) for r in low])
     partner = to_partner(other)
     mine_x = to_chip(mine)
     mine_c = to_core(mine)
     saved0 = relative(attn_saved, x, c)
-    keys = [(r, 0) for r in levels[1]] + second[:1]
-    partner, mine_x, mine_c, saved0 = hold(keys, partner, mine_x, mine_c, saved0)
+    partner, mine_x, mine_c, saved0 = stage(partner, mine_x, mine_c, saved0)
 
     saved1 = to_partner(saved0)
     partner_x = to_chip(partner)
     partner_c = to_core(partner)
+    came, saved1, partner_c, mine_x = stage([weights[r] for r in levels[1]], saved1, partner_c, mine_x)
+    weights.update(zip(levels[1], came))
     mine_xc = to_core(mine_x)
-    fetch([k for k in second if k[0] == top])
-    keys = [(r, 0) for r in levels[1]] + second[:1]
-    partner_c, mine_xc = hold(keys, partner_c, mine_xc)
-    fetch([(r, 0) for r in multi] + [k for k in second if k[0] in low])
-    keys = [(r, 0) for r in multi] + [k for k in second if k[0] in levels[1]]
-    saved1, partner_x = hold(keys, saved1, partner_x)
+    partner_x, mine_xc = stage(partner_x, mine_xc)
+    for level in levels[2:]:
+        for r in level:
+            weights[r] = to_plane(weights[r & (r - 1)], r & -r)
     partner_xc = to_core(partner_x)
     pieces = [mine, mine_x, mine_c, mine_xc, partner, partner_x, partner_c, partner_xc]
 
@@ -239,16 +226,13 @@
             sums[r ^ m] = add(sums[r ^ m], value)
         m *= 2
     ends = [1 << k for k in reversed(range(n.bit_length() - 1))]
-    (came,) = hold([k for k in second if k[0] in levels[1]], came)
-    fetch([k for k in second if k[0] in multi])
+    gathered, _ = stage([weights[r] for r in order], came)
+    gathered = jnp.stack(gathered)
     came = [to_plane(sums[m], m) for m in ends]
-    gathered = jnp.stack([jnp.concatenate([weights[r, h] for h in range(halves)]) for r in order])
     kept, sent = attn_part(pieces, gathered)
-    sent = to_partner(sent)
-    came, kept, sent, next1 = stage(came, kept, sent, next1)
+    came, next1, attn = stage(came, next1, [kept, sent])
     gradient = sums[0].astype(f32) + functools.reduce(jnp.add, [v.astype(f32) for v in came])
     new_weight, new_moment1, new_moment2 = adamw_step(gradient, weight, moment1, moment2)
-    grad_attn = absolute((kept + sent.astype(f32)).astype(bf16), x, c)
 
     held, results = {0: new_weight}, {}
     for k, wave in enumerate(levels):
@@ -262,12 +246,15 @@
             kept[r], came[r] = half[0], to_chip(half[1])
         if later:
             blocks, kept = stage([held[r] for r in later], kept)
-            blocks, came, results = stage(blocks, came, results)
+            if k == 0:
+                attn = [attn[0], to_partner(attn[1])]
+            blocks, came, results, attn = stage(blocks, came, results, attn)
             held.update(zip(later, blocks))
         for r in wave:
             total = add(kept[r], came[r])
             results[r] = (total[0], to_partner(total[1]))
 
+    grad_attn = absolute((attn[0] + attn[1].astype(f32)).astype(bf16), x, c)
     mine = jnp.stack([results[r][0] for r in range(n)])
     other = jnp.stack([results[r][1] for r in range(n)])
     both = jnp.stack([jnp.where(y == 0, mine, other), jnp.where(y == 0, other, mine)], axis=1)

time: 181 us -> 172 us (0.950)
  waiting for transfers between devices: 112 us -> 107 us
  other arithmetic: 12.9 us -> 9.39 us
    ppermute x34 -> x31, waiting for transfers between devices: 112 us -> 107 us  [flip(): lax.ppermute(value, axis, [(i, i ^ bit) for i in range(lax.axis_size(axis...]
    another operation x5 -> x1, other arithmetic: 4.73 us -> 2.83 us  [local(): gathered = jnp.stack(gathered)]
    ppermute x34 -> x31, starting transfers between devices: 27.4 us -> 28.9 us  [flip(): lax.ppermute(value, axis, [(i, i ^ bit) for i in range(lax.axis_size(axis...]
  transfers between devices with their start and end apart: 34 -> 31, of which waited for: 22 -> 17; matrix products, arithmetic and copies ran while one was open for 7% -> 4% of each run, Pallas kernels for 8% -> 8%
where the time goes in v3:
time: 172 us
  waiting for transfers between devices  107 us (62%)
  starting transfers between devices  28.9 us (17%)
  Pallas kernels  17.8 us (10%)
  other arithmetic  9.39 us (5%)
  local copies, waits for them, and re-layouts  8.07 us (5%)
    ppermute x31, waiting for transfers between devices, flip(): lax.ppermute(value, axis, [(i, i ^ bit) for i in range(lax.axis_size(axis...  107 us
    ppermute x31, starting transfers between devices, flip(): lax.ppermute(value, axis, [(i, i ^ bit) for i in range(lax.axis_size(axis...  28.9 us
    pallas_call x4, Pallas kernels, gradient_part(): pl.pallas_call(functools.partial(gradient_kernel, scale), grid=(steps,),...  7.43 us
    pallas_call x1, Pallas kernels, attn_part(): pl.pallas_call(attn_kernel, grid=(n,), in_specs=[pl.BlockSpec((1, own, to...  7.1 us
  transfers between devices with their start and end apart: 31, of which 17 were waited for; matrix products, arithmetic and copies ran while one was open for 4% of the time, Pallas kernels for 8%

profile of v3, /device:TPU:0, one launch (start us, length us, event | category | flops | bytes accessed | tf_op | source)
XLA Modules:
  0.0 171.6 jit_solution(12764104184829094763)
XLA Ops:
  1.3 1.7 copy.18
  4.9 3.0 %collective-permute-start.2 = (bf16[4,576,128]{2,1,0:T(8,128)(2,1)}, bf16[4,576,128]{2,1,0:T(8,128)(2,1)S(1)}, u32[]{:S(2)}, u32[]{:S(2)}) collective-permute-start(bf16[4,576,128]{2,1,0:T(8,128)(2,1)} %get-tuple-element.59), channel_id=1, source_target_pairs={{0,4},{4,0},{8,12},{12,8},{16,20},{20,16},{24,28},{28,24},{1,5},{5... | collective-permute-start | bytes 1769480 | tf_op jit(solution)/shard_map/ppermute | solution.py:34
  7.9 1.5 collective-permute-start.3
  9.4 1.6 collective-permute-start
  10.9 2.6 %collective-permute-start.1 = (bf16[576,512]{1,0:T(8,128)(2,1)S(1)}, bf16[576,512]{1,0:T(8,128)(2,1)}, u32[]{:S(2)}, u32[]{:S(2)}) collective-permute-start(bf16[576,512]{1,0:T(8,128)(2,1)S(1)} %copy-done.3), channel_id=1, source_target_pairs={{0,16},{4,20},{8,24},{12,28},{16,0},{20,4},{24,8},{28,12},{1,17},{... | collective-permute-start | bytes 1769480 | tf_op jit(solution)/shard_map/ppermute | solution.py:34
  15.1 6.3 %collective-permute-done.2.refs_4_ = bf16[4,576,128]{2,1,0:T(8,128)(2,1)S(1)} collective-permute-done((bf16[4,576,128]{2,1,0:T(8,128)(2,1)}, bf16[4,576,128]{2,1,0:T(8,128)(2,1)S(1)}, u32[]{:S(2)}, u32[]{:S(2)}) %collective-permute-start.2) | collective-permute-done | bytes 589856 | tf_op jit(solution)/shard_map/ppermute | solution.py:34
  21.4 2.2 %collective-permute-done.3.refs_1_ = bf16[4,576,128]{2,1,0:T(8,128)(2,1)S(1)} collective-permute-done((bf16[4,576,128]{2,1,0:T(8,128)(2,1)S(1)}, bf16[4,576,128]{2,1,0:T(8,128)(2,1)S(1)}, u32[]{:S(2)}, u32[]{:S(2)}) %collective-permute-start.3) | collective-permute-done | bytes 589856 | tf_op jit(solution)/shard_map/ppermute | solution.py:34
  23.9 1.7 %collective-permute-start.7 = (bf16[4,576,128]{2,1,0:T(8,128)(2,1)S(1)}, bf16[4,576,128]{2,1,0:T(8,128)(2,1)S(1)}, u32[]{:S(2)}, u32[]{:S(2)}) collective-permute-start(bf16[4,576,128]{2,1,0:T(8,128)(2,1)S(1)} %collective-permute-done.2.refs_4_), channel_id=1, source_target_pairs={{0,2},{1,3},{2,0},{3,1},{4,6},{5,7},{6,4},{7,5},{8,10},{9,11},{10,... | collective-permute-start | bytes 1769480 | tf_op jit(solution)/shard_map/ppermute | solution.py:34
  25.6 11.7 %collective-permute-done = bf16[576,512]{1,0:T(8,128)(2,1)S(1)} collective-permute-done((bf16[576,512]{1,0:T(8,128)(2,1)S(1)}, bf16[576,512]{1,0:T(8,128)(2,1)S(1)}, u32[]{:S(2)}, u32[]{:S(2)}) %collective-permute-start) | collective-permute-done | bytes 589856 | tf_op jit(solution)/shard_map/ppermute | solution.py:34
  37.4 2.5 %collective-permute-done.1 = bf16[576,512]{1,0:T(8,128)(2,1)} collective-permute-done((bf16[576,512]{1,0:T(8,128)(2,1)S(1)}, bf16[576,512]{1,0:T(8,128)(2,1)}, u32[]{:S(2)}, u32[]{:S(2)}) %collective-permute-start.1) | collective-permute-done | bytes 589856 | tf_op jit(solution)/shard_map/ppermute | solution.py:34
  39.8 2.0 %collective-permute-done.8.refs_3_ = bf16[4,576,128]{2,1,0:T(8,128)(2,1)S(1)} collective-permute-done((bf16[4,576,128]{2,1,0:T(8,128)(2,1)S(1)}, bf16[4,576,128]{2,1,0:T(8,128)(2,1)S(1)}, u32[]{:S(2)}, u32[]{:S(2)}) %collective-permute-start.8) | collective-permute-done | bytes 589856 | tf_op jit(solution)/shard_map/ppermute | solution.py:34
  42.0 1.9 %collective-permute-done.9.refs_7_ = bf16[4,576,128]{2,1,0:T(8,128)(2,1)S(1)} collective-permute-done((bf16[4,576,128]{2,1,0:T(8,128)(2,1)S(1)}, bf16[4,576,128]{2,1,0:T(8,128)(2,1)S(1)}, u32[]{:S(2)}, u32[]{:S(2)}) %collective-permute-start.9) | collective-permute-done | bytes 589856 | tf_op jit(solution)/shard_map/ppermute | solution.py:34
  44.7 1.9 %gradient_part.6 = bf16[576,512]{1,0:T(8,128)(2,1)S(1)} custom-call(bf16[4,576,128]{2,1,0:T(8,128)(2,1)S(1)} %get-tuple-element.58.refs_0_, bf16[4,576,128]{2,1,0:T(8,128)(2,1)S(1)} %collective-permute-done.3.refs_1_, bf16[4,576,128]{2,1,0:T(8,128)(2,1)S(1)} %collective-permute-done.4.refs_2_, bf16[4,576,128]{2,1,0:T(8,128)(2,1)S(1)} %collective-permute-done.8.refs_3_, ...), custom_call_target="tpu_custom_call" | custom-call | flops 603979776 | bytes 2818048 | tf_op jit(solution)/shard_map/gradient_part/pallas_call | solution.py:96
  47.0 1.6 collective-permute-start.14
  48.6 1.9 %gradient_part.7 = bf16[576,512]{1,0:T(8,128)(2,1)S(1)} custom-call(bf16[4,576,128]{2,1,0:T(8,128)(2,1)S(1)} %get-tuple-element.58.refs_0_, bf16[4,576,128]{2,1,0:T(8,128)(2,1)S(1)} %collective-permute-done.3.refs_1_, bf16[4,576,128]{2,1,0:T(8,128)(2,1)S(1)} %collective-permute-done.4.refs_2_, bf16[4,576,128]{2,1,0:T(8,128)(2,1)S(1)} %collective-permute-done.8.refs_3_, ...), custom_call_target="tpu_custom_call" | custom-call | flops 603979776 | bytes 2818048 | tf_op jit(solution)/shard_map/gradient_part/pallas_call | solution.py:96
  50.5 1.9 %gradient_part.5 = bf16[576,512]{1,0:T(8,128)(2,1)S(1)} custom-call(bf16[4,576,128]{2,1,0:T(8,128)(2,1)S(1)} %get-tuple-element.58.refs_0_, bf16[4,576,128]{2,1,0:T(8,128)(2,1)S(1)} %collective-permute-done.3.refs_1_, bf16[4,576,128]{2,1,0:T(8,128)(2,1)S(1)} %collective-permute-done.4.refs_2_, bf16[4,576,128]{2,1,0:T(8,128)(2,1)S(1)} %collective-permute-done.8.refs_3_, ...), custom_call_target="tpu_custom_call" | custom-call | flops 603979776 | bytes 2818048 | tf_op jit(solution)/shard_map/gradient_part/pallas_call | solution.py:96
  52.3 10.4 %collective-permute-done.10 = bf16[576,512]{1,0:T(8,128)(2,1)S(1)} collective-permute-done((bf16[576,512]{1,0:T(8,128)(2,1)S(1)}, bf16[576,512]{1,0:T(8,128)(2,1)S(1)}, u32[]{:S(2)}, u32[]{:S(2)}) %collective-permute-start.10) | collective-permute-done | bytes 589856 | tf_op jit(solution)/shard_map/ppermute | solution.py:34
  64.0 2.1 %collective-permute-start.12 = (bf16[576,512]{1,0:T(8,128)(2,1)S(1)}, bf16[576,512]{1,0:T(8,128)(2,1)S(1)}, u32[]{:S(2)}, u32[]{:S(2)}) collective-permute-start(bf16[576,512]{1,0:T(8,128)(2,1)S(1)} %gradient_part.7), channel_id=1, source_target_pairs={{0,8},{4,12},{8,0},{12,4},{16,24},{20,28},{24,16},{28,20},{1,9},{5... | collective-permute-start | bytes 1769480 | tf_op jit(solution)/shard_map/ppermute | solution.py:34
  66.7 1.9 %gradient_part.4 = bf16[576,512]{1,0:T(8,128)(2,1)S(1)} custom-call(bf16[4,576,128]{2,1,0:T(8,128)(2,1)S(1)} %get-tuple-element.58.refs_0_, bf16[4,576,128]{2,1,0:T(8,128)(2,1)S(1)} %collective-permute-done.3.refs_1_, bf16[4,576,128]{2,1,0:T(8,128)(2,1)S(1)} %collective-permute-done.4.refs_2_, bf16[4,576,128]{2,1,0:T(8,128)(2,1)S(1)} %collective-permute-done.8.refs_3_, ...), custom_call_target="tpu_custom_call" | custom-call | flops 603979776 | bytes 2818048 | tf_op jit(solution)/shard_map/gradient_part/pallas_call | solution.py:96
  68.5 17.3 %collective-permute-done.14 = bf16[576,512]{1,0:T(8,128)(2,1)S(1)} collective-permute-done((bf16[576,512]{1,0:T(8,128)(2,1)}, bf16[576,512]{1,0:T(8,128)(2,1)S(1)}, u32[]{:S(2)}, u32[]{:S(2)}) %collective-permute-start.14) | collective-permute-done | bytes 589856 | tf_op jit(solution)/shard_map/ppermute | solution.py:34
  85.8 2.8 %pad_maximum_fusion.refs_8_ = bf16[4,576,512]{2,1,0:T(8,128)(2,1)} fusion(bf16[1,576,512]{2,1,0:T(8,128)(2,1)S(1)} %bitcast.77, bf16[1,576,512]{2,1,0:T(8,128)(2,1)} %bitcast.12, bf16[1,576,512]{2,1,0:T(8,128)(2,1)S(1)} %bitcast.80, bf16[1,576,512]{2,1,0:T(8,128)(2,1)S(1)} %bitcast.81), kind=kLoop, calls=%fused_computation.2 | loop fusion | flops 3538944 | bytes 4718592 | tf_op jit(solution)/shard_map/stack | solution.py:230
  88.6 7.1 %attn_part.1 = (f32[512,512]{1,0:T(8,128)}, bf16[512,512]{1,0:T(8,128)(2,1)S(1)}) custom-call(bf16[4,576,128]{2,1,0:T(8,128)(2,1)S(1)} %get-tuple-element.58.refs_0_, bf16[4,576,128]{2,1,0:T(8,128)(2,1)S(1)} %collective-permute-done.3.refs_1_, bf16[4,576,128]{2,1,0:T(8,128)(2,1)S(1)} %collective-permute-done.4.refs_2_, ...), custom_call_target="tpu_custom_call" | custom-call | flops 2415919104 | bytes 8650752 | tf_op jit(solution)/shard_map/attn_part/pallas_call | solution.py:134
  95.8 4.1 %collective-permute-done.12 = bf16[576,512]{1,0:T(8,128)(2,1)S(1)} collective-permute-done((bf16[576,512]{1,0:T(8,128)(2,1)S(1)}, bf16[576,512]{1,0:T(8,128)(2,1)S(1)}, u32[]{:S(2)}, u32[]{:S(2)}) %collective-permute-start.12) | collective-permute-done | bytes 589856 | tf_op jit(solution)/shard_map/ppermute | solution.py:34
  99.9 2.5 %subtract_convert_fusion = (bf16[576,512]{1,0:T(8,128)(2,1)S(1)}, f32[576,512]{1,0:T(8,128)}, f32[576,512]{1,0:T(8,128)}) fusion(bf16[576,512]{1,0:T(8,128)(2,1)S(1)} %copy-done.3, bf16[576,512]{1,0:T(8,128)(2,1)S(1)} %collective-permute-done.12, bf16[576,512]{1,0:T(8,128)(2,1)S(1)} %collective-permute-done.11, bf16[576,512]{1,0:T(8,128)(2,1)S(1)} %gradient_part.4, ...), kind=kLoop, calls=%fused_computation.10 | loop fusion | flops 6193152 | bytes 7667712 | tf_op jit(solution)/shard_map/convert_element_type | solution.py:29
  104.7 1.7 collective-permute-start.15
  107.1 1.5 collective-permute-start.18
  108.6 24.0 %collective-permute-done.16.block = bf16[576,512]{1,0:T(8,128)(2,1)S(1)} collective-permute-done((bf16[576,512]{1,0:T(8,128)(2,1)S(1)}, bf16[576,512]{1,0:T(8,128)(2,1)S(1)}, u32[]{:S(2)}, u32[]{:S(2)}) %collective-permute-start.16) | collective-permute-done | bytes 589856 | tf_op jit(solution)/shard_map/ppermute | solution.py:34
  139.4 10.0 %collective-permute-done.20.block = bf16[576,512]{1,0:T(8,128)(2,1)S(1)} collective-permute-done((bf16[576,512]{1,0:T(8,128)(2,1)S(1)}, bf16[576,512]{1,0:T(8,128)(2,1)S(1)}, u32[]{:S(2)}, u32[]{:S(2)}) %collective-permute-start.20) | collective-permute-done | bytes 589856 | tf_op jit(solution)/shard_map/ppermute | solution.py:34
  149.4 1.9 %collective-permute-done.24 = bf16[2,576,128]{2,1,0:T(8,128)(2,1)S(1)} collective-permute-done((bf16[2,576,128]{2,1,0:T(8,128)(2,1)S(1)}, bf16[2,576,128]{2,1,0:T(8,128)(2,1)S(1)}, u32[]{:S(2)}, u32[]{:S(2)}) %collective-permute-start.24) | collective-permute-done | bytes 294944 | tf_op jit(solution)/shard_map/ppermute | solution.py:34
  153.0 1.5 collective-permute-start.28
  156.0 7.6 %collective-permute-done.27 = bf16[2,576,128]{2,1,0:T(8,128)(2,1)S(1)} collective-permute-done((bf16[2,576,128]{2,1,0:T(8,128)(2,1)S(1)}, bf16[2,576,128]{2,1,0:T(8,128)(2,1)S(1)}, u32[]{:S(2)}, u32[]{:S(2)}) %collective-permute-start.27) | collective-permute-done | bytes 294944 | tf_op jit(solution)/shard_map/ppermute | solution.py:34
  165.3 3.7 %collective-permute-done.30 = bf16[576,128]{1,0:T(8,128)(2,1)S(1)} collective-permute-done((bf16[576,128]{1,0:T(8,128)(2,1)S(1)}, bf16[576,128]{1,0:T(8,128)(2,1)S(1)}, u32[]{:S(2)}, u32[]{:S(2)}) %collective-permute-start.30) | collective-permute-done | bytes 147488 | tf_op jit(solution)/shard_map/ppermute | solution.py:34
  (96 shorter events, 24.8 us)
Async XLA Ops:
  4.9 16.5 %collective-permute-start.2 = (bf16[4,576,128]{2,1,0:T(8,128)(2,1)}, bf16[4,576,128]{2,1,0:T(8,128)(2,1)S(1)}, u32[]{:S(2)}, u32[]{:S(2)}) collective-permute-start(bf16[4,576,128]{2,1,0:T(8,128)(2,1)} %get-tuple-element.59), channel_id=1, source_target_pairs={{0,4},{4,0},{8,12},{12,8},{16,20},{20,16},{24,28},{28,24},{1,5},{5... | collective-permute-start | bytes 1769480 | tf_op jit(solution)/shard_map/ppermute | solution.py:34
  7.9 13.5 %collective-permute-start.4 = (bf16[4,576,128]{2,1,0:T(8,128)(2,1)S(1)}, bf16[4,576,128]{2,1,0:T(8,128)(2,1)S(1)}, u32[]{:S(2)}, u32[]{:S(2)}) collective-permute-start(bf16[4,576,128]{2,1,0:T(8,128)(2,1)S(1)} %get-tuple-element.58.refs_0_), channel_id=1, source_target_pairs={{0,1},{1,0},{2,3},{3,2},{4,5},{5,4},{6,7},{7,6},{8,9},{9,8},{10,11... | collective-permute-start | bytes 1769480 | tf_op jit(solution)/shard_map/ppermute | solution.py:34
  7.9 15.7 %collective-permute-start.3 = (bf16[4,576,128]{2,1,0:T(8,128)(2,1)S(1)}, bf16[4,576,128]{2,1,0:T(8,128)(2,1)S(1)}, u32[]{:S(2)}, u32[]{:S(2)}) collective-permute-start(bf16[4,576,128]{2,1,0:T(8,128)(2,1)S(1)} %get-tuple-element.58.refs_0_), channel_id=1, source_target_pairs={{0,2},{1,3},{2,0},{3,1},{4,6},{5,7},{6,4},{7,5},{8,10},{9,11},{10,... | collective-permute-start | bytes 1769480 | tf_op jit(solution)/shard_map/ppermute | solution.py:34
  9.4 28.0 %collective-permute-start = (bf16[576,512]{1,0:T(8,128)(2,1)S(1)}, bf16[576,512]{1,0:T(8,128)(2,1)S(1)}, u32[]{:S(2)}, u32[]{:S(2)}) collective-permute-start(bf16[576,512]{1,0:T(8,128)(2,1)S(1)} %copy-done.3), channel_id=1, source_target_pairs={{0,8},{4,12},{8,0},{12,4},{16,24},{20,28},{24,16},{28,20},{1,9},{5... | collective-permute-start | bytes 1769480 | tf_op jit(solution)/shard_map/ppermute | solution.py:34
  10.9 28.9 %collective-permute-start.1 = (bf16[576,512]{1,0:T(8,128)(2,1)S(1)}, bf16[576,512]{1,0:T(8,128)(2,1)}, u32[]{:S(2)}, u32[]{:S(2)}) collective-permute-start(bf16[576,512]{1,0:T(8,128)(2,1)S(1)} %copy-done.3), channel_id=1, source_target_pairs={{0,16},{4,20},{8,24},{12,28},{16,0},{20,4},{24,8},{28,12},{1,17},{... | collective-permute-start | bytes 1769480 | tf_op jit(solution)/shard_map/ppermute | solution.py:34
  23.6 16.2 %collective-permute-start.6 = (bf16[4,576,128]{2,1,0:T(8,128)(2,1)S(1)}, bf16[4,576,128]{2,1,0:T(8,128)(2,1)S(1)}, u32[]{:S(2)}, u32[]{:S(2)}) collective-permute-start(bf16[4,576,128]{2,1,0:T(8,128)(2,1)S(1)} %collective-permute-done.2.refs_4_), channel_id=1, source_target_pairs={{0,1},{1,0},{2,3},{3,2},{4,5},{5,4},{6,7},{7,6},{8,9},{9,8},{10,11... | collective-permute-start | bytes 1769480 | tf_op jit(solution)/shard_map/ppermute | solution.py:34
  23.6 16.2 %collective-permute-start.5 = (bf16[512,512]{1,0:T(8,128)(2,1)S(1)}, bf16[512,512]{1,0:T(8,128)(2,1)S(1)}, u32[]{:S(2)}, u32[]{:S(2)}) collective-permute-start(bf16[512,512]{1,0:T(8,128)(2,1)S(1)} %bitcast.65), channel_id=1, source_target_pairs={{0,4},{4,0},{8,12},{12,8},{16,20},{20,16},{24,28},{28,24},{1,5},{5... | collective-permute-start | bytes 1572872 | tf_op jit(solution)/shard_map/ppermute | solution.py:34
  23.9 16.0 %collective-permute-start.7 = (bf16[4,576,128]{2,1,0:T(8,128)(2,1)S(1)}, bf16[4,576,128]{2,1,0:T(8,128)(2,1)S(1)}, u32[]{:S(2)}, u32[]{:S(2)}) collective-permute-start(bf16[4,576,128]{2,1,0:T(8,128)(2,1)S(1)} %collective-permute-done.2.refs_4_), channel_id=1, source_target_pairs={{0,2},{1,3},{2,0},{3,1},{4,6},{5,7},{6,4},{7,5},{8,10},{9,11},{10,... | collective-permute-start | bytes 1769480 | tf_op jit(solution)/shard_map/ppermute | solution.py:34
  39.8 2.0 %collective-permute-start.8 = (bf16[4,576,128]{2,1,0:T(8,128)(2,1)S(1)}, bf16[4,576,128]{2,1,0:T(8,128)(2,1)S(1)}, u32[]{:S(2)}, u32[]{:S(2)}) collective-permute-start(bf16[4,576,128]{2,1,0:T(8,128)(2,1)S(1)} %collective-permute-done.3.refs_1_), channel_id=1, source_target_pairs={{0,1},{1,0},{2,3},{3,2},{4,5},{5,4},{6,7},{7,6},{8,9},{9,8},{10,11... | collective-permute-start | bytes 1769480 | tf_op jit(solution)/shard_map/ppermute | solution.py:34
  41.8 2.0 %collective-permute-start.9 = (bf16[4,576,128]{2,1,0:T(8,128)(2,1)S(1)}, bf16[4,576,128]{2,1,0:T(8,128)(2,1)S(1)}, u32[]{:S(2)}, u32[]{:S(2)}) collective-permute-start(bf16[4,576,128]{2,1,0:T(8,128)(2,1)S(1)} %collective-permute-done.7.refs_5_), channel_id=1, source_target_pairs={{0,1},{1,0},{2,3},{3,2},{4,5},{5,4},{6,7},{7,6},{8,9},{9,8},{10,11... | collective-permute-start | bytes 1769480 | tf_op jit(solution)/shard_map/ppermute | solution.py:34
  46.5 16.2 %collective-permute-start.10 = (bf16[576,512]{1,0:T(8,128)(2,1)S(1)}, bf16[576,512]{1,0:T(8,128)(2,1)S(1)}, u32[]{:S(2)}, u32[]{:S(2)}) collective-permute-start(bf16[576,512]{1,0:T(8,128)(2,1)S(1)} %gradient_part.6), channel_id=1, source_target_pairs={{0,8},{4,12},{8,0},{12,4},{16,24},{20,28},{24,16},{28,20},{1,9},{5... | collective-permute-start | bytes 1769480 | tf_op jit(solution)/shard_map/ppermute | solution.py:34
  47.0 38.8 %collective-permute-start.14 = (bf16[576,512]{1,0:T(8,128)(2,1)}, bf16[576,512]{1,0:T(8,128)(2,1)S(1)}, u32[]{:S(2)}, u32[]{:S(2)}) collective-permute-start(bf16[576,512]{1,0:T(8,128)(2,1)} %collective-permute-done.1), channel_id=1, source_target_pairs={{0,8},{4,12},{8,0},{12,4},{16,24},{20,28},{24,16},{28,20},{1,9},{5... | collective-permute-start | bytes 1769480 | tf_op jit(solution)/shard_map/ppermute | solution.py:34
  62.9 32.8 %collective-permute-start.11 = (bf16[576,512]{1,0:T(8,128)(2,1)S(1)}, bf16[576,512]{1,0:T(8,128)(2,1)S(1)}, u32[]{:S(2)}, u32[]{:S(2)}) collective-permute-start(bf16[576,512]{1,0:T(8,128)(2,1)S(1)} %add_convert_fusion.4), channel_id=1, source_target_pairs={{0,16},{4,20},{8,24},{12,28},{16,0},{20,4},{24,8},{28,12},{1,17},{... | collective-permute-start | bytes 1769480 | tf_op jit(solution)/shard_map/ppermute | solution.py:34
  64.0 35.9 %collective-permute-start.12 = (bf16[576,512]{1,0:T(8,128)(2,1)S(1)}, bf16[576,512]{1,0:T(8,128)(2,1)S(1)}, u32[]{:S(2)}, u32[]{:S(2)}) collective-permute-start(bf16[576,512]{1,0:T(8,128)(2,1)S(1)} %gradient_part.7), channel_id=1, source_target_pairs={{0,8},{4,12},{8,0},{12,4},{16,24},{20,28},{24,16},{28,20},{1,9},{5... | collective-permute-start | bytes 1769480 | tf_op jit(solution)/shard_map/ppermute | solution.py:34
  66.1 29.6 %collective-permute-start.13 = (bf16[512,512]{1,0:T(8,128)(2,1)S(1)}, bf16[512,512]{1,0:T(8,128)(2,1)S(1)}, u32[]{:S(2)}, u32[]{:S(2)}) collective-permute-start(bf16[512,512]{1,0:T(8,128)(2,1)S(1)} %bitcast.70), channel_id=1, source_target_pairs={{0,4},{4,0},{8,12},{12,8},{16,20},{20,16},{24,28},{28,24},{1,5},{5... | collective-permute-start | bytes 1572872 | tf_op jit(solution)/shard_map/ppermute | solution.py:34
  88.6 11.2 %copy-start.5 = (f32[576,512]{1,0:T(8,128)S(1)}, f32[576,512]{1,0:T(8,128)}, u32[]{:S(2)}) copy-start(f32[576,512]{1,0:T(8,128)} %param.14) | copy-start | bytes 3538948
  103.2 3.7 %collective-permute-start.17 = (bf16[2,2,576,128]{3,2,1,0:T(8,128)(2,1)S(1)}, bf16[2,2,576,128]{3,2,1,0:T(8,128)(2,1)S(1)}, u32[]{:S(2)}, u32[]{:S(2)}) collective-permute-start(bf16[2,2,576,128]{3,2,1,0:T(8,128)(2,1)S(1)} %get-tuple-element.83), channel_id=1, source_target_pairs={{0,1},{1,0},{2,3},{3,2},{4,5},{5,4},{6,7},{7,6},{8,9},{9,8},{10,11... | collective-permute-start | bytes 1769480 | tf_op jit(solution)/shard_map/ppermute | solution.py:34
  103.3 29.3 %collective-permute-start.16 = (bf16[576,512]{1,0:T(8,128)(2,1)S(1)}, bf16[576,512]{1,0:T(8,128)(2,1)S(1)}, u32[]{:S(2)}, u32[]{:S(2)}) collective-permute-start(bf16[576,512]{1,0:T(8,128)(2,1)S(1)} %get-tuple-element.110.block), channel_id=1, source_target_pairs={{0,16},{4,20},{8,24},{12,28},{16,0},{20,4},{24,8},{28,12},{1,17},{... | collective-permute-start | bytes 1769480 | tf_op jit(solution)/shard_map/ppermute | solution.py:34
  104.7 28.0 %collective-permute-start.15 = (bf16[576,512]{1,0:T(8,128)(2,1)S(1)}, bf16[576,512]{1,0:T(8,128)(2,1)S(1)}, u32[]{:S(2)}, u32[]{:S(2)}) collective-permute-start(bf16[576,512]{1,0:T(8,128)(2,1)S(1)} %get-tuple-element.110.block), channel_id=1, source_target_pairs={{0,8},{4,12},{8,0},{12,4},{16,24},{20,28},{24,16},{28,20},{1,9},{5... | collective-permute-start | bytes 1769480 | tf_op jit(solution)/shard_map/ppermute | solution.py:34
  106.4 26.3 %collective-permute-start.19 = (bf16[512,512]{1,0:T(8,128)(2,1)S(1)}, bf16[512,512]{1,0:T(8,128)(2,1)S(1)}, u32[]{:S(2)}, u32[]{:S(2)}) collective-permute-start(bf16[512,512]{1,0:T(8,128)(2,1)S(1)} %get-tuple-element.87), channel_id=1, source_target_pairs={{0,4},{4,0},{8,12},{12,8},{16,20},{20,16},{24,28},{28,24},{1,5},{5... | collective-permute-start | bytes 1572872 | tf_op jit(solution)/shard_map/ppermute | solution.py:34
  107.1 25.6 %collective-permute-start.18 = (bf16[2,576,128]{2,1,0:T(8,128)(2,1)S(1)}, bf16[2,576,128]{2,1,0:T(8,128)(2,1)S(1)}, u32[]{:S(2)}, u32[]{:S(2)}) collective-permute-start(bf16[2,576,128]{2,1,0:T(8,128)(2,1)S(1)} %get-tuple-element.123), channel_id=1, source_target_pairs={{0,2},{1,3},{2,0},{3,1},{4,6},{5,7},{6,4},{7,5},{8,10},{9,11},{10,... | collective-permute-start | bytes 884744 | tf_op jit(solution)/shard_map/ppermute | solution.py:34
  133.6 2.1 %collective-permute-start.21 = (bf16[2,2,576,128]{3,2,1,0:T(8,128)(2,1)S(1)}, bf16[2,2,576,128]{3,2,1,0:T(8,128)(2,1)S(1)}, u32[]{:S(2)}, u32[]{:S(2)}) collective-permute-start(bf16[2,2,576,128]{3,2,1,0:T(8,128)(2,1)S(1)} %get-tuple-element.91), channel_id=1, source_target_pairs={{0,1},{1,0},{2,3},{3,2},{4,5},{5,4},{6,7},{7,6},{8,9},{9,8},{10,11... | collective-permute-start | bytes 1769480 | tf_op jit(solution)/shard_map/ppermute | solution.py:34
  133.6 15.7 %collective-permute-start.20 = (bf16[576,512]{1,0:T(8,128)(2,1)S(1)}, bf16[576,512]{1,0:T(8,128)(2,1)S(1)}, u32[]{:S(2)}, u32[]{:S(2)}) collective-permute-start(bf16[576,512]{1,0:T(8,128)(2,1)S(1)} %collective-permute-done.16.block), channel_id=1, source_target_pairs={{0,8},{4,12},{8,0},{12,4},{16,24},{20,28},{24,16},{28,20},{1,9},{5... | collective-permute-start | bytes 1769480 | tf_op jit(solution)/shard_map/ppermute | solution.py:34
  134.8 2.1 %collective-permute-start.22 = (bf16[2,2,576,128]{3,2,1,0:T(8,128)(2,1)S(1)}, bf16[2,2,576,128]{3,2,1,0:T(8,128)(2,1)S(1)}, u32[]{:S(2)}, u32[]{:S(2)}) collective-permute-start(bf16[2,2,576,128]{3,2,1,0:T(8,128)(2,1)S(1)} %get-tuple-element.93), channel_id=1, source_target_pairs={{0,1},{1,0},{2,3},{3,2},{4,5},{5,4},{6,7},{7,6},{8,9},{9,8},{10,11... | collective-permute-start | bytes 1769480 | tf_op jit(solution)/shard_map/ppermute | solution.py:34
  135.8 13.6 %collective-permute-start.23 = (bf16[2,576,128]{2,1,0:T(8,128)(2,1)S(1)}, bf16[2,576,128]{2,1,0:T(8,128)(2,1)S(1)}, u32[]{:S(2)}, u32[]{:S(2)}) collective-permute-start(bf16[2,576,128]{2,1,0:T(8,128)(2,1)S(1)} %get-tuple-element.121), channel_id=1, source_target_pairs={{0,2},{1,3},{2,0},{3,1},{4,6},{5,7},{6,4},{7,5},{8,10},{9,11},{10,... | collective-permute-start | bytes 884744 | tf_op jit(solution)/shard_map/ppermute | solution.py:34
  137.1 14.1 %collective-permute-start.24 = (bf16[2,576,128]{2,1,0:T(8,128)(2,1)S(1)}, bf16[2,576,128]{2,1,0:T(8,128)(2,1)S(1)}, u32[]{:S(2)}, u32[]{:S(2)}) collective-permute-start(bf16[2,576,128]{2,1,0:T(8,128)(2,1)S(1)} %get-tuple-element.119), channel_id=1, source_target_pairs={{0,2},{1,3},{2,0},{3,1},{4,6},{5,7},{6,4},{7,5},{8,10},{9,11},{10,... | collective-permute-start | bytes 884744 | tf_op jit(solution)/shard_map/ppermute | solution.py:34
  138.2 11.2 %collective-permute-start.25 = (bf16[576,128]{1,0:T(8,128)(2,1)S(1)}, bf16[576,128]{1,0:T(8,128)(2,1)S(1)}, u32[]{:S(2)}, u32[]{:S(2)}) collective-permute-start(bf16[576,128]{1,0:T(8,128)(2,1)S(1)} %get-tuple-element.131), channel_id=1, source_target_pairs={{0,4},{4,0},{8,12},{12,8},{16,20},{20,16},{24,28},{28,24},{1,5},{5... | collective-permute-start | bytes 442376 | tf_op jit(solution)/shard_map/ppermute | solution.py:34
  152.1 2.5 %collective-permute-start.26 = (bf16[2,2,576,128]{3,2,1,0:T(8,128)(2,1)S(1)}, bf16[2,2,576,128]{3,2,1,0:T(8,128)(2,1)S(1)}, u32[]{:S(2)}, u32[]{:S(2)}) collective-permute-start(bf16[2,2,576,128]{3,2,1,0:T(8,128)(2,1)S(1)} %get-tuple-element.108), channel_id=1, source_target_pairs={{0,1},{1,0},{2,3},{3,2},{4,5},{5,4},{6,7},{7,6},{8,9},{9,8},{10,11... | collective-permute-start | bytes 1769480 | tf_op jit(solution)/shard_map/ppermute | solution.py:34
  152.3 13.0 %collective-permute-start.29 = (bf16[576,128]{1,0:T(8,128)(2,1)S(1)}, bf16[576,128]{1,0:T(8,128)(2,1)S(1)}, u32[]{:S(2)}, u32[]{:S(2)}) collective-permute-start(bf16[576,128]{1,0:T(8,128)(2,1)S(1)} %get-tuple-element.128), channel_id=1, source_target_pairs={{0,4},{4,0},{8,12},{12,8},{16,20},{20,16},{24,28},{28,24},{1,5},{5... | collective-permute-start | bytes 442376 | tf_op jit(solution)/shard_map/ppermute | solution.py:34
  153.0 12.3 %collective-permute-start.28 = (bf16[576,128]{1,0:T(8,128)(2,1)S(1)}, bf16[576,128]{1,0:T(8,128)(2,1)S(1)}, u32[]{:S(2)}, u32[]{:S(2)}) collective-permute-start(bf16[576,128]{1,0:T(8,128)(2,1)S(1)} %get-tuple-element.126), channel_id=1, source_target_pairs={{0,4},{4,0},{8,12},{12,8},{16,20},{20,16},{24,28},{28,24},{1,5},{5... | collective-permute-start | bytes 442376 | tf_op jit(solution)/shard_map/ppermute | solution.py:34
  154.7 8.9 %collective-permute-start.27 = (bf16[2,576,128]{2,1,0:T(8,128)(2,1)S(1)}, bf16[2,576,128]{2,1,0:T(8,128)(2,1)S(1)}, u32[]{:S(2)}, u32[]{:S(2)}) collective-permute-start(bf16[2,576,128]{2,1,0:T(8,128)(2,1)S(1)} %slice_bitcast_fusion), channel_id=1, source_target_pairs={{0,2},{1,3},{2,0},{3,1},{4,6},{5,7},{6,4},{7,5},{8,10},{9,11},{10,... | collective-permute-start | bytes 884744 | tf_op jit(solution)/shard_map/ppermute | solution.py:34
  163.8 5.2 %collective-permute-start.30 = (bf16[576,128]{1,0:T(8,128)(2,1)S(1)}, bf16[576,128]{1,0:T(8,128)(2,1)S(1)}, u32[]{:S(2)}, u32[]{:S(2)}) collective-permute-start(bf16[576,128]{1,0:T(8,128)(2,1)S(1)} %get-tuple-element.130), channel_id=1, source_target_pairs={{0,4},{4,0},{8,12},{12,8},{16,20},{20,16},{24,28},{28,24},{1,5},{5... | collective-permute-start | bytes 442376 | tf_op jit(solution)/shard_map/ppermute | solution.py:34
  (7 other events, 27.3 us)

commit v4 on v3

--- a/solution.py
+++ b/solution.py
@@ -54,20 +54,82 @@
     return lax.optimization_barrier(values)
 
 
-def relative(rows, x, c):
-    block = rows.shape[0] // 4
-    rows = rows.reshape(2, 2, block, rows.shape[1])
-    rows = jnp.where(x == 1, rows[::-1], rows)
-    rows = jnp.where(c == 1, rows[:, ::-1], rows)
-    return rows.transpose(1, 0, 2, 3).reshape(4 * block, -1)
-
-
-def absolute(rows, x, c):
-    block = rows.shape[0] // 4
-    rows = rows.reshape(2, 2, block, -1).transpose(1, 0, 2, 3)
-    rows = jnp.where(c == 1, rows[:, ::-1], rows)
-    rows = jnp.where(x == 1, rows[::-1], rows)
-    return rows.reshape(4 * block, -1)
+def copy_kernel(index, rows, out):
+    del index
+    out[...] = rows[...]
+
+
+def reorder(rows, index):
+    block, wide = rows.shape[0] // 4, rows.shape[1]
+    return pl.pallas_call(
+        copy_kernel,
+        grid_spec=pltpu.PrefetchScalarGridSpec(
+            num_scalar_prefetch=1,
+            grid=(4,),
+            in_specs=[pl.BlockSpec((block, wide), lambda i, index: (index[i], 0))],
+            out_specs=pl.BlockSpec((block, wide), lambda i, index: (i, 0)),
+        ),
+        out_shape=jax.ShapeDtypeStruct(rows.shape, rows.dtype),
+        compiler_params=params(),
+        cost_estimate=light(),
+        name="reorder",
+    )(index, rows)
+
+
+def split_kernel(starts, cotangent, mine, other, turned):
+    n, own, _ = mine.shape
+    turned[...] = cotangent[...].T
+    for j in range(n):
+        mine[j] = turned[pl.ds(pl.multiple_of(starts[j], 16), own)]
+        other[j] = turned[pl.ds(pl.multiple_of(starts[n + j], 16), own)]
+
+
+def split_features(cotangent, own, planes, y):
+    tok, features = cotangent.shape
+    n = features // (2 * own)
+    if own % 16:
+        blocks = jnp.take(cotangent.T.reshape(n, 2, own, tok), planes, axis=0)
+        mine = jnp.where(y == 0, blocks[:, 0], blocks[:, 1])
+        return mine, jnp.where(y == 0, blocks[:, 1], blocks[:, 0])
+    starts = jnp.concatenate([(2 * planes + y) * own, (2 * planes + 1 - y) * own]).astype(jnp.int32)
+    shape = jax.ShapeDtypeStruct((n, own, tok), bf16)
+    return pl.pallas_call(
+        split_kernel,
+        in_specs=[pl.BlockSpec(memory_space=pltpu.SMEM), pl.BlockSpec(memory_space=pltpu.VMEM)],
+        out_shape=[shape, shape],
+        scratch_shapes=[pltpu.VMEM((features, tok), bf16)],
+        compiler_params=params(),
+        cost_estimate=light(),
+        name="split_features",
+    )(starts, cotangent)
+
+
+def join_kernel(starts, *refs):
+    blocks, out, turned = refs[:-2], refs[-2], refs[-1]
+    own = blocks[0].shape[0]
+    for j, block in enumerate(blocks):
+        turned[pl.ds(pl.multiple_of(starts[j], 16), own)] = block[...]
+    out[...] = turned[...].T
+
+
+def join_features(mine, other, planes, y):
+    n, (own, tok) = len(mine), mine[0].shape
+    if own % 16:
+        mine, other = jnp.stack(mine), jnp.stack(other)
+        both = jnp.stack([jnp.where(y == 0, mine, other), jnp.where(y == 0, other, mine)], axis=1)
+        place = jnp.zeros(n, jnp.int32).at[planes].set(jnp.arange(n, dtype=jnp.int32))
+        return jnp.take(both, place, axis=0).reshape(2 * n * own, tok).T
+    starts = jnp.concatenate([(2 * planes + y) * own, (2 * planes + 1 - y) * own]).astype(jnp.int32)
+    vmem = pl.BlockSpec(memory_space=pltpu.VMEM)
+    return pl.pallas_call(
+        join_kernel,
+        in_specs=[pl.BlockSpec(memory_space=pltpu.SMEM)] + [vmem] * (2 * n),
+        out_shape=jax.ShapeDtypeStruct((tok, 2 * n * own), bf16),
+        scratch_shapes=[pltpu.VMEM((2 * n * own, tok), bf16)],
+        compiler_params=params(),
+        cost_estimate=light(),
+        name="join_features",
+    )(starts, *mine, *other)
 
 
 def params():
@@ -76,6 +138,10 @@
 
 def cost(flops, bytes_accessed):
     return pl.CostEstimate(flops=flops, bytes_accessed=bytes_accessed, transcendentals=0)
+
+
+def light():
+    return cost(10**6, 10**5)
 
 
 def gradient_kernel(scale, *refs):
@@ -100,7 +166,7 @@
         out_specs=pl.BlockSpec((part, wide), lambda i: (i, 0)),
         out_shape=jax.ShapeDtypeStruct((own, wide), bf16),
         compiler_params=params(),
-        cost_estimate=cost(4 * own * rows * wide, 2 * own * (2 * rows + wide) + 4 * rows * wide),
+        cost_estimate=light(),
         name="gradient_part",
     )(*pieces, saved0, saved1)
 
@@ -140,7 +206,7 @@
         out_shape=[jax.ShapeDtypeStruct((rows, wide), f32), jax.ShapeDtypeStruct((rows, wide), bf16)],
         scratch_shapes=[pltpu.VMEM((2 * rows, wide), f32)],
         compiler_params=params(),
-        cost_estimate=cost(4 * n * own * rows * wide, 2 * n * own * (2 * rows + wide) + 6 * rows * wide),
+        cost_estimate=light(),
         name="attn_part",
     )(*pieces, weights)
 
@@ -184,19 +250,19 @@
     top = n // 2
     levels = [[r for r in range(n) if r.bit_count() == k] for k in range(n.bit_length())]
 
+    inward = jnp.stack([2 * (x ^ chip) + (c ^ core) for core in range(2) for chip in range(2)]).astype(jnp.int32)
+    back = jnp.stack([2 * (c ^ core) + (x ^ chip) for chip in range(2) for core in range(2)]).astype(jnp.int32)
+
     weights = {0: weight}
     for r in reversed(levels[1]):
         weights[r] = to_plane(weight, r)
 
-    blocks = cotangent.T.reshape(n, 2, own, tok)
-    blocks = jnp.take(blocks, z ^ jnp.array(order), axis=0)
-    mine = jnp.where(y == 0, blocks[:, 0], blocks[:, 1])
-    other = jnp.where(y == 0, blocks[:, 1], blocks[:, 0])
+    mine, other = split_features(cotangent, own, z ^ jnp.array(order, jnp.int32), y)
     mine, other = stage(mine, other)
     partner = to_partner(other)
     mine_x = to_chip(mine)
     mine_c = to_core(mine)
-    saved0 = relative(attn_saved, x, c)
+    saved0 = reorder(attn_saved, inward)
     partner, mine_x, mine_c, saved0 = stage(partner, mine_x, mine_c, saved0)
 
     saved1 = to_partner(saved0)
@@ -215,20 +281,22 @@
     sums = {}
     for j, r in enumerate(order):
         sums[r] = gradient_part(pieces, saved0, saved1, j, scale)
-    next0 = relative(attn_next, x, c)
+    next0 = reorder(attn_next, inward)
     next1 = to_partner(next0)
     m = 1
     while m < top:
         sends = [r for r in sums if r & m and r != m]
         came = [to_plane(sums.pop(r), m) for r in sends]
-        came, sums[m] = stage(came, sums[m])
+        last = [r for r in order if r.bit_count() > 1]
+        old, came, sums[m] = stage([weights[r] for r in last], came, sums[m])
+        weights.update(zip(last, old))
         for r, value in zip(sends, came):
             sums[r ^ m] = add(sums[r ^ m], value)
         m *= 2
     ends = [1 << k for k in reversed(range(n.bit_length() - 1))]
     gathered, _ = stage([weights[r] for r in order], came)
     gathered = jnp.stack(gathered)
-    came = [to_plane(sums[m], m) for m in ends]
+    came = [to_plane(value, m) for m, value in zip(ends, stage(*[sums[m] for m in ends]))]
     kept, sent = attn_part(pieces, gathered)
     came, next1, attn = stage(came, next1, [kept, sent])
     gradient = sums[0].astype(f32) + functools.reduce(jnp.add, [v.astype(f32) for v in came])
@@ -254,11 +322,9 @@
             total = add(kept[r], came[r])
             results[r] = (total[0], to_partner(total[1]))
 
-    grad_attn = absolute((attn[0] + attn[1].astype(f32)).astype(bf16), x, c)
-    mine = jnp.stack([results[r][0] for r in range(n)])
-    other = jnp.stack([results[r][1] for r in range(n)])
-    both = jnp.stack([jnp.where(y == 0, mine, other), jnp.where(y == 0, other, mine)], axis=1)
-    next_out = jnp.take(both, z ^ jnp.arange(n), axis=0).reshape(2 * n * own, tok).T
+    grad_attn = reorder((attn[0] + attn[1].astype(f32)).astype(bf16), back)
+    mine, other = [[results[r][k] for r in range(n)] for k in range(2)]
+    next_out = join_features(mine, other, z ^ jnp.arange(n, dtype=jnp.int32), y)
     return (grad_attn, new_weight, new_moment1, new_moment2, next_out)
 
 

time: 172 us -> 172 us (level)
  Pallas kernels: 17.8 us -> 24 us
  local copies, waits for them, and re-layouts: 8.07 us -> 4.61 us
  starting transfers between devices: 28.9 us -> 26.6 us
  waiting for transfers between devices: 107 us -> 105 us
    pallas_call x0 -> x5, Pallas kernels: none -> 6.21 us  [the longest x3 3.25 us: reorder(): pl.pallas_call(copy_kernel, grid_spec=pltpu.PrefetchScalarGridSpec(num_sc...]
    reshape x3 -> x0, local copies, waits for them, and re-layouts: 2.58 us -> none  [the longest x1 1.41 us: local(): jnp.take(both, z ^ jnp.arange(n), axis=0).reshape(2 * n * own, tok)]
    ppermute x31, starting transfers between devices: 28.9 us -> 26.6 us  [flip(): lax.ppermute(value, axis, [(i, i ^ bit) for i in range(lax.axis_size(axis...]
    select_n x10 -> x0, other arithmetic: 2 us -> none  [the longest x1 0.9 us: local(): other = jnp.where(y == 0, blocks[:, 1], blocks[:, 0])]
  transfers between devices with their start and end apart: 31 -> 31, of which waited for: 17 -> 18; matrix products, arithmetic and copies ran while one was open for 4% -> 4% of each run, Pallas kernels for 8% -> 11%
where the time goes in v4:
time: 172 us
  waiting for transfers between devices  105 us (61%)
  starting transfers between devices  26.6 us (15%)
  Pallas kernels  24 us (14%)
  other arithmetic  10.1 us (6%)
  local copies, waits for them, and re-layouts  4.61 us (3%)
    ppermute x31, waiting for transfers between devices, flip(): lax.ppermute(value, axis, [(i, i ^ bit) for i in range(lax.axis_size(axis...  105 us
    ppermute x31, starting transfers between devices, flip(): lax.ppermute(value, axis, [(i, i ^ bit) for i in range(lax.axis_size(axis...  26.6 us
    pallas_call x4, Pallas kernels, gradient_part(): pl.pallas_call(functools.partial(gradient_kernel, scale), grid=(steps,),...  7.46 us
    pallas_call x1, Pallas kernels, attn_part(): pl.pallas_call(attn_kernel, grid=(n,), in_specs=[pl.BlockSpec((1, own, to...  7.11 us
    convert_element_type x1, other arithmetic, adamw_step(): new_weight = (weight.astype(f32) * (1.0 - learning_rate * weight_decay) -...  3.61 us
  transfers between devices with their start and end apart: 31, of which 18 were waited for; matrix products, arithmetic and copies ran while one was open for 4% of the time, Pallas kernels for 11%

profile of v4, /device:TPU:0, one launch (start us, length us, event | category | flops | bytes accessed | tf_op | source)
XLA Modules:
  0.0 171.6 jit_solution(17986321304678556587)
XLA Ops:
  3.6 3.0 %collective-permute-start.2 = (bf16[4,576,128]{2,1,0:T(8,128)(2,1)S(1)}, bf16[4,576,128]{2,1,0:T(8,128)(2,1)S(1)}, u32[]{:S(2)}, u32[]{:S(2)}) collective-permute-start(bf16[4,576,128]{2,1,0:T(8,128)(2,1)S(1)} %get-tuple-element.61), channel_id=1, source_target_pairs={{0,4},{4,0},{8,12},{12,8},{16,20},{20,16},{24,28},{28,24},{1,5},{5... | collective-permute-start | bytes 1769480 | tf_op jit(solution)/shard_map/ppermute | solution.py:34
  6.7 1.5 collective-permute-start.3
  8.2 1.6 collective-permute-start
  9.8 2.6 %collective-permute-start.1 = (bf16[576,512]{1,0:T(8,128)(2,1)}, bf16[576,512]{1,0:T(8,128)(2,1)}, u32[]{:S(2)}, u32[]{:S(2)}) collective-permute-start(bf16[576,512]{1,0:T(8,128)(2,1)} %param.10), channel_id=1, source_target_pairs={{0,16},{4,20},{8,24},{12,28},{16,0},{20,4},{24,8},{28,12},{1,17},{... | collective-permute-start | bytes 1769480 | tf_op jit(solution)/shard_map/ppermute | solution.py:34
  13.1 6.9 %collective-permute-done.2.refs_4_ = bf16[4,576,128]{2,1,0:T(8,128)(2,1)S(1)} collective-permute-done((bf16[4,576,128]{2,1,0:T(8,128)(2,1)S(1)}, bf16[4,576,128]{2,1,0:T(8,128)(2,1)S(1)}, u32[]{:S(2)}, u32[]{:S(2)}) %collective-permute-start.2) | collective-permute-done | bytes 589856 | tf_op jit(solution)/shard_map/ppermute | solution.py:34
  20.0 2.4 %collective-permute-done.3.refs_1_ = bf16[4,576,128]{2,1,0:T(8,128)(2,1)S(1)} collective-permute-done((bf16[4,576,128]{2,1,0:T(8,128)(2,1)S(1)}, bf16[4,576,128]{2,1,0:T(8,128)(2,1)S(1)}, u32[]{:S(2)}, u32[]{:S(2)}) %collective-permute-start.3) | collective-permute-done | bytes 589856 | tf_op jit(solution)/shard_map/ppermute | solution.py:34
  22.7 1.7 %collective-permute-start.7 = (bf16[4,576,128]{2,1,0:T(8,128)(2,1)S(1)}, bf16[4,576,128]{2,1,0:T(8,128)(2,1)S(1)}, u32[]{:S(2)}, u32[]{:S(2)}) collective-permute-start(bf16[4,576,128]{2,1,0:T(8,128)(2,1)S(1)} %collective-permute-done.2.refs_4_), channel_id=1, source_target_pairs={{0,2},{1,3},{2,0},{3,1},{4,6},{5,7},{6,4},{7,5},{8,10},{9,11},{10,... | collective-permute-start | bytes 1769480 | tf_op jit(solution)/shard_map/ppermute | solution.py:34
  24.4 12.0 %collective-permute-done = bf16[576,512]{1,0:T(8,128)(2,1)} collective-permute-done((bf16[576,512]{1,0:T(8,128)(2,1)}, bf16[576,512]{1,0:T(8,128)(2,1)}, u32[]{:S(2)}, u32[]{:S(2)}) %collective-permute-start) | collective-permute-done | bytes 589856 | tf_op jit(solution)/shard_map/ppermute | solution.py:34
  36.5 2.4 %collective-permute-done.1 = bf16[576,512]{1,0:T(8,128)(2,1)} collective-permute-done((bf16[576,512]{1,0:T(8,128)(2,1)}, bf16[576,512]{1,0:T(8,128)(2,1)}, u32[]{:S(2)}, u32[]{:S(2)}) %collective-permute-start.1) | collective-permute-done | bytes 589856 | tf_op jit(solution)/shard_map/ppermute | solution.py:34
  38.9 2.0 %collective-permute-done.8.refs_3_ = bf16[4,576,128]{2,1,0:T(8,128)(2,1)S(1)} collective-permute-done((bf16[4,576,128]{2,1,0:T(8,128)(2,1)S(1)}, bf16[4,576,128]{2,1,0:T(8,128)(2,1)S(1)}, u32[]{:S(2)}, u32[]{:S(2)}) %collective-permute-start.8) | collective-permute-done | bytes 589856 | tf_op jit(solution)/shard_map/ppermute | solution.py:34
  41.4 1.4 collective-permute-done.9.refs_7_
  43.7 1.9 %gradient_part.6 = bf16[576,512]{1,0:T(8,128)(2,1)S(1)} custom-call(bf16[4,576,128]{2,1,0:T(8,128)(2,1)S(1)} %get-tuple-element.60.refs_0_, bf16[4,576,128]{2,1,0:T(8,128)(2,1)S(1)} %collective-permute-done.3.refs_1_, bf16[4,576,128]{2,1,0:T(8,128)(2,1)S(1)} %collective-permute-done.4.refs_2_, bf16[4,576,128]{2,1,0:T(8,128)(2,1)S(1)} %collective-permute-done.8.refs_3_, ...), custom_call_target="tpu_custom_call" | custom-call | flops 1000000 | bytes 100000 | tf_op jit(solution)/shard_map/gradient_part/pallas_call | solution.py:162
  46.0 1.9 %gradient_part.7 = bf16[576,512]{1,0:T(8,128)(2,1)S(1)} custom-call(bf16[4,576,128]{2,1,0:T(8,128)(2,1)S(1)} %get-tuple-element.60.refs_0_, bf16[4,576,128]{2,1,0:T(8,128)(2,1)S(1)} %collective-permute-done.3.refs_1_, bf16[4,576,128]{2,1,0:T(8,128)(2,1)S(1)} %collective-permute-done.4.refs_2_, bf16[4,576,128]{2,1,0:T(8,128)(2,1)S(1)} %collective-permute-done.8.refs_3_, ...), custom_call_target="tpu_custom_call" | custom-call | flops 1000000 | bytes 100000 | tf_op jit(solution)/shard_map/gradient_part/pallas_call | solution.py:162
  47.9 1.9 %gradient_part.5 = bf16[576,512]{1,0:T(8,128)(2,1)S(1)} custom-call(bf16[4,576,128]{2,1,0:T(8,128)(2,1)S(1)} %get-tuple-element.60.refs_0_, bf16[4,576,128]{2,1,0:T(8,128)(2,1)S(1)} %collective-permute-done.3.refs_1_, bf16[4,576,128]{2,1,0:T(8,128)(2,1)S(1)} %collective-permute-done.4.refs_2_, bf16[4,576,128]{2,1,0:T(8,128)(2,1)S(1)} %collective-permute-done.8.refs_3_, ...), custom_call_target="tpu_custom_call" | custom-call | flops 1000000 | bytes 100000 | tf_op jit(solution)/shard_map/gradient_part/pallas_call | solution.py:162
  49.8 7.6 %collective-permute-done.10 = bf16[576,512]{1,0:T(8,128)(2,1)S(1)} collective-permute-done((bf16[576,512]{1,0:T(8,128)(2,1)}, bf16[576,512]{1,0:T(8,128)(2,1)S(1)}, u32[]{:S(2)}, u32[]{:S(2)}) %collective-permute-start.10) | collective-permute-done | bytes 589856 | tf_op jit(solution)/shard_map/ppermute | solution.py:34
  57.4 12.1 %collective-permute-done.11 = bf16[576,512]{1,0:T(8,128)(2,1)S(1)} collective-permute-done((bf16[576,512]{1,0:T(8,128)(2,1)S(1)}, bf16[576,512]{1,0:T(8,128)(2,1)S(1)}, u32[]{:S(2)}, u32[]{:S(2)}) %collective-permute-start.11) | collective-permute-done | bytes 589856 | tf_op jit(solution)/shard_map/ppermute | solution.py:34
  71.0 1.7 %collective-permute-start.13 = (bf16[576,512]{1,0:T(8,128)(2,1)S(1)}, bf16[576,512]{1,0:T(8,128)(2,1)S(1)}, u32[]{:S(2)}, u32[]{:S(2)}) collective-permute-start(bf16[576,512]{1,0:T(8,128)(2,1)S(1)} %gradient_part.7), channel_id=1, source_target_pairs={{0,8},{4,12},{8,0},{12,4},{16,24},{20,28},{24,16},{28,20},{1,9},{5... | collective-permute-start | bytes 1769480 | tf_op jit(solution)/shard_map/ppermute | solution.py:34
  73.9 1.9 %gradient_part.4 = bf16[576,512]{1,0:T(8,128)(2,1)S(1)} custom-call(bf16[4,576,128]{2,1,0:T(8,128)(2,1)S(1)} %get-tuple-element.60.refs_0_, bf16[4,576,128]{2,1,0:T(8,128)(2,1)S(1)} %collective-permute-done.3.refs_1_, bf16[4,576,128]{2,1,0:T(8,128)(2,1)S(1)} %collective-permute-done.4.refs_2_, bf16[4,576,128]{2,1,0:T(8,128)(2,1)S(1)} %collective-permute-done.8.refs_3_, ...), custom_call_target="tpu_custom_call" | custom-call | flops 1000000 | bytes 100000 | tf_op jit(solution)/shard_map/gradient_part/pallas_call | solution.py:162
  75.8 3.2 %pad_maximum_fusion.refs_8_ = bf16[4,576,512]{2,1,0:T(8,128)(2,1)} fusion(bf16[1,576,512]{2,1,0:T(8,128)(2,1)} %bitcast.11, bf16[1,576,512]{2,1,0:T(8,128)(2,1)} %bitcast.10, bf16[1,576,512]{2,1,0:T(8,128)(2,1)} %bitcast.9, bf16[1,576,512]{2,1,0:T(8,128)(2,1)S(1)} %bitcast.47), kind=kLoop, calls=%fused_computation | loop fusion | flops 3538944 | bytes 4718592 | tf_op jit(solution)/shard_map/stack | solution.py:298
  79.0 7.1 %attn_part.1 = (f32[512,512]{1,0:T(8,128)}, bf16[512,512]{1,0:T(8,128)(2,1)S(1)}) custom-call(bf16[4,576,128]{2,1,0:T(8,128)(2,1)S(1)} %get-tuple-element.60.refs_0_, bf16[4,576,128]{2,1,0:T(8,128)(2,1)S(1)} %collective-permute-done.3.refs_1_, bf16[4,576,128]{2,1,0:T(8,128)(2,1)S(1)} %collective-permute-done.4.refs_2_, ...), custom_call_target="tpu_custom_call" | custom-call | flops 1000000 | bytes 100000 | tf_op jit(solution)/shard_map/attn_part/pallas_call | solution.py:200
  86.3 11.7 %collective-permute-done.12 = bf16[576,512]{1,0:T(8,128)(2,1)S(1)} collective-permute-done((bf16[576,512]{1,0:T(8,128)(2,1)S(1)}, bf16[576,512]{1,0:T(8,128)(2,1)S(1)}, u32[]{:S(2)}, u32[]{:S(2)}) %collective-permute-start.12) | collective-permute-done | bytes 589856 | tf_op jit(solution)/shard_map/ppermute | solution.py:34
  98.3 3.6 %subtract_convert_fusion = (bf16[576,512]{1,0:T(8,128)(2,1)S(1)}, f32[576,512]{1,0:T(8,128)}, f32[576,512]{1,0:T(8,128)}) fusion(bf16[576,512]{1,0:T(8,128)(2,1)} %param.10, bf16[576,512]{1,0:T(8,128)(2,1)S(1)} %collective-permute-done.13, bf16[576,512]{1,0:T(8,128)(2,1)S(1)} %collective-permute-done.12, bf16[576,512]{1,0:T(8,128)(2,1)S(1)} %gradient_part.4, ...), kind=kLoop, calls=%fused_computation.7 | loop fusion | flops 6193152 | bytes 7667712 | tf_op jit(solution)/shard_map/convert_element_type | solution.py:29
  103.1 2.5 %collective-permute-start.15 = (bf16[576,512]{1,0:T(8,128)(2,1)S(1)}, bf16[576,512]{1,0:T(8,128)(2,1)S(1)}, u32[]{:S(2)}, u32[]{:S(2)}) collective-permute-start(bf16[576,512]{1,0:T(8,128)(2,1)S(1)} %get-tuple-element.115.block), channel_id=1, source_target_pairs={{0,8},{4,12},{8,0},{12,4},{16,24},{20,28},{24,16},{28,20},{1,9},{5... | collective-permute-start | bytes 1769480 | tf_op jit(solution)/shard_map/ppermute | solution.py:34
  106.3 1.4 collective-permute-start.18
  107.7 24.3 %collective-permute-done.16.block = bf16[576,512]{1,0:T(8,128)(2,1)S(1)} collective-permute-done((bf16[576,512]{1,0:T(8,128)(2,1)S(1)}, bf16[576,512]{1,0:T(8,128)(2,1)S(1)}, u32[]{:S(2)}, u32[]{:S(2)}) %collective-permute-start.16) | collective-permute-done | bytes 589856 | tf_op jit(solution)/shard_map/ppermute | solution.py:34
  137.2 1.6 collective-permute-start.24
  139.4 9.2 %collective-permute-done.20.block = bf16[576,512]{1,0:T(8,128)(2,1)S(1)} collective-permute-done((bf16[576,512]{1,0:T(8,128)(2,1)S(1)}, bf16[576,512]{1,0:T(8,128)(2,1)S(1)}, u32[]{:S(2)}, u32[]{:S(2)}) %collective-permute-start.20) | collective-permute-done | bytes 589856 | tf_op jit(solution)/shard_map/ppermute | solution.py:34
  148.6 2.8 %collective-permute-done.24 = bf16[2,576,128]{2,1,0:T(8,128)(2,1)S(1)} collective-permute-done((bf16[2,576,128]{2,1,0:T(8,128)(2,1)S(1)}, bf16[2,576,128]{2,1,0:T(8,128)(2,1)S(1)}, u32[]{:S(2)}, u32[]{:S(2)}) %collective-permute-start.24) | collective-permute-done | bytes 294944 | tf_op jit(solution)/shard_map/ppermute | solution.py:34
  158.0 6.4 %collective-permute-done.27 = bf16[2,576,128]{2,1,0:T(8,128)(2,1)S(1)} collective-permute-done((bf16[2,576,128]{2,1,0:T(8,128)(2,1)S(1)}, bf16[2,576,128]{2,1,0:T(8,128)(2,1)S(1)}, u32[]{:S(2)}, u32[]{:S(2)}) %collective-permute-start.27) | collective-permute-done | bytes 294944 | tf_op jit(solution)/shard_map/ppermute | solution.py:34
  165.2 1.9 %reorder.5 = bf16[512,512]{1,0:T(8,128)(2,1)} custom-call(s32[4]{0:T(128)S(1)} %pad_add_fusion.index, bf16[512,512]{1,0:T(8,128)(2,1)S(1)} %add_convert_fusion.5.rows), custom_call_target="tpu_custom_call" | custom-call | flops 1000000 | bytes 100000 | tf_op jit(solution)/shard_map/reorder/pallas_call | solution.py:64
  167.1 2.5 %collective-permute-done.30.refs_7_ = bf16[576,128]{1,0:T(8,128)(2,1)S(1)} collective-permute-done((bf16[576,128]{1,0:T(8,128)(2,1)S(1)}, bf16[576,128]{1,0:T(8,128)(2,1)S(1)}, u32[]{:S(2)}, u32[]{:S(2)}) %collective-permute-start.30) | collective-permute-done | bytes 147488 | tf_op jit(solution)/shard_map/ppermute | solution.py:34
  169.6 2.0 %join_features.1 = bf16[128,4608]{1,0:T(8,128)(2,1)} custom-call(s32[8]{0:T(128)S(1)} %pad_add_fusion.3.starts, bf16[576,128]{1,0:T(8,128)(2,1)S(1)} %get-tuple-element.106.refs_0_, bf16[576,128]{1,0:T(8,128)(2,1)S(1)} %get-tuple-element.129.refs_1_, bf16[576,128]{1,0:T(8,128)(2,1)S(1)} %get-tuple-element.127.refs_2_, ...), custom_call_target="tpu_custom_call" | custom-call | flops 1000000 | bytes 100000 | tf_op jit(solution)/shard_map/join_features/pallas_call | solution.py:124
  (97 shorter events, 24.1 us)
Async XLA Ops:
  3.6 16.4 %collective-permute-start.2 = (bf16[4,576,128]{2,1,0:T(8,128)(2,1)S(1)}, bf16[4,576,128]{2,1,0:T(8,128)(2,1)S(1)}, u32[]{:S(2)}, u32[]{:S(2)}) collective-permute-start(bf16[4,576,128]{2,1,0:T(8,128)(2,1)S(1)} %get-tuple-element.61), channel_id=1, source_target_pairs={{0,4},{4,0},{8,12},{12,8},{16,20},{20,16},{24,28},{28,24},{1,5},{5... | collective-permute-start | bytes 1769480 | tf_op jit(solution)/shard_map/ppermute | solution.py:34
  6.7 13.3 %collective-permute-start.4 = (bf16[4,576,128]{2,1,0:T(8,128)(2,1)S(1)}, bf16[4,576,128]{2,1,0:T(8,128)(2,1)S(1)}, u32[]{:S(2)}, u32[]{:S(2)}) collective-permute-start(bf16[4,576,128]{2,1,0:T(8,128)(2,1)S(1)} %get-tuple-element.60.refs_0_), channel_id=1, source_target_pairs={{0,1},{1,0},{2,3},{3,2},{4,5},{5,4},{6,7},{7,6},{8,9},{9,8},{10,11... | collective-permute-start | bytes 1769480 | tf_op jit(solution)/shard_map/ppermute | solution.py:34
  6.7 15.7 %collective-permute-start.3 = (bf16[4,576,128]{2,1,0:T(8,128)(2,1)S(1)}, bf16[4,576,128]{2,1,0:T(8,128)(2,1)S(1)}, u32[]{:S(2)}, u32[]{:S(2)}) collective-permute-start(bf16[4,576,128]{2,1,0:T(8,128)(2,1)S(1)} %get-tuple-element.60.refs_0_), channel_id=1, source_target_pairs={{0,2},{1,3},{2,0},{3,1},{4,6},{5,7},{6,4},{7,5},{8,10},{9,11},{10,... | collective-permute-start | bytes 1769480 | tf_op jit(solution)/shard_map/ppermute | solution.py:34
  8.2 28.3 %collective-permute-start = (bf16[576,512]{1,0:T(8,128)(2,1)}, bf16[576,512]{1,0:T(8,128)(2,1)}, u32[]{:S(2)}, u32[]{:S(2)}) collective-permute-start(bf16[576,512]{1,0:T(8,128)(2,1)} %param.10), channel_id=1, source_target_pairs={{0,8},{4,12},{8,0},{12,4},{16,24},{20,28},{24,16},{28,20},{1,9},{5... | collective-permute-start | bytes 1769480 | tf_op jit(solution)/shard_map/ppermute | solution.py:34
  9.8 29.1 %collective-permute-start.1 = (bf16[576,512]{1,0:T(8,128)(2,1)}, bf16[576,512]{1,0:T(8,128)(2,1)}, u32[]{:S(2)}, u32[]{:S(2)}) collective-permute-start(bf16[576,512]{1,0:T(8,128)(2,1)} %param.10), channel_id=1, source_target_pairs={{0,16},{4,20},{8,24},{12,28},{16,0},{20,4},{24,8},{28,12},{1,17},{... | collective-permute-start | bytes 1769480 | tf_op jit(solution)/shard_map/ppermute | solution.py:34
  22.4 16.4 %collective-permute-start.6 = (bf16[4,576,128]{2,1,0:T(8,128)(2,1)S(1)}, bf16[4,576,128]{2,1,0:T(8,128)(2,1)S(1)}, u32[]{:S(2)}, u32[]{:S(2)}) collective-permute-start(bf16[4,576,128]{2,1,0:T(8,128)(2,1)S(1)} %collective-permute-done.2.refs_4_), channel_id=1, source_target_pairs={{0,1},{1,0},{2,3},{3,2},{4,5},{5,4},{6,7},{7,6},{8,9},{9,8},{10,11... | collective-permute-start | bytes 1769480 | tf_op jit(solution)/shard_map/ppermute | solution.py:34
  22.4 16.4 %collective-permute-start.5 = (bf16[512,512]{1,0:T(8,128)(2,1)S(1)}, bf16[512,512]{1,0:T(8,128)(2,1)S(1)}, u32[]{:S(2)}, u32[]{:S(2)}) collective-permute-start(bf16[512,512]{1,0:T(8,128)(2,1)S(1)} %reorder.3.refs_8_), channel_id=1, source_target_pairs={{0,4},{4,0},{8,12},{12,8},{16,20},{20,16},{24,28},{28,24},{1,5},{5... | collective-permute-start | bytes 1572872 | tf_op jit(solution)/shard_map/ppermute | solution.py:34
  22.7 16.2 %collective-permute-start.7 = (bf16[4,576,128]{2,1,0:T(8,128)(2,1)S(1)}, bf16[4,576,128]{2,1,0:T(8,128)(2,1)S(1)}, u32[]{:S(2)}, u32[]{:S(2)}) collective-permute-start(bf16[4,576,128]{2,1,0:T(8,128)(2,1)S(1)} %collective-permute-done.2.refs_4_), channel_id=1, source_target_pairs={{0,2},{1,3},{2,0},{3,1},{4,6},{5,7},{6,4},{7,5},{8,10},{9,11},{10,... | collective-permute-start | bytes 1769480 | tf_op jit(solution)/shard_map/ppermute | solution.py:34
  38.9 2.0 %collective-permute-start.8 = (bf16[4,576,128]{2,1,0:T(8,128)(2,1)S(1)}, bf16[4,576,128]{2,1,0:T(8,128)(2,1)S(1)}, u32[]{:S(2)}, u32[]{:S(2)}) collective-permute-start(bf16[4,576,128]{2,1,0:T(8,128)(2,1)S(1)} %collective-permute-done.3.refs_1_), channel_id=1, source_target_pairs={{0,1},{1,0},{2,3},{3,2},{4,5},{5,4},{6,7},{7,6},{8,9},{9,8},{10,11... | collective-permute-start | bytes 1769480 | tf_op jit(solution)/shard_map/ppermute | solution.py:34
  40.9 2.0 %collective-permute-start.9 = (bf16[4,576,128]{2,1,0:T(8,128)(2,1)S(1)}, bf16[4,576,128]{2,1,0:T(8,128)(2,1)S(1)}, u32[]{:S(2)}, u32[]{:S(2)}) collective-permute-start(bf16[4,576,128]{2,1,0:T(8,128)(2,1)S(1)} %collective-permute-done.7.refs_5_), channel_id=1, source_target_pairs={{0,1},{1,0},{2,3},{3,2},{4,5},{5,4},{6,7},{7,6},{8,9},{9,8},{10,11... | collective-permute-start | bytes 1769480 | tf_op jit(solution)/shard_map/ppermute | solution.py:34
  41.0 16.4 %collective-permute-start.10 = (bf16[576,512]{1,0:T(8,128)(2,1)}, bf16[576,512]{1,0:T(8,128)(2,1)S(1)}, u32[]{:S(2)}, u32[]{:S(2)}) collective-permute-start(bf16[576,512]{1,0:T(8,128)(2,1)} %collective-permute-done.1), channel_id=1, source_target_pairs={{0,8},{4,12},{8,0},{12,4},{16,24},{20,28},{24,16},{28,20},{1,9},{5... | collective-permute-start | bytes 1769480 | tf_op jit(solution)/shard_map/ppermute | solution.py:34
  45.6 23.9 %collective-permute-start.11 = (bf16[576,512]{1,0:T(8,128)(2,1)S(1)}, bf16[576,512]{1,0:T(8,128)(2,1)S(1)}, u32[]{:S(2)}, u32[]{:S(2)}) collective-permute-start(bf16[576,512]{1,0:T(8,128)(2,1)S(1)} %gradient_part.6), channel_id=1, source_target_pairs={{0,8},{4,12},{8,0},{12,4},{16,24},{20,28},{24,16},{28,20},{1,9},{5... | collective-permute-start | bytes 1769480 | tf_op jit(solution)/shard_map/ppermute | solution.py:34
  49.8 22.9 %copy-start.5 = (bf16[512,512]{1,0:T(8,128)(2,1)S(1)}, bf16[512,512]{1,0:T(8,128)(2,1)}, u32[]{:S(2)}) copy-start(bf16[512,512]{1,0:T(8,128)(2,1)} %rows.3) | copy-start | bytes 1572868
  69.6 28.4 %collective-permute-start.12 = (bf16[576,512]{1,0:T(8,128)(2,1)S(1)}, bf16[576,512]{1,0:T(8,128)(2,1)S(1)}, u32[]{:S(2)}, u32[]{:S(2)}) collective-permute-start(bf16[576,512]{1,0:T(8,128)(2,1)S(1)} %add_convert_fusion.4), channel_id=1, source_target_pairs={{0,16},{4,20},{8,24},{12,28},{16,0},{20,4},{24,8},{28,12},{1,17},{... | collective-permute-start | bytes 1769480 | tf_op jit(solution)/shard_map/ppermute | solution.py:34
  71.0 27.4 %collective-permute-start.13 = (bf16[576,512]{1,0:T(8,128)(2,1)S(1)}, bf16[576,512]{1,0:T(8,128)(2,1)S(1)}, u32[]{:S(2)}, u32[]{:S(2)}) collective-permute-start(bf16[576,512]{1,0:T(8,128)(2,1)S(1)} %gradient_part.7), channel_id=1, source_target_pairs={{0,8},{4,12},{8,0},{12,4},{16,24},{20,28},{24,16},{28,20},{1,9},{5... | collective-permute-start | bytes 1769480 | tf_op jit(solution)/shard_map/ppermute | solution.py:34
  73.4 12.9 %collective-permute-start.14 = (bf16[512,512]{1,0:T(8,128)(2,1)S(1)}, bf16[512,512]{1,0:T(8,128)(2,1)S(1)}, u32[]{:S(2)}, u32[]{:S(2)}) collective-permute-start(bf16[512,512]{1,0:T(8,128)(2,1)S(1)} %reorder.4.next0), channel_id=1, source_target_pairs={{0,4},{4,0},{8,12},{12,8},{16,20},{20,16},{24,28},{28,24},{1,5},{5... | collective-permute-start | bytes 1572872 | tf_op jit(solution)/shard_map/ppermute | solution.py:34
  102.8 3.3 %collective-permute-start.17 = (bf16[2,2,576,128]{3,2,1,0:T(8,128)(2,1)S(1)}, bf16[2,2,576,128]{3,2,1,0:T(8,128)(2,1)S(1)}, u32[]{:S(2)}, u32[]{:S(2)}) collective-permute-start(bf16[2,2,576,128]{3,2,1,0:T(8,128)(2,1)S(1)} %get-tuple-element.88), channel_id=1, source_target_pairs={{0,1},{1,0},{2,3},{3,2},{4,5},{5,4},{6,7},{7,6},{8,9},{9,8},{10,11... | collective-permute-start | bytes 1769480 | tf_op jit(solution)/shard_map/ppermute | solution.py:34
  102.8 29.1 %collective-permute-start.16 = (bf16[576,512]{1,0:T(8,128)(2,1)S(1)}, bf16[576,512]{1,0:T(8,128)(2,1)S(1)}, u32[]{:S(2)}, u32[]{:S(2)}) collective-permute-start(bf16[576,512]{1,0:T(8,128)(2,1)S(1)} %get-tuple-element.115.block), channel_id=1, source_target_pairs={{0,16},{4,20},{8,24},{12,28},{16,0},{20,4},{24,8},{28,12},{1,17},{... | collective-permute-start | bytes 1769480 | tf_op jit(solution)/shard_map/ppermute | solution.py:34
  103.1 28.8 %collective-permute-start.15 = (bf16[576,512]{1,0:T(8,128)(2,1)S(1)}, bf16[576,512]{1,0:T(8,128)(2,1)S(1)}, u32[]{:S(2)}, u32[]{:S(2)}) collective-permute-start(bf16[576,512]{1,0:T(8,128)(2,1)S(1)} %get-tuple-element.115.block), channel_id=1, source_target_pairs={{0,8},{4,12},{8,0},{12,4},{16,24},{20,28},{24,16},{28,20},{1,9},{5... | collective-permute-start | bytes 1769480 | tf_op jit(solution)/shard_map/ppermute | solution.py:34
  105.6 26.3 %collective-permute-start.19 = (bf16[512,512]{1,0:T(8,128)(2,1)S(1)}, bf16[512,512]{1,0:T(8,128)(2,1)S(1)}, u32[]{:S(2)}, u32[]{:S(2)}) collective-permute-start(bf16[512,512]{1,0:T(8,128)(2,1)S(1)} %get-tuple-element.92), channel_id=1, source_target_pairs={{0,4},{4,0},{8,12},{12,8},{16,20},{20,16},{24,28},{28,24},{1,5},{5... | collective-permute-start | bytes 1572872 | tf_op jit(solution)/shard_map/ppermute | solution.py:34
  106.3 25.6 %collective-permute-start.18 = (bf16[2,576,128]{2,1,0:T(8,128)(2,1)S(1)}, bf16[2,576,128]{2,1,0:T(8,128)(2,1)S(1)}, u32[]{:S(2)}, u32[]{:S(2)}) collective-permute-start(bf16[2,576,128]{2,1,0:T(8,128)(2,1)S(1)} %get-tuple-element.122), channel_id=1, source_target_pairs={{0,2},{1,3},{2,0},{3,1},{4,6},{5,7},{6,4},{7,5},{8,10},{9,11},{10,... | collective-permute-start | bytes 884744 | tf_op jit(solution)/shard_map/ppermute | solution.py:34
  132.8 2.1 %collective-permute-start.21 = (bf16[2,2,576,128]{3,2,1,0:T(8,128)(2,1)S(1)}, bf16[2,2,576,128]{3,2,1,0:T(8,128)(2,1)S(1)}, u32[]{:S(2)}, u32[]{:S(2)}) collective-permute-start(bf16[2,2,576,128]{3,2,1,0:T(8,128)(2,1)S(1)} %get-tuple-element.96), channel_id=1, source_target_pairs={{0,1},{1,0},{2,3},{3,2},{4,5},{5,4},{6,7},{7,6},{8,9},{9,8},{10,11... | collective-permute-start | bytes 1769480 | tf_op jit(solution)/shard_map/ppermute | solution.py:34
  132.9 15.7 %collective-permute-start.20 = (bf16[576,512]{1,0:T(8,128)(2,1)S(1)}, bf16[576,512]{1,0:T(8,128)(2,1)S(1)}, u32[]{:S(2)}, u32[]{:S(2)}) collective-permute-start(bf16[576,512]{1,0:T(8,128)(2,1)S(1)} %collective-permute-done.16.block), channel_id=1, source_target_pairs={{0,8},{4,12},{8,0},{12,4},{16,24},{20,28},{24,16},{28,20},{1,9},{5... | collective-permute-start | bytes 1769480 | tf_op jit(solution)/shard_map/ppermute | solution.py:34
  133.7 2.6 %collective-permute-start.22 = (bf16[2,2,576,128]{3,2,1,0:T(8,128)(2,1)S(1)}, bf16[2,2,576,128]{3,2,1,0:T(8,128)(2,1)S(1)}, u32[]{:S(2)}, u32[]{:S(2)}) collective-permute-start(bf16[2,2,576,128]{3,2,1,0:T(8,128)(2,1)S(1)} %get-tuple-element.98), channel_id=1, source_target_pairs={{0,1},{1,0},{2,3},{3,2},{4,5},{5,4},{6,7},{7,6},{8,9},{9,8},{10,11... | collective-permute-start | bytes 1769480 | tf_op jit(solution)/shard_map/ppermute | solution.py:34
  135.8 12.7 %collective-permute-start.23 = (bf16[2,576,128]{2,1,0:T(8,128)(2,1)}, bf16[2,576,128]{2,1,0:T(8,128)(2,1)}, u32[]{:S(2)}, u32[]{:S(2)}) collective-permute-start(bf16[2,576,128]{2,1,0:T(8,128)(2,1)} %get-tuple-element.120), channel_id=1, source_target_pairs={{0,2},{1,3},{2,0},{3,1},{4,6},{5,7},{6,4},{7,5},{8,10},{9,11},{10,... | collective-permute-start | bytes 884744 | tf_op jit(solution)/shard_map/ppermute | solution.py:34
  137.2 14.2 %collective-permute-start.24 = (bf16[2,576,128]{2,1,0:T(8,128)(2,1)S(1)}, bf16[2,576,128]{2,1,0:T(8,128)(2,1)S(1)}, u32[]{:S(2)}, u32[]{:S(2)}) collective-permute-start(bf16[2,576,128]{2,1,0:T(8,128)(2,1)S(1)} %get-tuple-element.118), channel_id=1, source_target_pairs={{0,2},{1,3},{2,0},{3,1},{4,6},{5,7},{6,4},{7,5},{8,10},{9,11},{10,... | collective-permute-start | bytes 884744 | tf_op jit(solution)/shard_map/ppermute | solution.py:34
  138.8 9.7 %collective-permute-start.25 = (bf16[576,128]{1,0:T(8,128)(2,1)S(1)}, bf16[576,128]{1,0:T(8,128)(2,1)S(1)}, u32[]{:S(2)}, u32[]{:S(2)}) collective-permute-start(bf16[576,128]{1,0:T(8,128)(2,1)S(1)} %get-tuple-element.130), channel_id=1, source_target_pairs={{0,4},{4,0},{8,12},{12,8},{16,20},{20,16},{24,28},{28,24},{1,5},{5... | collective-permute-start | bytes 442376 | tf_op jit(solution)/shard_map/ppermute | solution.py:34
  152.9 2.1 %collective-permute-start.26 = (bf16[2,2,576,128]{3,2,1,0:T(8,128)(2,1)S(1)}, bf16[2,2,576,128]{3,2,1,0:T(8,128)(2,1)S(1)}, u32[]{:S(2)}, u32[]{:S(2)}) collective-permute-start(bf16[2,2,576,128]{3,2,1,0:T(8,128)(2,1)S(1)} %get-tuple-element.113), channel_id=1, source_target_pairs={{0,1},{1,0},{2,3},{3,2},{4,5},{5,4},{6,7},{7,6},{8,9},{9,8},{10,11... | collective-permute-start | bytes 1769480 | tf_op jit(solution)/shard_map/ppermute | solution.py:34
  155.2 9.1 %collective-permute-start.27 = (bf16[2,576,128]{2,1,0:T(8,128)(2,1)S(1)}, bf16[2,576,128]{2,1,0:T(8,128)(2,1)S(1)}, u32[]{:S(2)}, u32[]{:S(2)}) collective-permute-start(bf16[2,576,128]{2,1,0:T(8,128)(2,1)S(1)} %slice_bitcast_fusion), channel_id=1, source_target_pairs={{0,2},{1,3},{2,0},{3,1},{4,6},{5,7},{6,4},{7,5},{8,10},{9,11},{10,... | collective-permute-start | bytes 884744 | tf_op jit(solution)/shard_map/ppermute | solution.py:34
  155.8 11.3 %collective-permute-start.29 = (bf16[576,128]{1,0:T(8,128)(2,1)S(1)}, bf16[576,128]{1,0:T(8,128)(2,1)S(1)}, u32[]{:S(2)}, u32[]{:S(2)}) collective-permute-start(bf16[576,128]{1,0:T(8,128)(2,1)S(1)} %get-tuple-element.126), channel_id=1, source_target_pairs={{0,4},{4,0},{8,12},{12,8},{16,20},{20,16},{24,28},{28,24},{1,5},{5... | collective-permute-start | bytes 442376 | tf_op jit(solution)/shard_map/ppermute | solution.py:34
  156.7 10.5 %collective-permute-start.28 = (bf16[576,128]{1,0:T(8,128)(2,1)S(1)}, bf16[576,128]{1,0:T(8,128)(2,1)S(1)}, u32[]{:S(2)}, u32[]{:S(2)}) collective-permute-start(bf16[576,128]{1,0:T(8,128)(2,1)S(1)} %get-tuple-element.128), channel_id=1, source_target_pairs={{0,4},{4,0},{8,12},{12,8},{16,20},{20,16},{24,28},{28,24},{1,5},{5... | collective-permute-start | bytes 442376 | tf_op jit(solution)/shard_map/ppermute | solution.py:34
  164.4 5.2 %collective-permute-start.30 = (bf16[576,128]{1,0:T(8,128)(2,1)S(1)}, bf16[576,128]{1,0:T(8,128)(2,1)S(1)}, u32[]{:S(2)}, u32[]{:S(2)}) collective-permute-start(bf16[576,128]{1,0:T(8,128)(2,1)S(1)} %get-tuple-element.124), channel_id=1, source_target_pairs={{0,4},{4,0},{8,12},{12,8},{16,20},{20,16},{24,28},{28,24},{1,5},{5... | collective-permute-start | bytes 442376 | tf_op jit(solution)/shard_map/ppermute | solution.py:34
  (13 other events, 93.4 us)

commit v5 on v4

--- a/solution.py
+++ b/solution.py
@@ -104,32 +104,33 @@
     )(starts, cotangent)
 
 
-def join_kernel(starts, *refs):
+def join_kernel(cuts, starts, *refs):
     blocks, out, turned = refs[:-2], refs[-2], refs[-1]
-    own = blocks[0].shape[0]
-    for j, block in enumerate(blocks):
-        turned[pl.ds(pl.multiple_of(starts[j], 16), own)] = block[...]
+    for j, (block, first, rows) in enumerate(cuts):
+        turned[pl.ds(pl.multiple_of(starts[j], 16), rows)] = blocks[block][first : first + rows]
     out[...] = turned[...].T
 
 
-def join_features(mine, other, planes, y):
+def join_features(mine, other, cuts, planes, offsets, y):
     n, (own, tok) = len(mine), mine[0].shape
     if own % 16:
         mine, other = jnp.stack(mine), jnp.stack(other)
         both = jnp.stack([jnp.where(y == 0, mine, other), jnp.where(y == 0, other, mine)], axis=1)
         place = jnp.zeros(n, jnp.int32).at[planes].set(jnp.arange(n, dtype=jnp.int32))
         return jnp.take(both, place, axis=0).reshape(2 * n * own, tok).T
-    starts = jnp.concatenate([(2 * planes + y) * own, (2 * planes + 1 - y) * own]).astype(jnp.int32)
+    offsets = jnp.array(offsets, jnp.int32)
+    starts = [(2 * planes + parity) * own + offsets for parity in (y, 1 - y)]
+    cuts = cuts + [(n + block, first, rows) for block, first, rows in cuts]
     vmem = pl.BlockSpec(memory_space=pltpu.VMEM)
     return pl.pallas_call(
-        join_kernel,
+        functools.partial(join_kernel, cuts),
         in_specs=[pl.BlockSpec(memory_space=pltpu.SMEM)] + [vmem] * (2 * n),
         out_shape=jax.ShapeDtypeStruct((tok, 2 * n * own), bf16),
         scratch_shapes=[pltpu.VMEM((2 * n * own, tok), bf16)],
         compiler_params=params(),
         cost_estimate=light(),
         name="join_features",
-    )(starts, *mine, *other)
+    )(jnp.concatenate(starts).astype(jnp.int32), *mine, *other)
 
 
 def params():
@@ -281,50 +282,95 @@
     sums = {}
     for j, r in enumerate(order):
         sums[r] = gradient_part(pieces, saved0, saved1, j, scale)
+    last = [r for r in order if r.bit_count() > 1]
+    halved = n == 4 and own % 32 == 0
+    cut = own // 2
+    if halved:
+        far = sums.pop(3)
+        came = to_plane(far[:cut], 1)
+        old, came, far, near = stage([weights[r] for r in last], came, far, sums[1])
+        weights.update(zip(last, old))
+        came_a = to_plane(add(sums[2][:cut], came), 2)
+        came_b = to_plane(far[cut:], 1)
+        came_a, came_b, near = stage(came_a, came_b, near)
+        came_b = to_plane(add(sums[2][cut:], came_b), 2)
+        came = [came_b, to_plane(near, 1)]
+    else:
+        m = 1
+        while m < top:
+            sends = [r for r in sums if r & m and r != m]
+            came = [to_plane(sums.pop(r), m) for r in sends]
+            old, came, sums[m] = stage([weights[r] for r in last], came, sums[m])
+            weights.update(zip(last, old))
+            for r, value in zip(sends, came):
+                sums[r ^ m] = add(sums[r ^ m], value)
+            m *= 2
+        ends = [1 << k for k in reversed(range(n.bit_length() - 1))]
+        came = [to_plane(value, m) for m, value in zip(ends, stage(*[sums[m] for m in ends]))]
     next0 = reorder(attn_next, inward)
     next1 = to_partner(next0)
-    m = 1
-    while m < top:
-        sends = [r for r in sums if r & m and r != m]
-        came = [to_plane(sums.pop(r), m) for r in sends]
-        last = [r for r in order if r.bit_count() > 1]
-        old, came, sums[m] = stage([weights[r] for r in last], came, sums[m])
-        weights.update(zip(last, old))
-        for r, value in zip(sends, came):
-            sums[r ^ m] = add(sums[r ^ m], value)
-        m *= 2
-    ends = [1 << k for k in reversed(range(n.bit_length() - 1))]
-    gathered, _ = stage([weights[r] for r in order], came)
-    gathered = jnp.stack(gathered)
-    came = [to_plane(value, m) for m, value in zip(ends, stage(*[sums[m] for m in ends]))]
-    kept, sent = attn_part(pieces, gathered)
+    kept, sent = attn_part(pieces, jnp.stack([weights[r] for r in order]))
     came, next1, attn = stage(came, next1, [kept, sent])
+    if halved:
+        came[0] = jnp.concatenate([came_a, came[0]])
     gradient = sums[0].astype(f32) + functools.reduce(jnp.add, [v.astype(f32) for v in came])
     new_weight, new_moment1, new_moment2 = adamw_step(gradient, weight, moment1, moment2)
 
-    held, results = {0: new_weight}, {}
-    for k, wave in enumerate(levels):
-        later = levels[k + 1] if k + 1 < len(levels) else []
-        for r in reversed(later):
-            held[r] = to_plane(held[r & (r - 1)], r & -r)
-        kept, came = {}, {}
-        for r in wave:
-            block, sent = outward_part(held[r], next0, next1)
-            half = add(block, to_core(sent))
-            kept[r], came[r] = half[0], to_chip(half[1])
-        if later:
-            blocks, kept = stage([held[r] for r in later], kept)
-            if k == 0:
-                attn = [attn[0], to_partner(attn[1])]
-            blocks, came, results, attn = stage(blocks, came, results, attn)
-            held.update(zip(later, blocks))
-        for r in wave:
-            total = add(kept[r], came[r])
-            results[r] = (total[0], to_partner(total[1]))
+    def outward(block):
+        own_core, other_core = outward_part(block, next0, next1)
+        half = add(own_core, to_core(other_core))
+        return half[0], to_chip(half[1])
+
+    def finish(kept, came):
+        total = add(kept, came)
+        return total[0], to_partner(total[1])
+
+    if halved:
+        near = to_plane(new_weight, 1)
+        far_a = to_plane(new_weight[:cut], 2)
+        kept0, came0 = outward(new_weight)
+        near, far_a, kept0 = stage(near, far_a, kept0)
+        near, far_a, came0, rest, attn = stage(near, far_a, came0, new_weight, attn)
+        far_b = to_plane(rest[cut:], 2)
+        both_a = to_plane(far_a, 1)
+        attn = [attn[0], to_partner(attn[1])]
+        kept1, came1 = outward(near)
+        far_b, both_a, kept1 = stage(far_b, both_a, kept1)
+        far_b, both_a, came1, attn = stage(far_b, both_a, came1, attn)
+        both_b = to_plane(far_b, 1)
+        result0 = finish(kept0, came0)
+        kept2, came2 = outward(jnp.concatenate([far_a, both_a]))
+        both_b, kept2 = stage(both_b, kept2)
+        both_b, came2, result0 = stage(both_b, came2, result0)
+        result1, result2 = finish(kept1, came1), finish(kept2, came2)
+        results = [result0, result1, result2, finish(*outward(jnp.concatenate([far_b, both_b])))]
+        cuts = [(0, 0, own), (1, 0, own), (2, 0, cut), (2, cut, cut), (3, 0, cut), (3, cut, cut)]
+        offsets = [0, 0, 0, 0, cut, cut]
+        planes = z ^ jnp.array([0, 1, 2, 3, 2, 3], jnp.int32)
+    else:
+        held, results = {0: new_weight}, {}
+        for k, wave in enumerate(levels):
+            later = levels[k + 1] if k + 1 < len(levels) else []
+            for r in reversed(later):
+                held[r] = to_plane(held[r & (r - 1)], r & -r)
+            kept, came = {}, {}
+            for r in wave:
+                kept[r], came[r] = outward(held[r])
+            if later:
+                blocks, kept = stage([held[r] for r in later], kept)
+                if k == 0:
+                    attn = [attn[0], to_partner(attn[1])]
+                blocks, came, results, attn = stage(blocks, came, results, attn)
+                held.update(zip(later, blocks))
+            for r in wave:
+                results[r] = finish(kept[r], came[r])
+        results = [results[r] for r in range(n)]
+        cuts, offsets = [(r, 0, own) for r in range(n)], [0] * n
+        planes = z ^ jnp.arange(n, dtype=jnp.int32)
 
     grad_attn = reorder((attn[0] + attn[1].astype(f32)).astype(bf16), back)
-    mine, other = [[results[r][k] for r in range(n)] for k in range(2)]
-    next_out = join_features(mine, other, z ^ jnp.arange(n, dtype=jnp.int32), y)
+    mine, other = [[result[k] for result in results] for k in range(2)]
+    next_out = join_features(mine, other, cuts, planes, offsets, y)
     return (grad_attn, new_weight, new_moment1, new_moment2, next_out)
 
 

time: 172 us -> 178 us (1.035)
  starting transfers between devices: 26.6 us -> 35.2 us
  waiting for transfers between devices: 105 us -> 103 us
    ppermute x31 -> x35, starting transfers between devices: 26.6 us -> 35.2 us  [flip(): lax.ppermute(value, axis, [(i, i ^ bit) for i in range(lax.axis_size(axis...]
    ppermute x31 -> x35, waiting for transfers between devices: 105 us -> 103 us  [flip(): lax.ppermute(value, axis, [(i, i ^ bit) for i in range(lax.axis_size(axis...]
  transfers between devices with their start and end apart: 31 -> 35, of which waited for: 18 -> 22; matrix products, arithmetic and copies ran while one was open for 4% -> 3% of each run, Pallas kernels for 11% -> 10%
where the time goes in v5:
time: 178 us
  waiting for transfers between devices  103 us (58%)
  starting transfers between devices  35.2 us (20%)
  Pallas kernels  24 us (13%)
  other arithmetic  11.2 us (6%)
  local copies, waits for them, and re-layouts  3.37 us (2%)
    ppermute x35, waiting for transfers between devices, flip(): lax.ppermute(value, axis, [(i, i ^ bit) for i in range(lax.axis_size(axis...  103 us
    ppermute x35, starting transfers between devices, flip(): lax.ppermute(value, axis, [(i, i ^ bit) for i in range(lax.axis_size(axis...  35.2 us
    pallas_call x4, Pallas kernels, gradient_part(): pl.pallas_call(functools.partial(gradient_kernel, scale), grid=(steps,),...  7.41 us
    pallas_call x1, Pallas kernels, attn_part(): pl.pallas_call(attn_kernel, grid=(n,), in_specs=[pl.BlockSpec((1, own, to...  7.1 us
    convert_element_type x1, other arithmetic, adamw_step(): new_weight = (weight.astype(f32) * (1.0 - learning_rate * weight_decay) -...  3.59 us
  transfers between devices with their start and end apart: 35, of which 22 were waited for; matrix products, arithmetic and copies ran while one was open for 3% of the time, Pallas kernels for 10%

profile of v5, /device:TPU:0, one launch (start us, length us, event | category | flops | bytes accessed | tf_op | source)
XLA Modules:
  0.0 177.5 jit_solution(3555223100064145837)
XLA Ops:
  3.6 3.0 %collective-permute-start.2 = (bf16[4,576,128]{2,1,0:T(8,128)(2,1)S(1)}, bf16[4,576,128]{2,1,0:T(8,128)(2,1)S(1)}, u32[]{:S(2)}, u32[]{:S(2)}) collective-permute-start(bf16[4,576,128]{2,1,0:T(8,128)(2,1)S(1)} %get-tuple-element.64), channel_id=1, source_target_pairs={{0,4},{4,0},{8,12},{12,8},{16,20},{20,16},{24,28},{28,24},{1,5},{5... | collective-permute-start | bytes 1769480 | tf_op jit(solution)/shard_map/ppermute | solution.py:34
  8.2 1.6 collective-permute-start
  9.8 2.6 %collective-permute-start.1 = (bf16[576,512]{1,0:T(8,128)(2,1)}, bf16[576,512]{1,0:T(8,128)(2,1)}, u32[]{:S(2)}, u32[]{:S(2)}) collective-permute-start(bf16[576,512]{1,0:T(8,128)(2,1)} %param.12), channel_id=1, source_target_pairs={{0,16},{4,20},{8,24},{12,28},{16,0},{20,4},{24,8},{28,12},{1,17},{... | collective-permute-start | bytes 1769480 | tf_op jit(solution)/shard_map/ppermute | solution.py:34
  13.1 6.9 %collective-permute-done.2.refs_4_ = bf16[4,576,128]{2,1,0:T(8,128)(2,1)S(1)} collective-permute-done((bf16[4,576,128]{2,1,0:T(8,128)(2,1)S(1)}, bf16[4,576,128]{2,1,0:T(8,128)(2,1)S(1)}, u32[]{:S(2)}, u32[]{:S(2)}) %collective-permute-start.2) | collective-permute-done | bytes 589856 | tf_op jit(solution)/shard_map/ppermute | solution.py:34
  20.0 2.4 %collective-permute-done.3.refs_1_ = bf16[4,576,128]{2,1,0:T(8,128)(2,1)S(1)} collective-permute-done((bf16[4,576,128]{2,1,0:T(8,128)(2,1)S(1)}, bf16[4,576,128]{2,1,0:T(8,128)(2,1)S(1)}, u32[]{:S(2)}, u32[]{:S(2)}) %collective-permute-start.3) | collective-permute-done | bytes 589856 | tf_op jit(solution)/shard_map/ppermute | solution.py:34
  22.7 1.7 collective-permute-start.7
  24.4 12.0 %collective-permute-done = bf16[576,512]{1,0:T(8,128)(2,1)} collective-permute-done((bf16[576,512]{1,0:T(8,128)(2,1)}, bf16[576,512]{1,0:T(8,128)(2,1)}, u32[]{:S(2)}, u32[]{:S(2)}) %collective-permute-start) | collective-permute-done | bytes 589856 | tf_op jit(solution)/shard_map/ppermute | solution.py:34
  36.5 2.4 %collective-permute-done.1 = bf16[576,512]{1,0:T(8,128)(2,1)} collective-permute-done((bf16[576,512]{1,0:T(8,128)(2,1)}, bf16[576,512]{1,0:T(8,128)(2,1)}, u32[]{:S(2)}, u32[]{:S(2)}) %collective-permute-start.1) | collective-permute-done | bytes 589856 | tf_op jit(solution)/shard_map/ppermute | solution.py:34
  38.9 2.0 %collective-permute-done.8.refs_3_ = bf16[4,576,128]{2,1,0:T(8,128)(2,1)S(1)} collective-permute-done((bf16[4,576,128]{2,1,0:T(8,128)(2,1)S(1)}, bf16[4,576,128]{2,1,0:T(8,128)(2,1)S(1)}, u32[]{:S(2)}, u32[]{:S(2)}) %collective-permute-start.8) | collective-permute-done | bytes 589856 | tf_op jit(solution)/shard_map/ppermute | solution.py:34
  43.7 1.8 %gradient_part.6 = bf16[576,512]{1,0:T(8,128)(2,1)S(1)} custom-call(bf16[4,576,128]{2,1,0:T(8,128)(2,1)S(1)} %get-tuple-element.63.refs_0_, bf16[4,576,128]{2,1,0:T(8,128)(2,1)S(1)} %collective-permute-done.3.refs_1_, bf16[4,576,128]{2,1,0:T(8,128)(2,1)S(1)} %collective-permute-done.4.refs_2_, bf16[4,576,128]{2,1,0:T(8,128)(2,1)S(1)} %collective-permute-done.8.refs_3_, ...), custom_call_target="tpu_custom_call" | custom-call | flops 1000000 | bytes 100000 | tf_op jit(solution)/shard_map/gradient_part/pallas_call | solution.py:163
  46.1 1.9 %gradient_part.5 = bf16[576,512]{1,0:T(8,128)(2,1)S(1)} custom-call(bf16[4,576,128]{2,1,0:T(8,128)(2,1)S(1)} %get-tuple-element.63.refs_0_, bf16[4,576,128]{2,1,0:T(8,128)(2,1)S(1)} %collective-permute-done.3.refs_1_, bf16[4,576,128]{2,1,0:T(8,128)(2,1)S(1)} %collective-permute-done.4.refs_2_, bf16[4,576,128]{2,1,0:T(8,128)(2,1)S(1)} %collective-permute-done.8.refs_3_, ...), custom_call_target="tpu_custom_call" | custom-call | flops 1000000 | bytes 100000 | tf_op jit(solution)/shard_map/gradient_part/pallas_call | solution.py:163
  47.9 1.9 %gradient_part.7 = bf16[576,512]{1,0:T(8,128)(2,1)S(1)} custom-call(bf16[4,576,128]{2,1,0:T(8,128)(2,1)S(1)} %get-tuple-element.63.refs_0_, bf16[4,576,128]{2,1,0:T(8,128)(2,1)S(1)} %collective-permute-done.3.refs_1_, bf16[4,576,128]{2,1,0:T(8,128)(2,1)S(1)} %collective-permute-done.4.refs_2_, bf16[4,576,128]{2,1,0:T(8,128)(2,1)S(1)} %collective-permute-done.8.refs_3_, ...), custom_call_target="tpu_custom_call" | custom-call | flops 1000000 | bytes 100000 | tf_op jit(solution)/shard_map/gradient_part/pallas_call | solution.py:163
  49.8 7.6 %collective-permute-done.10 = bf16[576,512]{1,0:T(8,128)(2,1)S(1)} collective-permute-done((bf16[576,512]{1,0:T(8,128)(2,1)}, bf16[576,512]{1,0:T(8,128)(2,1)S(1)}, u32[]{:S(2)}, u32[]{:S(2)}) %collective-permute-start.10) | collective-permute-done | bytes 589856 | tf_op jit(solution)/shard_map/ppermute | solution.py:34
  57.4 5.8 %collective-permute-done.11 = bf16[288,512]{1,0:T(8,128)(2,1)S(1)} collective-permute-done((bf16[288,512]{1,0:T(8,128)(2,1)S(1)}, bf16[288,512]{1,0:T(8,128)(2,1)S(1)}, u32[]{:S(2)}, u32[]{:S(2)}) %collective-permute-start.11) | collective-permute-done | bytes 294944 | tf_op jit(solution)/shard_map/ppermute | solution.py:34
  63.7 2.7 %collective-permute-start.12 = (bf16[288,512]{1,0:T(8,128)(2,1)S(1)}, bf16[288,512]{1,0:T(8,128)(2,1)S(1)}, u32[]{:S(2)}, u32[]{:S(2)}) collective-permute-start(bf16[288,512]{1,0:T(8,128)(2,1)S(1)} %add_convert_fusion.9), channel_id=1, source_target_pairs={{0,16},{4,20},{8,24},{12,28},{16,0},{20,4},{24,8},{28,12},{1,17},{... | collective-permute-start | bytes 884744 | tf_op jit(solution)/shard_map/ppermute | solution.py:34
  66.4 11.4 %collective-permute-done.13 = bf16[288,512]{1,0:T(8,128)(2,1)S(1)} collective-permute-done((bf16[288,512]{1,0:T(8,128)(2,1)S(1)}, bf16[288,512]{1,0:T(8,128)(2,1)S(1)}, u32[]{:S(2)}, u32[]{:S(2)}) %collective-permute-start.13) | collective-permute-done | bytes 294944 | tf_op jit(solution)/shard_map/ppermute | solution.py:34
  80.9 2.9 %collective-permute-start.14 = (bf16[288,512]{1,0:T(8,128)(2,1)S(1)}, bf16[288,512]{1,0:T(8,128)(2,1)S(1)}, u32[]{:S(2)}, u32[]{:S(2)}) collective-permute-start(bf16[288,512]{1,0:T(8,128)(2,1)S(1)} %add_convert_fusion.8), channel_id=1, source_target_pairs={{0,16},{4,20},{8,24},{12,28},{16,0},{20,4},{24,8},{28,12},{1,17},{... | collective-permute-start | bytes 884744 | tf_op jit(solution)/shard_map/ppermute | solution.py:34
  83.8 1.9 %gradient_part.4 = bf16[576,512]{1,0:T(8,128)(2,1)S(1)} custom-call(bf16[4,576,128]{2,1,0:T(8,128)(2,1)S(1)} %get-tuple-element.63.refs_0_, bf16[4,576,128]{2,1,0:T(8,128)(2,1)S(1)} %collective-permute-done.3.refs_1_, bf16[4,576,128]{2,1,0:T(8,128)(2,1)S(1)} %collective-permute-done.4.refs_2_, bf16[4,576,128]{2,1,0:T(8,128)(2,1)S(1)} %collective-permute-done.8.refs_3_, ...), custom_call_target="tpu_custom_call" | custom-call | flops 1000000 | bytes 100000 | tf_op jit(solution)/shard_map/gradient_part/pallas_call | solution.py:163
  85.7 3.2 %pad_maximum_fusion.refs_8_ = bf16[4,576,512]{2,1,0:T(8,128)(2,1)} fusion(bf16[1,576,512]{2,1,0:T(8,128)(2,1)} %bitcast.11, bf16[1,576,512]{2,1,0:T(8,128)(2,1)} %bitcast.10, bf16[1,576,512]{2,1,0:T(8,128)(2,1)} %bitcast.9, bf16[1,576,512]{2,1,0:T(8,128)(2,1)S(1)} %bitcast.47), kind=kLoop, calls=%fused_computation | loop fusion | flops 3538944 | bytes 4718592 | tf_op jit(solution)/shard_map/stack | solution.py:312
  88.9 7.1 %attn_part.1 = (f32[512,512]{1,0:T(8,128)}, bf16[512,512]{1,0:T(8,128)(2,1)S(1)}) custom-call(bf16[4,576,128]{2,1,0:T(8,128)(2,1)S(1)} %get-tuple-element.63.refs_0_, bf16[4,576,128]{2,1,0:T(8,128)(2,1)S(1)} %collective-permute-done.3.refs_1_, bf16[4,576,128]{2,1,0:T(8,128)(2,1)S(1)} %collective-permute-done.4.refs_2_, ...), custom_call_target="tpu_custom_call" | custom-call | flops 1000000 | bytes 100000 | tf_op jit(solution)/shard_map/attn_part/pallas_call | solution.py:201
  96.0 1.6 collective-permute-done.14
  98.3 3.6 %subtract_convert_fusion = (bf16[576,512]{1,0:T(8,128)(2,1)S(1)}, f32[576,512]{1,0:T(8,128)}, f32[576,512]{1,0:T(8,128)}) fusion(bf16[576,512]{1,0:T(8,128)(2,1)} %param.12, bf16[576,512]{1,0:T(8,128)(2,1)S(1)} %collective-permute-done.15, bf16[288,512]{1,0:T(8,128)(2,1)S(1)} %collective-permute-done.14, bf16[288,512]{1,0:T(8,128)(2,1)S(1)} %collective-permute-done.12, ...), kind=kLoop, calls=%fused_computation.7 | loop fusion | flops 7077888 | bytes 7667712 | tf_op jit(solution)/shard_map/convert_element_type | solution.py:29
  104.2 1.7 collective-permute-start.18
  106.7 17.1 %collective-permute-done.18 = bf16[288,512]{1,0:T(8,128)(2,1)S(1)} collective-permute-done((bf16[288,512]{1,0:T(8,128)(2,1)S(1)}, bf16[288,512]{1,0:T(8,128)(2,1)S(1)}, u32[]{:S(2)}, u32[]{:S(2)}) %collective-permute-start.18) | collective-permute-done | bytes 294944 | tf_op jit(solution)/shard_map/ppermute | solution.py:34
  125.9 2.3 %collective-permute-start.21 = (bf16[288,512]{1,0:T(8,128)(2,1)S(1)}, bf16[288,512]{1,0:T(8,128)(2,1)}, u32[]{:S(2)}, u32[]{:S(2)}) collective-permute-start(bf16[288,512]{1,0:T(8,128)(2,1)S(1)} %slice.73), channel_id=1, source_target_pairs={{0,16},{4,20},{8,24},{12,28},{16,0},{20,4},{24,8},{28,12},{1,17},{... | collective-permute-start | bytes 884744 | tf_op jit(solution)/shard_map/ppermute | solution.py:34
  131.0 11.6 %collective-permute-done.21 = bf16[288,512]{1,0:T(8,128)(2,1)} collective-permute-done((bf16[288,512]{1,0:T(8,128)(2,1)S(1)}, bf16[288,512]{1,0:T(8,128)(2,1)}, u32[]{:S(2)}, u32[]{:S(2)}) %collective-permute-start.21) | collective-permute-done | bytes 294944 | tf_op jit(solution)/shard_map/ppermute | solution.py:34
  149.5 5.0 %collective-permute-done.26 = bf16[288,512]{1,0:T(8,128)(2,1)S(1)} collective-permute-done((bf16[288,512]{1,0:T(8,128)(2,1)}, bf16[288,512]{1,0:T(8,128)(2,1)S(1)}, u32[]{:S(2)}, u32[]{:S(2)}) %collective-permute-start.26) | collective-permute-done | bytes 294944 | tf_op jit(solution)/shard_map/ppermute | solution.py:34
  154.5 2.5 %collective-permute-done.28 = bf16[2,576,128]{2,1,0:T(8,128)(2,1)S(1)} collective-permute-done((bf16[2,576,128]{2,1,0:T(8,128)(2,1)S(1)}, bf16[2,576,128]{2,1,0:T(8,128)(2,1)S(1)}, u32[]{:S(2)}, u32[]{:S(2)}) %collective-permute-start.28) | collective-permute-done | bytes 294944 | tf_op jit(solution)/shard_map/ppermute | solution.py:34
  163.2 7.1 %collective-permute-done.31 = bf16[2,576,128]{2,1,0:T(8,128)(2,1)S(1)} collective-permute-done((bf16[2,576,128]{2,1,0:T(8,128)(2,1)S(1)}, bf16[2,576,128]{2,1,0:T(8,128)(2,1)S(1)}, u32[]{:S(2)}, u32[]{:S(2)}) %collective-permute-start.31) | collective-permute-done | bytes 294944 | tf_op jit(solution)/shard_map/ppermute | solution.py:34
  171.7 1.9 %reorder.5 = bf16[512,512]{1,0:T(8,128)(2,1)} custom-call(s32[4]{0:T(128)S(1)} %pad_add_fusion.index, bf16[512,512]{1,0:T(8,128)(2,1)S(1)} %add_convert_fusion.4.rows), custom_call_target="tpu_custom_call" | custom-call | flops 1000000 | bytes 100000 | tf_op jit(solution)/shard_map/reorder/pallas_call | solution.py:64
  173.6 1.9 %collective-permute-done.34.refs_7_ = bf16[576,128]{1,0:T(8,128)(2,1)S(1)} collective-permute-done((bf16[576,128]{1,0:T(8,128)(2,1)S(1)}, bf16[576,128]{1,0:T(8,128)(2,1)S(1)}, u32[]{:S(2)}, u32[]{:S(2)}) %collective-permute-start.34) | collective-permute-done | bytes 147488 | tf_op jit(solution)/shard_map/ppermute | solution.py:34
  175.5 2.0 %join_features.1 = bf16[128,4608]{1,0:T(8,128)(2,1)} custom-call(s32[12]{0:T(128)S(1)} %pad_add_fusion.3.starts, bf16[576,128]{1,0:T(8,128)(2,1)S(1)} %get-tuple-element.112.refs_0_, bf16[576,128]{1,0:T(8,128)(2,1)S(1)} %get-tuple-element.135.refs_1_, bf16[576,128]{1,0:T(8,128)(2,1)S(1)} %get-tuple-element.133.refs_2_, ...), custom_call_target="tpu_custom_call" | custom-call | flops 1000000 | bytes 100000 | tf_op jit(solution)/shard_map/join_features/pallas_call | solution.py:125
  (119 shorter events, 35.5 us)
Async XLA Ops:
  3.6 16.4 %collective-permute-start.2 = (bf16[4,576,128]{2,1,0:T(8,128)(2,1)S(1)}, bf16[4,576,128]{2,1,0:T(8,128)(2,1)S(1)}, u32[]{:S(2)}, u32[]{:S(2)}) collective-permute-start(bf16[4,576,128]{2,1,0:T(8,128)(2,1)S(1)} %get-tuple-element.64), channel_id=1, source_target_pairs={{0,4},{4,0},{8,12},{12,8},{16,20},{20,16},{24,28},{28,24},{1,5},{5... | collective-permute-start | bytes 1769480 | tf_op jit(solution)/shard_map/ppermute | solution.py:34
  6.7 13.3 %collective-permute-start.4 = (bf16[4,576,128]{2,1,0:T(8,128)(2,1)S(1)}, bf16[4,576,128]{2,1,0:T(8,128)(2,1)S(1)}, u32[]{:S(2)}, u32[]{:S(2)}) collective-permute-start(bf16[4,576,128]{2,1,0:T(8,128)(2,1)S(1)} %get-tuple-element.63.refs_0_), channel_id=1, source_target_pairs={{0,1},{1,0},{2,3},{3,2},{4,5},{5,4},{6,7},{7,6},{8,9},{9,8},{10,11... | collective-permute-start | bytes 1769480 | tf_op jit(solution)/shard_map/ppermute | solution.py:34
  6.7 15.7 %collective-permute-start.3 = (bf16[4,576,128]{2,1,0:T(8,128)(2,1)S(1)}, bf16[4,576,128]{2,1,0:T(8,128)(2,1)S(1)}, u32[]{:S(2)}, u32[]{:S(2)}) collective-permute-start(bf16[4,576,128]{2,1,0:T(8,128)(2,1)S(1)} %get-tuple-element.63.refs_0_), channel_id=1, source_target_pairs={{0,2},{1,3},{2,0},{3,1},{4,6},{5,7},{6,4},{7,5},{8,10},{9,11},{10,... | collective-permute-start | bytes 1769480 | tf_op jit(solution)/shard_map/ppermute | solution.py:34
  8.2 28.3 %collective-permute-start = (bf16[576,512]{1,0:T(8,128)(2,1)}, bf16[576,512]{1,0:T(8,128)(2,1)}, u32[]{:S(2)}, u32[]{:S(2)}) collective-permute-start(bf16[576,512]{1,0:T(8,128)(2,1)} %param.12), channel_id=1, source_target_pairs={{0,8},{4,12},{8,0},{12,4},{16,24},{20,28},{24,16},{28,20},{1,9},{5... | collective-permute-start | bytes 1769480 | tf_op jit(solution)/shard_map/ppermute | solution.py:34
  9.8 29.1 %collective-permute-start.1 = (bf16[576,512]{1,0:T(8,128)(2,1)}, bf16[576,512]{1,0:T(8,128)(2,1)}, u32[]{:S(2)}, u32[]{:S(2)}) collective-permute-start(bf16[576,512]{1,0:T(8,128)(2,1)} %param.12), channel_id=1, source_target_pairs={{0,16},{4,20},{8,24},{12,28},{16,0},{20,4},{24,8},{28,12},{1,17},{... | collective-permute-start | bytes 1769480 | tf_op jit(solution)/shard_map/ppermute | solution.py:34
  22.4 16.4 %collective-permute-start.6 = (bf16[4,576,128]{2,1,0:T(8,128)(2,1)S(1)}, bf16[4,576,128]{2,1,0:T(8,128)(2,1)S(1)}, u32[]{:S(2)}, u32[]{:S(2)}) collective-permute-start(bf16[4,576,128]{2,1,0:T(8,128)(2,1)S(1)} %collective-permute-done.2.refs_4_), channel_id=1, source_target_pairs={{0,1},{1,0},{2,3},{3,2},{4,5},{5,4},{6,7},{7,6},{8,9},{9,8},{10,11... | collective-permute-start | bytes 1769480 | tf_op jit(solution)/shard_map/ppermute | solution.py:34
  22.4 16.4 %collective-permute-start.5 = (bf16[512,512]{1,0:T(8,128)(2,1)S(1)}, bf16[512,512]{1,0:T(8,128)(2,1)S(1)}, u32[]{:S(2)}, u32[]{:S(2)}) collective-permute-start(bf16[512,512]{1,0:T(8,128)(2,1)S(1)} %reorder.3.refs_8_), channel_id=1, source_target_pairs={{0,4},{4,0},{8,12},{12,8},{16,20},{20,16},{24,28},{28,24},{1,5},{5... | collective-permute-start | bytes 1572872 | tf_op jit(solution)/shard_map/ppermute | solution.py:34
  22.7 16.2 %collective-permute-start.7 = (bf16[4,576,128]{2,1,0:T(8,128)(2,1)S(1)}, bf16[4,576,128]{2,1,0:T(8,128)(2,1)S(1)}, u32[]{:S(2)}, u32[]{:S(2)}) collective-permute-start(bf16[4,576,128]{2,1,0:T(8,128)(2,1)S(1)} %collective-permute-done.2.refs_4_), channel_id=1, source_target_pairs={{0,2},{1,3},{2,0},{3,1},{4,6},{5,7},{6,4},{7,5},{8,10},{9,11},{10,... | collective-permute-start | bytes 1769480 | tf_op jit(solution)/shard_map/ppermute | solution.py:34
  41.0 16.4 %collective-permute-start.10 = (bf16[576,512]{1,0:T(8,128)(2,1)}, bf16[576,512]{1,0:T(8,128)(2,1)S(1)}, u32[]{:S(2)}, u32[]{:S(2)}) collective-permute-start(bf16[576,512]{1,0:T(8,128)(2,1)} %collective-permute-done.1), channel_id=1, source_target_pairs={{0,8},{4,12},{8,0},{12,4},{16,24},{20,28},{24,16},{28,20},{1,9},{5... | collective-permute-start | bytes 1769480 | tf_op jit(solution)/shard_map/ppermute | solution.py:34
  45.6 17.6 %collective-permute-start.11 = (bf16[288,512]{1,0:T(8,128)(2,1)S(1)}, bf16[288,512]{1,0:T(8,128)(2,1)S(1)}, u32[]{:S(2)}, u32[]{:S(2)}) collective-permute-start(bf16[288,512]{1,0:T(8,128)(2,1)S(1)} %slice.89), channel_id=1, source_target_pairs={{0,8},{4,12},{8,0},{12,4},{16,24},{20,28},{24,16},{28,20},{1,9},{5... | collective-permute-start | bytes 884744 | tf_op jit(solution)/shard_map/ppermute | solution.py:34
  63.2 14.7 %collective-permute-start.13 = (bf16[288,512]{1,0:T(8,128)(2,1)S(1)}, bf16[288,512]{1,0:T(8,128)(2,1)S(1)}, u32[]{:S(2)}, u32[]{:S(2)}) collective-permute-start(bf16[288,512]{1,0:T(8,128)(2,1)S(1)} %slice.68), channel_id=1, source_target_pairs={{0,8},{4,12},{8,0},{12,4},{16,24},{20,28},{24,16},{28,20},{1,9},{5... | collective-permute-start | bytes 884744 | tf_op jit(solution)/shard_map/ppermute | solution.py:34
  63.7 15.5 %collective-permute-start.12 = (bf16[288,512]{1,0:T(8,128)(2,1)S(1)}, bf16[288,512]{1,0:T(8,128)(2,1)S(1)}, u32[]{:S(2)}, u32[]{:S(2)}) collective-permute-start(bf16[288,512]{1,0:T(8,128)(2,1)S(1)} %add_convert_fusion.9), channel_id=1, source_target_pairs={{0,16},{4,20},{8,24},{12,28},{16,0},{20,4},{24,8},{28,12},{1,17},{... | collective-permute-start | bytes 884744 | tf_op jit(solution)/shard_map/ppermute | solution.py:34
  79.3 19.0 %collective-permute-start.15 = (bf16[576,512]{1,0:T(8,128)(2,1)S(1)}, bf16[576,512]{1,0:T(8,128)(2,1)S(1)}, u32[]{:S(2)}, u32[]{:S(2)}) collective-permute-start(bf16[576,512]{1,0:T(8,128)(2,1)S(1)} %gradient_part.7), channel_id=1, source_target_pairs={{0,8},{4,12},{8,0},{12,4},{16,24},{20,28},{24,16},{28,20},{1,9},{5... | collective-permute-start | bytes 1769480 | tf_op jit(solution)/shard_map/ppermute | solution.py:34
  80.3 15.7 %collective-permute-start.16 = (bf16[512,512]{1,0:T(8,128)(2,1)S(1)}, bf16[512,512]{1,0:T(8,128)(2,1)S(1)}, u32[]{:S(2)}, u32[]{:S(2)}) collective-permute-start(bf16[512,512]{1,0:T(8,128)(2,1)S(1)} %reorder.4.next0), channel_id=1, source_target_pairs={{0,4},{4,0},{8,12},{12,8},{16,20},{20,16},{24,28},{28,24},{1,5},{5... | collective-permute-start | bytes 1572872 | tf_op jit(solution)/shard_map/ppermute | solution.py:34
  80.9 16.6 %collective-permute-start.14 = (bf16[288,512]{1,0:T(8,128)(2,1)S(1)}, bf16[288,512]{1,0:T(8,128)(2,1)S(1)}, u32[]{:S(2)}, u32[]{:S(2)}) collective-permute-start(bf16[288,512]{1,0:T(8,128)(2,1)S(1)} %add_convert_fusion.8), channel_id=1, source_target_pairs={{0,16},{4,20},{8,24},{12,28},{16,0},{20,4},{24,8},{28,12},{1,17},{... | collective-permute-start | bytes 884744 | tf_op jit(solution)/shard_map/ppermute | solution.py:34
  102.7 3.2 %collective-permute-start.19 = (bf16[2,2,576,128]{3,2,1,0:T(8,128)(2,1)S(1)}, bf16[2,2,576,128]{3,2,1,0:T(8,128)(2,1)S(1)}, u32[]{:S(2)}, u32[]{:S(2)}) collective-permute-start(bf16[2,2,576,128]{3,2,1,0:T(8,128)(2,1)S(1)} %get-tuple-element.89), channel_id=1, source_target_pairs={{0,1},{1,0},{2,3},{3,2},{4,5},{5,4},{6,7},{7,6},{8,9},{9,8},{10,11... | collective-permute-start | bytes 1769480 | tf_op jit(solution)/shard_map/ppermute | solution.py:34
  102.8 22.1 %collective-permute-start.17 = (bf16[576,512]{1,0:T(8,128)(2,1)S(1)}, bf16[576,512]{1,0:T(8,128)(2,1)S(1)}, u32[]{:S(2)}, u32[]{:S(2)}) collective-permute-start(bf16[576,512]{1,0:T(8,128)(2,1)S(1)} %get-tuple-element.94.block), channel_id=1, source_target_pairs={{0,8},{4,12},{8,0},{12,4},{16,24},{20,28},{24,16},{28,20},{1,9},{5... | collective-permute-start | bytes 1769480 | tf_op jit(solution)/shard_map/ppermute | solution.py:34
  104.2 19.6 %collective-permute-start.18 = (bf16[288,512]{1,0:T(8,128)(2,1)S(1)}, bf16[288,512]{1,0:T(8,128)(2,1)S(1)}, u32[]{:S(2)}, u32[]{:S(2)}) collective-permute-start(bf16[288,512]{1,0:T(8,128)(2,1)S(1)} %slice.91), channel_id=1, source_target_pairs={{0,16},{4,20},{8,24},{12,28},{16,0},{20,4},{24,8},{28,12},{1,17},{... | collective-permute-start | bytes 884744 | tf_op jit(solution)/shard_map/ppermute | solution.py:34
  106.1 18.8 %collective-permute-start.20 = (bf16[2,576,128]{2,1,0:T(8,128)(2,1)S(1)}, bf16[2,576,128]{2,1,0:T(8,128)(2,1)S(1)}, u32[]{:S(2)}, u32[]{:S(2)}) collective-permute-start(bf16[2,576,128]{2,1,0:T(8,128)(2,1)S(1)} %get-tuple-element.128), channel_id=1, source_target_pairs={{0,2},{1,3},{2,0},{3,1},{4,6},{5,7},{6,4},{7,5},{8,10},{9,11},{10,... | collective-permute-start | bytes 884744 | tf_op jit(solution)/shard_map/ppermute | solution.py:34
  125.8 3.7 %collective-permute-start.23 = (bf16[2,2,576,128]{3,2,1,0:T(8,128)(2,1)S(1)}, bf16[2,2,576,128]{3,2,1,0:T(8,128)(2,1)S(1)}, u32[]{:S(2)}, u32[]{:S(2)}) collective-permute-start(bf16[2,2,576,128]{3,2,1,0:T(8,128)(2,1)S(1)} %get-tuple-element.98), channel_id=1, source_target_pairs={{0,1},{1,0},{2,3},{3,2},{4,5},{5,4},{6,7},{7,6},{8,9},{9,8},{10,11... | collective-permute-start | bytes 1769480 | tf_op jit(solution)/shard_map/ppermute | solution.py:34
  125.9 16.8 %collective-permute-start.21 = (bf16[288,512]{1,0:T(8,128)(2,1)S(1)}, bf16[288,512]{1,0:T(8,128)(2,1)}, u32[]{:S(2)}, u32[]{:S(2)}) collective-permute-start(bf16[288,512]{1,0:T(8,128)(2,1)S(1)} %slice.73), channel_id=1, source_target_pairs={{0,16},{4,20},{8,24},{12,28},{16,0},{20,4},{24,8},{28,12},{1,17},{... | collective-permute-start | bytes 884744 | tf_op jit(solution)/shard_map/ppermute | solution.py:34
  128.2 14.5 %collective-permute-start.22 = (bf16[288,512]{1,0:T(8,128)(2,1)S(1)}, bf16[288,512]{1,0:T(8,128)(2,1)S(1)}, u32[]{:S(2)}, u32[]{:S(2)}) collective-permute-start(bf16[288,512]{1,0:T(8,128)(2,1)S(1)} %collective-permute-done.18), channel_id=1, source_target_pairs={{0,8},{4,12},{8,0},{12,4},{16,24},{20,28},{24,16},{28,20},{1,9},{5... | collective-permute-start | bytes 884744 | tf_op jit(solution)/shard_map/ppermute | solution.py:34
  129.0 13.8 %collective-permute-start.25 = (bf16[512,512]{1,0:T(8,128)(2,1)S(1)}, bf16[512,512]{1,0:T(8,128)(2,1)S(1)}, u32[]{:S(2)}, u32[]{:S(2)}) collective-permute-start(bf16[512,512]{1,0:T(8,128)(2,1)S(1)} %get-tuple-element.102), channel_id=1, source_target_pairs={{0,4},{4,0},{8,12},{12,8},{16,20},{20,16},{24,28},{28,24},{1,5},{5... | collective-permute-start | bytes 1572872 | tf_op jit(solution)/shard_map/ppermute | solution.py:34
  129.7 13.0 %collective-permute-start.24 = (bf16[2,576,128]{2,1,0:T(8,128)(2,1)S(1)}, bf16[2,576,128]{2,1,0:T(8,128)(2,1)S(1)}, u32[]{:S(2)}, u32[]{:S(2)}) collective-permute-start(bf16[2,576,128]{2,1,0:T(8,128)(2,1)S(1)} %get-tuple-element.126), channel_id=1, source_target_pairs={{0,2},{1,3},{2,0},{3,1},{4,6},{5,7},{6,4},{7,5},{8,10},{9,11},{10,... | collective-permute-start | bytes 884744 | tf_op jit(solution)/shard_map/ppermute | solution.py:34
  144.4 2.2 %collective-permute-start.27 = (bf16[2,2,576,128]{3,2,1,0:T(8,128)(2,1)S(1)}, bf16[2,2,576,128]{3,2,1,0:T(8,128)(2,1)}, u32[]{:S(2)}, u32[]{:S(2)}) collective-permute-start(bf16[2,2,576,128]{3,2,1,0:T(8,128)(2,1)S(1)} %get-tuple-element.108), channel_id=1, source_target_pairs={{0,1},{1,0},{2,3},{3,2},{4,5},{5,4},{6,7},{7,6},{8,9},{9,8},{10,11... | collective-permute-start | bytes 1769480 | tf_op jit(solution)/shard_map/ppermute | solution.py:34
  144.7 9.8 %collective-permute-start.29 = (bf16[576,128]{1,0:T(8,128)(2,1)S(1)}, bf16[576,128]{1,0:T(8,128)(2,1)S(1)}, u32[]{:S(2)}, u32[]{:S(2)}) collective-permute-start(bf16[576,128]{1,0:T(8,128)(2,1)S(1)} %get-tuple-element.136), channel_id=1, source_target_pairs={{0,4},{4,0},{8,12},{12,8},{16,20},{20,16},{24,28},{28,24},{1,5},{5... | collective-permute-start | bytes 442376 | tf_op jit(solution)/shard_map/ppermute | solution.py:34
  145.3 9.2 %collective-permute-start.26 = (bf16[288,512]{1,0:T(8,128)(2,1)}, bf16[288,512]{1,0:T(8,128)(2,1)S(1)}, u32[]{:S(2)}, u32[]{:S(2)}) collective-permute-start(bf16[288,512]{1,0:T(8,128)(2,1)} %collective-permute-done.21), channel_id=1, source_target_pairs={{0,8},{4,12},{8,0},{12,4},{16,24},{20,28},{24,16},{28,20},{1,9},{5... | collective-permute-start | bytes 884744 | tf_op jit(solution)/shard_map/ppermute | solution.py:34
  147.9 9.1 %collective-permute-start.28 = (bf16[2,576,128]{2,1,0:T(8,128)(2,1)S(1)}, bf16[2,576,128]{2,1,0:T(8,128)(2,1)S(1)}, u32[]{:S(2)}, u32[]{:S(2)}) collective-permute-start(bf16[2,576,128]{2,1,0:T(8,128)(2,1)S(1)} %get-tuple-element.124), channel_id=1, source_target_pairs={{0,2},{1,3},{2,0},{3,1},{4,6},{5,7},{6,4},{7,5},{8,10},{9,11},{10,... | collective-permute-start | bytes 884744 | tf_op jit(solution)/shard_map/ppermute | solution.py:34
  159.1 14.5 %collective-permute-start.32 = (bf16[576,128]{1,0:T(8,128)(2,1)S(1)}, bf16[576,128]{1,0:T(8,128)(2,1)S(1)}, u32[]{:S(2)}, u32[]{:S(2)}) collective-permute-start(bf16[576,128]{1,0:T(8,128)(2,1)S(1)} %get-tuple-element.134), channel_id=1, source_target_pairs={{0,4},{4,0},{8,12},{12,8},{16,20},{20,16},{24,28},{28,24},{1,5},{5... | collective-permute-start | bytes 442376 | tf_op jit(solution)/shard_map/ppermute | solution.py:34
  161.1 9.1 %collective-permute-start.31 = (bf16[2,576,128]{2,1,0:T(8,128)(2,1)S(1)}, bf16[2,576,128]{2,1,0:T(8,128)(2,1)S(1)}, u32[]{:S(2)}, u32[]{:S(2)}) collective-permute-start(bf16[2,576,128]{2,1,0:T(8,128)(2,1)S(1)} %slice_bitcast_fusion), channel_id=1, source_target_pairs={{0,2},{1,3},{2,0},{3,1},{4,6},{5,7},{6,4},{7,5},{8,10},{9,11},{10,... | collective-permute-start | bytes 884744 | tf_op jit(solution)/shard_map/ppermute | solution.py:34
  162.4 11.2 %collective-permute-start.33 = (bf16[576,128]{1,0:T(8,128)(2,1)S(1)}, bf16[576,128]{1,0:T(8,128)(2,1)S(1)}, u32[]{:S(2)}, u32[]{:S(2)}) collective-permute-start(bf16[576,128]{1,0:T(8,128)(2,1)S(1)} %get-tuple-element.132), channel_id=1, source_target_pairs={{0,4},{4,0},{8,12},{12,8},{16,20},{20,16},{24,28},{28,24},{1,5},{5... | collective-permute-start | bytes 442376 | tf_op jit(solution)/shard_map/ppermute | solution.py:34
  170.3 5.2 %collective-permute-start.34 = (bf16[576,128]{1,0:T(8,128)(2,1)S(1)}, bf16[576,128]{1,0:T(8,128)(2,1)S(1)}, u32[]{:S(2)}, u32[]{:S(2)}) collective-permute-start(bf16[576,128]{1,0:T(8,128)(2,1)S(1)} %get-tuple-element.130), channel_id=1, source_target_pairs={{0,4},{4,0},{8,12},{12,8},{16,20},{20,16},{24,28},{28,24},{1,5},{5... | collective-permute-start | bytes 442376 | tf_op jit(solution)/shard_map/ppermute | solution.py:34
  (20 other events, 122.2 us)

commit v6 on v4

--- a/solution.py
+++ b/solution.py
@@ -17,7 +17,6 @@
 epsilon = 1e-08
 bf16 = jnp.bfloat16
 f32 = jnp.float32
-VMEM_LIMIT = 48 * 2**20
 
 
 def adamw_step(gradient, weight, moment1, moment2):
@@ -70,7 +69,7 @@
             out_specs=pl.BlockSpec((block, wide), lambda i, index: (i, 0)),
         ),
         out_shape=jax.ShapeDtypeStruct(rows.shape, rows.dtype),
-        compiler_params=params(),
+        compiler_params=params(4),
         cost_estimate=light(),
         name="reorder",
     )(index, rows)
@@ -98,7 +97,7 @@
         in_specs=[pl.BlockSpec(memory_space=pltpu.SMEM), pl.BlockSpec(memory_space=pltpu.VMEM)],
         out_shape=[shape, shape],
         scratch_shapes=[pltpu.VMEM((features, tok), bf16)],
-        compiler_params=params(),
+        compiler_params=params(12),
         cost_estimate=light(),
         name="split_features",
     )(starts, cotangent)
@@ -126,14 +125,14 @@
         in_specs=[pl.BlockSpec(memory_space=pltpu.SMEM)] + [vmem] * (2 * n),
         out_shape=jax.ShapeDtypeStruct((tok, 2 * n * own), bf16),
         scratch_shapes=[pltpu.VMEM((2 * n * own, tok), bf16)],
-        compiler_params=params(),
+        compiler_params=params(12),
         cost_estimate=light(),
         name="join_features",
     )(starts, *mine, *other)
 
 
-def params():
-    return pltpu.CompilerParams(vmem_limit_bytes=VMEM_LIMIT)
+def params(mib):
+    return pltpu.CompilerParams(vmem_limit_bytes=mib * 2**20)
 
 
 def cost(flops, bytes_accessed):
@@ -165,7 +164,7 @@
         in_specs=[pl.BlockSpec((1, part, tok), lambda i: (index, i, 0))] * 8 + [whole] * 2,
         out_specs=pl.BlockSpec((part, wide), lambda i: (i, 0)),
         out_shape=jax.ShapeDtypeStruct((own, wide), bf16),
-        compiler_params=params(),
+        compiler_params=params(12),
         cost_estimate=light(),
         name="gradient_part",
     )(*pieces, saved0, saved1)
@@ -205,7 +204,7 @@
         out_specs=[whole, whole],
         out_shape=[jax.ShapeDtypeStruct((rows, wide), f32), jax.ShapeDtypeStruct((rows, wide), bf16)],
         scratch_shapes=[pltpu.VMEM((2 * rows, wide), f32)],
-        compiler_params=params(),
+        compiler_params=params(24),
         cost_estimate=light(),
         name="attn_part",
     )(*pieces, weights)
@@ -229,7 +228,7 @@
     return pl.pallas_call(
         outward_kernel,
         out_shape=[shape, shape],
-        compiler_params=params(),
+        compiler_params=params(12),
         cost_estimate=cost(4 * own * rows * wide, 2 * (own * wide + 2 * rows * wide + 2 * own * rows)),
         name="outward_part",
     )(block, next0, next1)

time: 172 us -> 172 us (level)
  waiting for transfers between devices: 105 us -> 113 us
  Pallas kernels: 24 us -> 18.2 us
    ppermute x31, waiting for transfers between devices: 105 us -> 113 us  [flip(): lax.ppermute(value, axis, [(i, i ^ bit) for i in range(lax.axis_size(axis...]
    pallas_call x4, Pallas kernels: 7.46 us -> 3.83 us  [gradient_part(): pl.pallas_call(functools.partial(gradient_kernel, scale), grid=(steps,),...]
    pallas_call x1, Pallas kernels: 7.11 us -> 4.91 us  [attn_part(): pl.pallas_call(attn_kernel, grid=(n,), in_specs=[pl.BlockSpec((1, own, to...]
  transfers between devices with their start and end apart: 31 -> 31, of which waited for: 18 -> 18; matrix products, arithmetic and copies ran while one was open for 4% -> 3% of each run, Pallas kernels for 11% -> 7%
where the time goes in v6:
time: 172 us
  waiting for transfers between devices  113 us (66%)
  starting transfers between devices  26.6 us (15%)
  Pallas kernels  18.2 us (11%)
  other arithmetic  8.76 us (5%)
  local copies, waits for them, and re-layouts  4.25 us (2%)
    ppermute x31, waiting for transfers between devices, flip(): lax.ppermute(value, axis, [(i, i ^ bit) for i in range(lax.axis_size(axis...  113 us
    ppermute x31, starting transfers between devices, flip(): lax.ppermute(value, axis, [(i, i ^ bit) for i in range(lax.axis_size(axis...  26.6 us
    pallas_call x1, Pallas kernels, attn_part(): pl.pallas_call(attn_kernel, grid=(n,), in_specs=[pl.BlockSpec((1, own, to...  4.91 us
    pallas_call x4, Pallas kernels, gradient_part(): pl.pallas_call(functools.partial(gradient_kernel, scale), grid=(steps,),...  3.83 us
    convert_element_type x1, other arithmetic, adamw_step(): new_weight = (weight.astype(f32) * (1.0 - learning_rate * weight_decay) -...  3.59 us
  transfers between devices with their start and end apart: 31, of which 18 were waited for; matrix products, arithmetic and copies ran while one was open for 3% of the time, Pallas kernels for 7%

profile of v6, /device:TPU:0, one launch (start us, length us, event | category | flops | bytes accessed | tf_op | source)
XLA Modules:
  0.0 172.0 jit_solution(11407096159316506960)
XLA Ops:
  3.6 3.0 %collective-permute-start.2 = (bf16[4,576,128]{2,1,0:T(8,128)(2,1)S(1)}, bf16[4,576,128]{2,1,0:T(8,128)(2,1)S(1)}, u32[]{:S(2)}, u32[]{:S(2)}) collective-permute-start(bf16[4,576,128]{2,1,0:T(8,128)(2,1)S(1)} %get-tuple-element.61), channel_id=1, source_target_pairs={{0,4},{4,0},{8,12},{12,8},{16,20},{20,16},{24,28},{28,24},{1,5},{5... | collective-permute-start | bytes 1769480 | tf_op jit(solution)/shard_map/ppermute | solution.py:33
  6.7 1.5 collective-permute-start.3
  8.2 1.6 collective-permute-start
  9.8 2.6 %collective-permute-start.1 = (bf16[576,512]{1,0:T(8,128)(2,1)}, bf16[576,512]{1,0:T(8,128)(2,1)}, u32[]{:S(2)}, u32[]{:S(2)}) collective-permute-start(bf16[576,512]{1,0:T(8,128)(2,1)} %param.10), channel_id=1, source_target_pairs={{0,16},{4,20},{8,24},{12,28},{16,0},{20,4},{24,8},{28,12},{1,17},{... | collective-permute-start | bytes 1769480 | tf_op jit(solution)/shard_map/ppermute | solution.py:33
  13.1 6.9 %collective-permute-done.2.refs_4_ = bf16[4,576,128]{2,1,0:T(8,128)(2,1)S(1)} collective-permute-done((bf16[4,576,128]{2,1,0:T(8,128)(2,1)S(1)}, bf16[4,576,128]{2,1,0:T(8,128)(2,1)S(1)}, u32[]{:S(2)}, u32[]{:S(2)}) %collective-permute-start.2) | collective-permute-done | bytes 589856 | tf_op jit(solution)/shard_map/ppermute | solution.py:33
  20.0 2.4 %collective-permute-done.3.refs_1_ = bf16[4,576,128]{2,1,0:T(8,128)(2,1)S(1)} collective-permute-done((bf16[4,576,128]{2,1,0:T(8,128)(2,1)S(1)}, bf16[4,576,128]{2,1,0:T(8,128)(2,1)S(1)}, u32[]{:S(2)}, u32[]{:S(2)}) %collective-permute-start.3) | collective-permute-done | bytes 589856 | tf_op jit(solution)/shard_map/ppermute | solution.py:33
  22.7 1.7 %collective-permute-start.7 = (bf16[4,576,128]{2,1,0:T(8,128)(2,1)S(1)}, bf16[4,576,128]{2,1,0:T(8,128)(2,1)S(1)}, u32[]{:S(2)}, u32[]{:S(2)}) collective-permute-start(bf16[4,576,128]{2,1,0:T(8,128)(2,1)S(1)} %collective-permute-done.2.refs_4_), channel_id=1, source_target_pairs={{0,2},{1,3},{2,0},{3,1},{4,6},{5,7},{6,4},{7,5},{8,10},{9,11},{10,... | collective-permute-start | bytes 1769480 | tf_op jit(solution)/shard_map/ppermute | solution.py:33
  24.4 12.0 %collective-permute-done = bf16[576,512]{1,0:T(8,128)(2,1)} collective-permute-done((bf16[576,512]{1,0:T(8,128)(2,1)}, bf16[576,512]{1,0:T(8,128)(2,1)}, u32[]{:S(2)}, u32[]{:S(2)}) %collective-permute-start) | collective-permute-done | bytes 589856 | tf_op jit(solution)/shard_map/ppermute | solution.py:33
  36.5 2.4 %collective-permute-done.1 = bf16[576,512]{1,0:T(8,128)(2,1)} collective-permute-done((bf16[576,512]{1,0:T(8,128)(2,1)}, bf16[576,512]{1,0:T(8,128)(2,1)}, u32[]{:S(2)}, u32[]{:S(2)}) %collective-permute-start.1) | collective-permute-done | bytes 589856 | tf_op jit(solution)/shard_map/ppermute | solution.py:33
  38.9 2.0 %collective-permute-done.8.refs_3_ = bf16[4,576,128]{2,1,0:T(8,128)(2,1)S(1)} collective-permute-done((bf16[4,576,128]{2,1,0:T(8,128)(2,1)S(1)}, bf16[4,576,128]{2,1,0:T(8,128)(2,1)S(1)}, u32[]{:S(2)}, u32[]{:S(2)}) %collective-permute-start.8) | collective-permute-done | bytes 589856 | tf_op jit(solution)/shard_map/ppermute | solution.py:33
  41.4 1.4 collective-permute-done.9.refs_7_
  46.3 11.1 %collective-permute-done.10 = bf16[576,512]{1,0:T(8,128)(2,1)S(1)} collective-permute-done((bf16[576,512]{1,0:T(8,128)(2,1)}, bf16[576,512]{1,0:T(8,128)(2,1)S(1)}, u32[]{:S(2)}, u32[]{:S(2)}) %collective-permute-start.10) | collective-permute-done | bytes 589856 | tf_op jit(solution)/shard_map/ppermute | solution.py:33
  57.4 12.1 %collective-permute-done.11 = bf16[576,512]{1,0:T(8,128)(2,1)S(1)} collective-permute-done((bf16[576,512]{1,0:T(8,128)(2,1)S(1)}, bf16[576,512]{1,0:T(8,128)(2,1)S(1)}, u32[]{:S(2)}, u32[]{:S(2)}) %collective-permute-start.11) | collective-permute-done | bytes 589856 | tf_op jit(solution)/shard_map/ppermute | solution.py:33
  69.6 1.3 collective-permute-start.12
  71.0 1.7 %collective-permute-start.13 = (bf16[576,512]{1,0:T(8,128)(2,1)S(1)}, bf16[576,512]{1,0:T(8,128)(2,1)S(1)}, u32[]{:S(2)}, u32[]{:S(2)}) collective-permute-start(bf16[576,512]{1,0:T(8,128)(2,1)S(1)} %gradient_part.7), channel_id=1, source_target_pairs={{0,8},{4,12},{8,0},{12,4},{16,24},{20,28},{24,16},{28,20},{1,9},{5... | collective-permute-start | bytes 1769480 | tf_op jit(solution)/shard_map/ppermute | solution.py:33
  74.9 1.7 pad_maximum_fusion.refs_8_
  76.7 4.9 %attn_part.1 = (f32[512,512]{1,0:T(8,128)S(1)}, bf16[512,512]{1,0:T(8,128)(2,1)S(1)}) custom-call(bf16[4,576,128]{2,1,0:T(8,128)(2,1)S(1)} %get-tuple-element.60.refs_0_, bf16[4,576,128]{2,1,0:T(8,128)(2,1)S(1)} %collective-permute-done.3.refs_1_, bf16[4,576,128]{2,1,0:T(8,128)(2,1)S(1)} %collective-permute-done.4.refs_2_, ...), custom_call_target="tpu_custom_call" | custom-call | flops 1000000 | bytes 100000 | tf_op jit(solution)/shard_map/attn_part/pallas_call | solution.py:199
  81.6 4.7 %collective-permute-done.14.next1 = bf16[512,512]{1,0:T(8,128)(2,1)S(1)} collective-permute-done((bf16[512,512]{1,0:T(8,128)(2,1)S(1)}, bf16[512,512]{1,0:T(8,128)(2,1)S(1)}, u32[]{:S(2)}, u32[]{:S(2)}) %collective-permute-start.14) | collective-permute-done | bytes 524320 | tf_op jit(solution)/shard_map/ppermute | solution.py:33
  86.3 11.7 %collective-permute-done.12 = bf16[576,512]{1,0:T(8,128)(2,1)S(1)} collective-permute-done((bf16[576,512]{1,0:T(8,128)(2,1)S(1)}, bf16[576,512]{1,0:T(8,128)(2,1)S(1)}, u32[]{:S(2)}, u32[]{:S(2)}) %collective-permute-start.12) | collective-permute-done | bytes 589856 | tf_op jit(solution)/shard_map/ppermute | solution.py:33
  98.3 3.6 %subtract_convert_fusion = (bf16[576,512]{1,0:T(8,128)(2,1)S(1)}, f32[576,512]{1,0:T(8,128)}, f32[576,512]{1,0:T(8,128)}) fusion(bf16[576,512]{1,0:T(8,128)(2,1)} %param.10, bf16[576,512]{1,0:T(8,128)(2,1)S(1)} %collective-permute-done.13, bf16[576,512]{1,0:T(8,128)(2,1)S(1)} %collective-permute-done.12, bf16[576,512]{1,0:T(8,128)(2,1)S(1)} %gradient_part.4, ...), kind=kLoop, calls=%fused_computation.7 | loop fusion | flops 6193152 | bytes 7667712 | tf_op jit(solution)/shard_map/convert_element_type | solution.py:28
  103.0 2.5 %collective-permute-start.15 = (bf16[576,512]{1,0:T(8,128)(2,1)S(1)}, bf16[576,512]{1,0:T(8,128)(2,1)S(1)}, u32[]{:S(2)}, u32[]{:S(2)}) collective-permute-start(bf16[576,512]{1,0:T(8,128)(2,1)S(1)} %get-tuple-element.115.block), channel_id=1, source_target_pairs={{0,8},{4,12},{8,0},{12,4},{16,24},{20,28},{24,16},{28,20},{1,9},{5... | collective-permute-start | bytes 1769480 | tf_op jit(solution)/shard_map/ppermute | solution.py:33
  106.3 1.4 collective-permute-start.18
  107.6 24.2 %collective-permute-done.16.block = bf16[576,512]{1,0:T(8,128)(2,1)S(1)} collective-permute-done((bf16[576,512]{1,0:T(8,128)(2,1)S(1)}, bf16[576,512]{1,0:T(8,128)(2,1)S(1)}, u32[]{:S(2)}, u32[]{:S(2)}) %collective-permute-start.16) | collective-permute-done | bytes 589856 | tf_op jit(solution)/shard_map/ppermute | solution.py:33
  137.3 1.6 collective-permute-start.24
  139.5 9.1 %collective-permute-done.20.block = bf16[576,512]{1,0:T(8,128)(2,1)S(1)} collective-permute-done((bf16[576,512]{1,0:T(8,128)(2,1)S(1)}, bf16[576,512]{1,0:T(8,128)(2,1)S(1)}, u32[]{:S(2)}, u32[]{:S(2)}) %collective-permute-start.20) | collective-permute-done | bytes 589856 | tf_op jit(solution)/shard_map/ppermute | solution.py:33
  148.5 2.9 %collective-permute-done.24 = bf16[2,576,128]{2,1,0:T(8,128)(2,1)} collective-permute-done((bf16[2,576,128]{2,1,0:T(8,128)(2,1)}, bf16[2,576,128]{2,1,0:T(8,128)(2,1)}, u32[]{:S(2)}, u32[]{:S(2)}) %collective-permute-start.24) | collective-permute-done | bytes 294944 | tf_op jit(solution)/shard_map/ppermute | solution.py:33
  153.6 1.4 add_convert_fusion.6
  157.0 1.3 collective-permute-start.28
  158.4 6.4 %collective-permute-done.27 = bf16[2,576,128]{2,1,0:T(8,128)(2,1)S(1)} collective-permute-done((bf16[2,576,128]{2,1,0:T(8,128)(2,1)S(1)}, bf16[2,576,128]{2,1,0:T(8,128)(2,1)S(1)}, u32[]{:S(2)}, u32[]{:S(2)}) %collective-permute-start.27) | collective-permute-done | bytes 294944 | tf_op jit(solution)/shard_map/ppermute | solution.py:33
  165.6 1.9 %reorder.5 = bf16[512,512]{1,0:T(8,128)(2,1)} custom-call(s32[4]{0:T(128)S(1)} %pad_add_fusion.index, bf16[512,512]{1,0:T(8,128)(2,1)S(1)} %add_convert_fusion.5.rows), custom_call_target="tpu_custom_call" | custom-call | flops 1000000 | bytes 100000 | tf_op jit(solution)/shard_map/reorder/pallas_call | solution.py:63
  167.5 2.5 %collective-permute-done.30.refs_7_ = bf16[576,128]{1,0:T(8,128)(2,1)S(1)} collective-permute-done((bf16[576,128]{1,0:T(8,128)(2,1)S(1)}, bf16[576,128]{1,0:T(8,128)(2,1)S(1)}, u32[]{:S(2)}, u32[]{:S(2)}) %collective-permute-start.30) | collective-permute-done | bytes 147488 | tf_op jit(solution)/shard_map/ppermute | solution.py:33
  170.0 2.0 %join_features.1 = bf16[128,4608]{1,0:T(8,128)(2,1)} custom-call(s32[8]{0:T(128)S(1)} %pad_add_fusion.3.starts, bf16[576,128]{1,0:T(8,128)(2,1)S(1)} %get-tuple-element.106.refs_0_, bf16[576,128]{1,0:T(8,128)(2,1)S(1)} %get-tuple-element.129.refs_1_, bf16[576,128]{1,0:T(8,128)(2,1)S(1)} %get-tuple-element.127.refs_2_, ...), custom_call_target="tpu_custom_call" | custom-call | flops 1000000 | bytes 100000 | tf_op jit(solution)/shard_map/join_features/pallas_call | solution.py:123
  (93 shorter events, 23.3 us)
Async XLA Ops:
  3.6 16.4 %collective-permute-start.2 = (bf16[4,576,128]{2,1,0:T(8,128)(2,1)S(1)}, bf16[4,576,128]{2,1,0:T(8,128)(2,1)S(1)}, u32[]{:S(2)}, u32[]{:S(2)}) collective-permute-start(bf16[4,576,128]{2,1,0:T(8,128)(2,1)S(1)} %get-tuple-element.61), channel_id=1, source_target_pairs={{0,4},{4,0},{8,12},{12,8},{16,20},{20,16},{24,28},{28,24},{1,5},{5... | collective-permute-start | bytes 1769480 | tf_op jit(solution)/shard_map/ppermute | solution.py:33
  6.7 13.3 %collective-permute-start.4 = (bf16[4,576,128]{2,1,0:T(8,128)(2,1)S(1)}, bf16[4,576,128]{2,1,0:T(8,128)(2,1)S(1)}, u32[]{:S(2)}, u32[]{:S(2)}) collective-permute-start(bf16[4,576,128]{2,1,0:T(8,128)(2,1)S(1)} %get-tuple-element.60.refs_0_), channel_id=1, source_target_pairs={{0,1},{1,0},{2,3},{3,2},{4,5},{5,4},{6,7},{7,6},{8,9},{9,8},{10,11... | collective-permute-start | bytes 1769480 | tf_op jit(solution)/shard_map/ppermute | solution.py:33
  6.7 15.7 %collective-permute-start.3 = (bf16[4,576,128]{2,1,0:T(8,128)(2,1)S(1)}, bf16[4,576,128]{2,1,0:T(8,128)(2,1)S(1)}, u32[]{:S(2)}, u32[]{:S(2)}) collective-permute-start(bf16[4,576,128]{2,1,0:T(8,128)(2,1)S(1)} %get-tuple-element.60.refs_0_), channel_id=1, source_target_pairs={{0,2},{1,3},{2,0},{3,1},{4,6},{5,7},{6,4},{7,5},{8,10},{9,11},{10,... | collective-permute-start | bytes 1769480 | tf_op jit(solution)/shard_map/ppermute | solution.py:33
  8.2 28.3 %collective-permute-start = (bf16[576,512]{1,0:T(8,128)(2,1)}, bf16[576,512]{1,0:T(8,128)(2,1)}, u32[]{:S(2)}, u32[]{:S(2)}) collective-permute-start(bf16[576,512]{1,0:T(8,128)(2,1)} %param.10), channel_id=1, source_target_pairs={{0,8},{4,12},{8,0},{12,4},{16,24},{20,28},{24,16},{28,20},{1,9},{5... | collective-permute-start | bytes 1769480 | tf_op jit(solution)/shard_map/ppermute | solution.py:33
  9.8 29.1 %collective-permute-start.1 = (bf16[576,512]{1,0:T(8,128)(2,1)}, bf16[576,512]{1,0:T(8,128)(2,1)}, u32[]{:S(2)}, u32[]{:S(2)}) collective-permute-start(bf16[576,512]{1,0:T(8,128)(2,1)} %param.10), channel_id=1, source_target_pairs={{0,16},{4,20},{8,24},{12,28},{16,0},{20,4},{24,8},{28,12},{1,17},{... | collective-permute-start | bytes 1769480 | tf_op jit(solution)/shard_map/ppermute | solution.py:33
  22.4 16.4 %collective-permute-start.6 = (bf16[4,576,128]{2,1,0:T(8,128)(2,1)S(1)}, bf16[4,576,128]{2,1,0:T(8,128)(2,1)S(1)}, u32[]{:S(2)}, u32[]{:S(2)}) collective-permute-start(bf16[4,576,128]{2,1,0:T(8,128)(2,1)S(1)} %collective-permute-done.2.refs_4_), channel_id=1, source_target_pairs={{0,1},{1,0},{2,3},{3,2},{4,5},{5,4},{6,7},{7,6},{8,9},{9,8},{10,11... | collective-permute-start | bytes 1769480 | tf_op jit(solution)/shard_map/ppermute | solution.py:33
  22.4 16.4 %collective-permute-start.5 = (bf16[512,512]{1,0:T(8,128)(2,1)S(1)}, bf16[512,512]{1,0:T(8,128)(2,1)S(1)}, u32[]{:S(2)}, u32[]{:S(2)}) collective-permute-start(bf16[512,512]{1,0:T(8,128)(2,1)S(1)} %reorder.3.refs_8_), channel_id=1, source_target_pairs={{0,4},{4,0},{8,12},{12,8},{16,20},{20,16},{24,28},{28,24},{1,5},{5... | collective-permute-start | bytes 1572872 | tf_op jit(solution)/shard_map/ppermute | solution.py:33
  22.7 16.2 %collective-permute-start.7 = (bf16[4,576,128]{2,1,0:T(8,128)(2,1)S(1)}, bf16[4,576,128]{2,1,0:T(8,128)(2,1)S(1)}, u32[]{:S(2)}, u32[]{:S(2)}) collective-permute-start(bf16[4,576,128]{2,1,0:T(8,128)(2,1)S(1)} %collective-permute-done.2.refs_4_), channel_id=1, source_target_pairs={{0,2},{1,3},{2,0},{3,1},{4,6},{5,7},{6,4},{7,5},{8,10},{9,11},{10,... | collective-permute-start | bytes 1769480 | tf_op jit(solution)/shard_map/ppermute | solution.py:33
  38.9 2.0 %collective-permute-start.8 = (bf16[4,576,128]{2,1,0:T(8,128)(2,1)S(1)}, bf16[4,576,128]{2,1,0:T(8,128)(2,1)S(1)}, u32[]{:S(2)}, u32[]{:S(2)}) collective-permute-start(bf16[4,576,128]{2,1,0:T(8,128)(2,1)S(1)} %collective-permute-done.3.refs_1_), channel_id=1, source_target_pairs={{0,1},{1,0},{2,3},{3,2},{4,5},{5,4},{6,7},{7,6},{8,9},{9,8},{10,11... | collective-permute-start | bytes 1769480 | tf_op jit(solution)/shard_map/ppermute | solution.py:33
  40.9 2.0 %collective-permute-start.9 = (bf16[4,576,128]{2,1,0:T(8,128)(2,1)S(1)}, bf16[4,576,128]{2,1,0:T(8,128)(2,1)S(1)}, u32[]{:S(2)}, u32[]{:S(2)}) collective-permute-start(bf16[4,576,128]{2,1,0:T(8,128)(2,1)S(1)} %collective-permute-done.7.refs_5_), channel_id=1, source_target_pairs={{0,1},{1,0},{2,3},{3,2},{4,5},{5,4},{6,7},{7,6},{8,9},{9,8},{10,11... | collective-permute-start | bytes 1769480 | tf_op jit(solution)/shard_map/ppermute | solution.py:33
  41.0 16.4 %collective-permute-start.10 = (bf16[576,512]{1,0:T(8,128)(2,1)}, bf16[576,512]{1,0:T(8,128)(2,1)S(1)}, u32[]{:S(2)}, u32[]{:S(2)}) collective-permute-start(bf16[576,512]{1,0:T(8,128)(2,1)} %collective-permute-done.1), channel_id=1, source_target_pairs={{0,8},{4,12},{8,0},{12,4},{16,24},{20,28},{24,16},{28,20},{1,9},{5... | collective-permute-start | bytes 1769480 | tf_op jit(solution)/shard_map/ppermute | solution.py:33
  43.8 25.6 %collective-permute-start.11 = (bf16[576,512]{1,0:T(8,128)(2,1)S(1)}, bf16[576,512]{1,0:T(8,128)(2,1)S(1)}, u32[]{:S(2)}, u32[]{:S(2)}) collective-permute-start(bf16[576,512]{1,0:T(8,128)(2,1)S(1)} %gradient_part.6), channel_id=1, source_target_pairs={{0,8},{4,12},{8,0},{12,4},{16,24},{20,28},{24,16},{28,20},{1,9},{5... | collective-permute-start | bytes 1769480 | tf_op jit(solution)/shard_map/ppermute | solution.py:33
  69.6 28.4 %collective-permute-start.12 = (bf16[576,512]{1,0:T(8,128)(2,1)S(1)}, bf16[576,512]{1,0:T(8,128)(2,1)S(1)}, u32[]{:S(2)}, u32[]{:S(2)}) collective-permute-start(bf16[576,512]{1,0:T(8,128)(2,1)S(1)} %add_convert_fusion.4), channel_id=1, source_target_pairs={{0,16},{4,20},{8,24},{12,28},{16,0},{20,4},{24,8},{28,12},{1,17},{... | collective-permute-start | bytes 1769480 | tf_op jit(solution)/shard_map/ppermute | solution.py:33
  71.0 27.4 %collective-permute-start.13 = (bf16[576,512]{1,0:T(8,128)(2,1)S(1)}, bf16[576,512]{1,0:T(8,128)(2,1)S(1)}, u32[]{:S(2)}, u32[]{:S(2)}) collective-permute-start(bf16[576,512]{1,0:T(8,128)(2,1)S(1)} %gradient_part.7), channel_id=1, source_target_pairs={{0,8},{4,12},{8,0},{12,4},{16,24},{20,28},{24,16},{28,20},{1,9},{5... | collective-permute-start | bytes 1769480 | tf_op jit(solution)/shard_map/ppermute | solution.py:33
  73.4 59.5 %copy-start.4 = (bf16[512,512]{1,0:T(8,128)(2,1)}, bf16[512,512]{1,0:T(8,128)(2,1)S(1)}, u32[]{:S(2)}) copy-start(bf16[512,512]{1,0:T(8,128)(2,1)S(1)} %reorder.4.next0) | copy-start | bytes 1572868
  73.4 12.9 %collective-permute-start.14 = (bf16[512,512]{1,0:T(8,128)(2,1)S(1)}, bf16[512,512]{1,0:T(8,128)(2,1)S(1)}, u32[]{:S(2)}, u32[]{:S(2)}) collective-permute-start(bf16[512,512]{1,0:T(8,128)(2,1)S(1)} %reorder.4.next0), channel_id=1, source_target_pairs={{0,4},{4,0},{8,12},{12,8},{16,20},{20,16},{24,28},{28,24},{1,5},{5... | collective-permute-start | bytes 1572872 | tf_op jit(solution)/shard_map/ppermute | solution.py:33
  102.7 3.3 %collective-permute-start.17 = (bf16[2,2,576,128]{3,2,1,0:T(8,128)(2,1)S(1)}, bf16[2,2,576,128]{3,2,1,0:T(8,128)(2,1)S(1)}, u32[]{:S(2)}, u32[]{:S(2)}) collective-permute-start(bf16[2,2,576,128]{3,2,1,0:T(8,128)(2,1)S(1)} %get-tuple-element.88), channel_id=1, source_target_pairs={{0,1},{1,0},{2,3},{3,2},{4,5},{5,4},{6,7},{7,6},{8,9},{9,8},{10,11... | collective-permute-start | bytes 1769480 | tf_op jit(solution)/shard_map/ppermute | solution.py:33
  102.8 29.1 %collective-permute-start.16 = (bf16[576,512]{1,0:T(8,128)(2,1)S(1)}, bf16[576,512]{1,0:T(8,128)(2,1)S(1)}, u32[]{:S(2)}, u32[]{:S(2)}) collective-permute-start(bf16[576,512]{1,0:T(8,128)(2,1)S(1)} %get-tuple-element.115.block), channel_id=1, source_target_pairs={{0,16},{4,20},{8,24},{12,28},{16,0},{20,4},{24,8},{28,12},{1,17},{... | collective-permute-start | bytes 1769480 | tf_op jit(solution)/shard_map/ppermute | solution.py:33
  103.0 28.8 %collective-permute-start.15 = (bf16[576,512]{1,0:T(8,128)(2,1)S(1)}, bf16[576,512]{1,0:T(8,128)(2,1)S(1)}, u32[]{:S(2)}, u32[]{:S(2)}) collective-permute-start(bf16[576,512]{1,0:T(8,128)(2,1)S(1)} %get-tuple-element.115.block), channel_id=1, source_target_pairs={{0,8},{4,12},{8,0},{12,4},{16,24},{20,28},{24,16},{28,20},{1,9},{5... | collective-permute-start | bytes 1769480 | tf_op jit(solution)/shard_map/ppermute | solution.py:33
  105.5 26.3 %collective-permute-start.19 = (bf16[512,512]{1,0:T(8,128)(2,1)S(1)}, bf16[512,512]{1,0:T(8,128)(2,1)S(1)}, u32[]{:S(2)}, u32[]{:S(2)}) collective-permute-start(bf16[512,512]{1,0:T(8,128)(2,1)S(1)} %get-tuple-element.92), channel_id=1, source_target_pairs={{0,4},{4,0},{8,12},{12,8},{16,20},{20,16},{24,28},{28,24},{1,5},{5... | collective-permute-start | bytes 1572872 | tf_op jit(solution)/shard_map/ppermute | solution.py:33
  106.3 25.6 %collective-permute-start.18 = (bf16[2,576,128]{2,1,0:T(8,128)(2,1)S(1)}, bf16[2,576,128]{2,1,0:T(8,128)(2,1)S(1)}, u32[]{:S(2)}, u32[]{:S(2)}) collective-permute-start(bf16[2,576,128]{2,1,0:T(8,128)(2,1)S(1)} %get-tuple-element.122), channel_id=1, source_target_pairs={{0,2},{1,3},{2,0},{3,1},{4,6},{5,7},{6,4},{7,5},{8,10},{9,11},{10,... | collective-permute-start | bytes 884744 | tf_op jit(solution)/shard_map/ppermute | solution.py:33
  132.7 2.1 %collective-permute-start.21 = (bf16[2,2,576,128]{3,2,1,0:T(8,128)(2,1)S(1)}, bf16[2,2,576,128]{3,2,1,0:T(8,128)(2,1)S(1)}, u32[]{:S(2)}, u32[]{:S(2)}) collective-permute-start(bf16[2,2,576,128]{3,2,1,0:T(8,128)(2,1)S(1)} %get-tuple-element.96), channel_id=1, source_target_pairs={{0,1},{1,0},{2,3},{3,2},{4,5},{5,4},{6,7},{7,6},{8,9},{9,8},{10,11... | collective-permute-start | bytes 1769480 | tf_op jit(solution)/shard_map/ppermute | solution.py:33
  132.8 15.7 %collective-permute-start.20 = (bf16[576,512]{1,0:T(8,128)(2,1)S(1)}, bf16[576,512]{1,0:T(8,128)(2,1)S(1)}, u32[]{:S(2)}, u32[]{:S(2)}) collective-permute-start(bf16[576,512]{1,0:T(8,128)(2,1)S(1)} %collective-permute-done.16.block), channel_id=1, source_target_pairs={{0,8},{4,12},{8,0},{12,4},{16,24},{20,28},{24,16},{28,20},{1,9},{5... | collective-permute-start | bytes 1769480 | tf_op jit(solution)/shard_map/ppermute | solution.py:33
  133.7 2.6 %collective-permute-start.22 = (bf16[2,2,576,128]{3,2,1,0:T(8,128)(2,1)S(1)}, bf16[2,2,576,128]{3,2,1,0:T(8,128)(2,1)S(1)}, u32[]{:S(2)}, u32[]{:S(2)}) collective-permute-start(bf16[2,2,576,128]{3,2,1,0:T(8,128)(2,1)S(1)} %get-tuple-element.98), channel_id=1, source_target_pairs={{0,1},{1,0},{2,3},{3,2},{4,5},{5,4},{6,7},{7,6},{8,9},{9,8},{10,11... | collective-permute-start | bytes 1769480 | tf_op jit(solution)/shard_map/ppermute | solution.py:33
  135.8 12.7 %collective-permute-start.23 = (bf16[2,576,128]{2,1,0:T(8,128)(2,1)}, bf16[2,576,128]{2,1,0:T(8,128)(2,1)}, u32[]{:S(2)}, u32[]{:S(2)}) collective-permute-start(bf16[2,576,128]{2,1,0:T(8,128)(2,1)} %get-tuple-element.120), channel_id=1, source_target_pairs={{0,2},{1,3},{2,0},{3,1},{4,6},{5,7},{6,4},{7,5},{8,10},{9,11},{10,... | collective-permute-start | bytes 884744 | tf_op jit(solution)/shard_map/ppermute | solution.py:33
  137.3 14.2 %collective-permute-start.24 = (bf16[2,576,128]{2,1,0:T(8,128)(2,1)}, bf16[2,576,128]{2,1,0:T(8,128)(2,1)}, u32[]{:S(2)}, u32[]{:S(2)}) collective-permute-start(bf16[2,576,128]{2,1,0:T(8,128)(2,1)} %get-tuple-element.118), channel_id=1, source_target_pairs={{0,2},{1,3},{2,0},{3,1},{4,6},{5,7},{6,4},{7,5},{8,10},{9,11},{10,... | collective-permute-start | bytes 884744 | tf_op jit(solution)/shard_map/ppermute | solution.py:33
  138.9 9.6 %collective-permute-start.25 = (bf16[576,128]{1,0:T(8,128)(2,1)S(1)}, bf16[576,128]{1,0:T(8,128)(2,1)S(1)}, u32[]{:S(2)}, u32[]{:S(2)}) collective-permute-start(bf16[576,128]{1,0:T(8,128)(2,1)S(1)} %get-tuple-element.130), channel_id=1, source_target_pairs={{0,4},{4,0},{8,12},{12,8},{16,20},{20,16},{24,28},{28,24},{1,5},{5... | collective-permute-start | bytes 442376 | tf_op jit(solution)/shard_map/ppermute | solution.py:33
  153.4 2.1 %collective-permute-start.26 = (bf16[2,2,576,128]{3,2,1,0:T(8,128)(2,1)S(1)}, bf16[2,2,576,128]{3,2,1,0:T(8,128)(2,1)S(1)}, u32[]{:S(2)}, u32[]{:S(2)}) collective-permute-start(bf16[2,2,576,128]{3,2,1,0:T(8,128)(2,1)S(1)} %get-tuple-element.113), channel_id=1, source_target_pairs={{0,1},{1,0},{2,3},{3,2},{4,5},{5,4},{6,7},{7,6},{8,9},{9,8},{10,11... | collective-permute-start | bytes 1769480 | tf_op jit(solution)/shard_map/ppermute | solution.py:33
  155.6 9.1 %collective-permute-start.27 = (bf16[2,576,128]{2,1,0:T(8,128)(2,1)S(1)}, bf16[2,576,128]{2,1,0:T(8,128)(2,1)S(1)}, u32[]{:S(2)}, u32[]{:S(2)}) collective-permute-start(bf16[2,576,128]{2,1,0:T(8,128)(2,1)S(1)} %slice_bitcast_fusion), channel_id=1, source_target_pairs={{0,2},{1,3},{2,0},{3,1},{4,6},{5,7},{6,4},{7,5},{8,10},{9,11},{10,... | collective-permute-start | bytes 884744 | tf_op jit(solution)/shard_map/ppermute | solution.py:33
  156.2 11.3 %collective-permute-start.29 = (bf16[576,128]{1,0:T(8,128)(2,1)S(1)}, bf16[576,128]{1,0:T(8,128)(2,1)S(1)}, u32[]{:S(2)}, u32[]{:S(2)}) collective-permute-start(bf16[576,128]{1,0:T(8,128)(2,1)S(1)} %get-tuple-element.126), channel_id=1, source_target_pairs={{0,4},{4,0},{8,12},{12,8},{16,20},{20,16},{24,28},{28,24},{1,5},{5... | collective-permute-start | bytes 442376 | tf_op jit(solution)/shard_map/ppermute | solution.py:33
  157.0 10.5 %collective-permute-start.28 = (bf16[576,128]{1,0:T(8,128)(2,1)S(1)}, bf16[576,128]{1,0:T(8,128)(2,1)S(1)}, u32[]{:S(2)}, u32[]{:S(2)}) collective-permute-start(bf16[576,128]{1,0:T(8,128)(2,1)S(1)} %get-tuple-element.128), channel_id=1, source_target_pairs={{0,4},{4,0},{8,12},{12,8},{16,20},{20,16},{24,28},{28,24},{1,5},{5... | collective-permute-start | bytes 442376 | tf_op jit(solution)/shard_map/ppermute | solution.py:33
  164.8 5.2 %collective-permute-start.30 = (bf16[576,128]{1,0:T(8,128)(2,1)S(1)}, bf16[576,128]{1,0:T(8,128)(2,1)S(1)}, u32[]{:S(2)}, u32[]{:S(2)}) collective-permute-start(bf16[576,128]{1,0:T(8,128)(2,1)S(1)} %get-tuple-element.124), channel_id=1, source_target_pairs={{0,4},{4,0},{8,12},{12,8},{16,20},{20,16},{24,28},{28,24},{1,5},{5... | collective-permute-start | bytes 442376 | tf_op jit(solution)/shard_map/ppermute | solution.py:33
  (11 other events, 158.9 us)

commit v7 on v3

--- a/solution.py
+++ b/solution.py
@@ -17,7 +17,6 @@
 epsilon = 1e-08
 bf16 = jnp.bfloat16
 f32 = jnp.float32
-VMEM_LIMIT = 48 * 2**20
 
 
 def adamw_step(gradient, weight, moment1, moment2):
@@ -70,8 +69,8 @@
     return rows.reshape(4 * block, -1)
 
 
-def params():
-    return pltpu.CompilerParams(vmem_limit_bytes=VMEM_LIMIT)
+def params(mib):
+    return pltpu.CompilerParams(vmem_limit_bytes=mib * 2**20)
 
 
 def cost(flops, bytes_accessed):
@@ -99,7 +98,7 @@
         in_specs=[pl.BlockSpec((1, part, tok), lambda i: (index, i, 0))] * 8 + [whole] * 2,
         out_specs=pl.BlockSpec((part, wide), lambda i: (i, 0)),
         out_shape=jax.ShapeDtypeStruct((own, wide), bf16),
-        compiler_params=params(),
+        compiler_params=params(12),
         cost_estimate=cost(4 * own * rows * wide, 2 * own * (2 * rows + wide) + 4 * rows * wide),
         name="gradient_part",
     )(*pieces, saved0, saved1)
@@ -139,7 +138,7 @@
         out_specs=[whole, whole],
         out_shape=[jax.ShapeDtypeStruct((rows, wide), f32), jax.ShapeDtypeStruct((rows, wide), bf16)],
         scratch_shapes=[pltpu.VMEM((2 * rows, wide), f32)],
-        compiler_params=params(),
+        compiler_params=params(24),
         cost_estimate=cost(4 * n * own * rows * wide, 2 * n * own * (2 * rows + wide) + 6 * rows * wide),
         name="attn_part",
     )(*pieces, weights)
@@ -163,7 +162,7 @@
     return pl.pallas_call(
         outward_kernel,
         out_shape=[shape, shape],
-        compiler_params=params(),
+        compiler_params=params(12),
         cost_estimate=cost(4 * own * rows * wide, 2 * (own * wide + 2 * rows * wide + 2 * own * rows)),
         name="outward_part",
     )(block, next0, next1)

time: 172 us -> 170 us (0.988)
  waiting for transfers between devices: 107 us -> 113 us
  Pallas kernels: 17.8 us -> 12.2 us
    ppermute x31, waiting for transfers between devices: 107 us -> 113 us  [flip(): lax.ppermute(value, axis, [(i, i ^ bit) for i in range(lax.axis_size(axis...]
    pallas_call x4, Pallas kernels: 7.43 us -> 3.83 us  [gradient_part(): pl.pallas_call(functools.partial(gradient_kernel, scale), grid=(steps,),...]
    pallas_call x1, Pallas kernels: 7.1 us -> 5.12 us  [attn_part(): pl.pallas_call(attn_kernel, grid=(n,), in_specs=[pl.BlockSpec((1, own, to...]
  transfers between devices with their start and end apart: 31 -> 31, of which waited for: 17 -> 17; matrix products, arithmetic and copies ran while one was open for 4% -> 3% of each run, Pallas kernels for 8% -> 5%
where the time goes in v7:
time: 170 us
  waiting for transfers between devices  113 us (66%)
  starting transfers between devices  28.9 us (17%)
  Pallas kernels  12.2 us (7%)
  other arithmetic  7.96 us (5%)
  local copies, waits for them, and re-layouts  6.96 us (4%)
    ppermute x31, waiting for transfers between devices, flip(): lax.ppermute(value, axis, [(i, i ^ bit) for i in range(lax.axis_size(axis...  113 us
    ppermute x31, starting transfers between devices, flip(): lax.ppermute(value, axis, [(i, i ^ bit) for i in range(lax.axis_size(axis...  28.9 us
    pallas_call x1, Pallas kernels, attn_part(): pl.pallas_call(attn_kernel, grid=(n,), in_specs=[pl.BlockSpec((1, own, to...  5.12 us
    pallas_call x4, Pallas kernels, gradient_part(): pl.pallas_call(functools.partial(gradient_kernel, scale), grid=(steps,),...  3.83 us
  transfers between devices with their start and end apart: 31, of which 17 were waited for; matrix products, arithmetic and copies ran while one was open for 3% of the time, Pallas kernels for 5%

profile of v7, /device:TPU:0, one launch (start us, length us, event | category | flops | bytes accessed | tf_op | source)
XLA Modules:
  0.0 169.9 jit_solution(12757645455599454697)
XLA Ops:
  1.3 1.7 copy.18
  4.9 3.0 %collective-permute-start.2 = (bf16[4,576,128]{2,1,0:T(8,128)(2,1)}, bf16[4,576,128]{2,1,0:T(8,128)(2,1)S(1)}, u32[]{:S(2)}, u32[]{:S(2)}) collective-permute-start(bf16[4,576,128]{2,1,0:T(8,128)(2,1)} %get-tuple-element.59), channel_id=1, source_target_pairs={{0,4},{4,0},{8,12},{12,8},{16,20},{20,16},{24,28},{28,24},{1,5},{5... | collective-permute-start | bytes 1769480 | tf_op jit(solution)/shard_map/ppermute | solution.py:33
  7.9 1.5 collective-permute-start.3
  9.4 1.6 collective-permute-start
  10.9 2.6 %collective-permute-start.1 = (bf16[576,512]{1,0:T(8,128)(2,1)S(1)}, bf16[576,512]{1,0:T(8,128)(2,1)}, u32[]{:S(2)}, u32[]{:S(2)}) collective-permute-start(bf16[576,512]{1,0:T(8,128)(2,1)S(1)} %copy-done.1), channel_id=1, source_target_pairs={{0,16},{4,20},{8,24},{12,28},{16,0},{20,4},{24,8},{28,12},{1,17},{... | collective-permute-start | bytes 1769480 | tf_op jit(solution)/shard_map/ppermute | solution.py:33
  13.5 1.1 copy.19
  15.1 6.3 %collective-permute-done.2.refs_4_ = bf16[4,576,128]{2,1,0:T(8,128)(2,1)S(1)} collective-permute-done((bf16[4,576,128]{2,1,0:T(8,128)(2,1)}, bf16[4,576,128]{2,1,0:T(8,128)(2,1)S(1)}, u32[]{:S(2)}, u32[]{:S(2)}) %collective-permute-start.2) | collective-permute-done | bytes 589856 | tf_op jit(solution)/shard_map/ppermute | solution.py:33
  21.4 2.2 %collective-permute-done.3.refs_1_ = bf16[4,576,128]{2,1,0:T(8,128)(2,1)S(1)} collective-permute-done((bf16[4,576,128]{2,1,0:T(8,128)(2,1)S(1)}, bf16[4,576,128]{2,1,0:T(8,128)(2,1)S(1)}, u32[]{:S(2)}, u32[]{:S(2)}) %collective-permute-start.3) | collective-permute-done | bytes 589856 | tf_op jit(solution)/shard_map/ppermute | solution.py:33
  23.9 1.7 %collective-permute-start.7 = (bf16[4,576,128]{2,1,0:T(8,128)(2,1)S(1)}, bf16[4,576,128]{2,1,0:T(8,128)(2,1)S(1)}, u32[]{:S(2)}, u32[]{:S(2)}) collective-permute-start(bf16[4,576,128]{2,1,0:T(8,128)(2,1)S(1)} %collective-permute-done.2.refs_4_), channel_id=1, source_target_pairs={{0,2},{1,3},{2,0},{3,1},{4,6},{5,7},{6,4},{7,5},{8,10},{9,11},{10,... | collective-permute-start | bytes 1769480 | tf_op jit(solution)/shard_map/ppermute | solution.py:33
  25.6 11.7 %collective-permute-done = bf16[576,512]{1,0:T(8,128)(2,1)S(1)} collective-permute-done((bf16[576,512]{1,0:T(8,128)(2,1)S(1)}, bf16[576,512]{1,0:T(8,128)(2,1)S(1)}, u32[]{:S(2)}, u32[]{:S(2)}) %collective-permute-start) | collective-permute-done | bytes 589856 | tf_op jit(solution)/shard_map/ppermute | solution.py:33
  37.4 2.5 %collective-permute-done.1 = bf16[576,512]{1,0:T(8,128)(2,1)} collective-permute-done((bf16[576,512]{1,0:T(8,128)(2,1)S(1)}, bf16[576,512]{1,0:T(8,128)(2,1)}, u32[]{:S(2)}, u32[]{:S(2)}) %collective-permute-start.1) | collective-permute-done | bytes 589856 | tf_op jit(solution)/shard_map/ppermute | solution.py:33
  39.8 2.0 %collective-permute-done.8.refs_3_ = bf16[4,576,128]{2,1,0:T(8,128)(2,1)S(1)} collective-permute-done((bf16[4,576,128]{2,1,0:T(8,128)(2,1)S(1)}, bf16[4,576,128]{2,1,0:T(8,128)(2,1)S(1)}, u32[]{:S(2)}, u32[]{:S(2)}) %collective-permute-start.8) | collective-permute-done | bytes 589856 | tf_op jit(solution)/shard_map/ppermute | solution.py:33
  42.0 1.9 %collective-permute-done.9.refs_7_ = bf16[4,576,128]{2,1,0:T(8,128)(2,1)S(1)} collective-permute-done((bf16[4,576,128]{2,1,0:T(8,128)(2,1)S(1)}, bf16[4,576,128]{2,1,0:T(8,128)(2,1)S(1)}, u32[]{:S(2)}, u32[]{:S(2)}) %collective-permute-start.9) | collective-permute-done | bytes 589856 | tf_op jit(solution)/shard_map/ppermute | solution.py:33
  45.3 1.6 collective-permute-start.14
  48.8 12.2 %collective-permute-done.10 = bf16[576,512]{1,0:T(8,128)(2,1)S(1)} collective-permute-done((bf16[576,512]{1,0:T(8,128)(2,1)S(1)}, bf16[576,512]{1,0:T(8,128)(2,1)S(1)}, u32[]{:S(2)}, u32[]{:S(2)}) %collective-permute-start.10) | collective-permute-done | bytes 589856 | tf_op jit(solution)/shard_map/ppermute | solution.py:33
  62.2 2.1 %collective-permute-start.12 = (bf16[576,512]{1,0:T(8,128)(2,1)S(1)}, bf16[576,512]{1,0:T(8,128)(2,1)S(1)}, u32[]{:S(2)}, u32[]{:S(2)}) collective-permute-start(bf16[576,512]{1,0:T(8,128)(2,1)S(1)} %gradient_part.7), channel_id=1, source_target_pairs={{0,8},{4,12},{8,0},{12,4},{16,24},{20,28},{24,16},{28,20},{1,9},{5... | collective-permute-start | bytes 1769480 | tf_op jit(solution)/shard_map/ppermute | solution.py:33
  65.9 18.1 %collective-permute-done.14 = bf16[576,512]{1,0:T(8,128)(2,1)S(1)} collective-permute-done((bf16[576,512]{1,0:T(8,128)(2,1)}, bf16[576,512]{1,0:T(8,128)(2,1)S(1)}, u32[]{:S(2)}, u32[]{:S(2)}) %collective-permute-start.14) | collective-permute-done | bytes 589856 | tf_op jit(solution)/shard_map/ppermute | solution.py:33
  84.1 1.4 pad_maximum_fusion.refs_8_
  85.5 5.1 %attn_part.1 = (f32[512,512]{1,0:T(8,128)S(1)}, bf16[512,512]{1,0:T(8,128)(2,1)S(1)}) custom-call(bf16[4,576,128]{2,1,0:T(8,128)(2,1)S(1)} %get-tuple-element.58.refs_0_, bf16[4,576,128]{2,1,0:T(8,128)(2,1)S(1)} %collective-permute-done.3.refs_1_, bf16[4,576,128]{2,1,0:T(8,128)(2,1)S(1)} %collective-permute-done.4.refs_2_, ...), custom_call_target="tpu_custom_call" | custom-call | flops 2415919104 | bytes 8650752 | tf_op jit(solution)/shard_map/attn_part/pallas_call | solution.py:133
  90.6 7.5 %collective-permute-done.12 = bf16[576,512]{1,0:T(8,128)(2,1)S(1)} collective-permute-done((bf16[576,512]{1,0:T(8,128)(2,1)S(1)}, bf16[576,512]{1,0:T(8,128)(2,1)S(1)}, u32[]{:S(2)}, u32[]{:S(2)}) %collective-permute-start.12) | collective-permute-done | bytes 589856 | tf_op jit(solution)/shard_map/ppermute | solution.py:33
  98.2 2.5 %subtract_convert_fusion = (bf16[576,512]{1,0:T(8,128)(2,1)S(1)}, f32[576,512]{1,0:T(8,128)}, f32[576,512]{1,0:T(8,128)}) fusion(bf16[576,512]{1,0:T(8,128)(2,1)S(1)} %copy-done.1, bf16[576,512]{1,0:T(8,128)(2,1)S(1)} %collective-permute-done.12, bf16[576,512]{1,0:T(8,128)(2,1)S(1)} %collective-permute-done.11, bf16[576,512]{1,0:T(8,128)(2,1)S(1)} %gradient_part.4, ...), kind=kLoop, calls=%fused_computation.10 | loop fusion | flops 6193152 | bytes 7667712 | tf_op jit(solution)/shard_map/convert_element_type | solution.py:28
  101.6 1.4 collective-permute-start.16
  103.0 1.7 collective-permute-start.15
  105.4 1.5 collective-permute-start.18
  106.9 24.0 %collective-permute-done.16.block = bf16[576,512]{1,0:T(8,128)(2,1)S(1)} collective-permute-done((bf16[576,512]{1,0:T(8,128)(2,1)S(1)}, bf16[576,512]{1,0:T(8,128)(2,1)S(1)}, u32[]{:S(2)}, u32[]{:S(2)}) %collective-permute-start.16) | collective-permute-done | bytes 589856 | tf_op jit(solution)/shard_map/ppermute | solution.py:33
  136.5 1.1 collective-permute-start.25
  137.6 10.0 %collective-permute-done.20.block = bf16[576,512]{1,0:T(8,128)(2,1)S(1)} collective-permute-done((bf16[576,512]{1,0:T(8,128)(2,1)S(1)}, bf16[576,512]{1,0:T(8,128)(2,1)S(1)}, u32[]{:S(2)}, u32[]{:S(2)}) %collective-permute-start.20) | collective-permute-done | bytes 589856 | tf_op jit(solution)/shard_map/ppermute | solution.py:33
  147.7 1.9 %collective-permute-done.24 = bf16[2,576,128]{2,1,0:T(8,128)(2,1)S(1)} collective-permute-done((bf16[2,576,128]{2,1,0:T(8,128)(2,1)S(1)}, bf16[2,576,128]{2,1,0:T(8,128)(2,1)S(1)}, u32[]{:S(2)}, u32[]{:S(2)}) %collective-permute-start.24) | collective-permute-done | bytes 294944 | tf_op jit(solution)/shard_map/ppermute | solution.py:33
  151.3 1.5 collective-permute-start.28
  154.1 7.9 %collective-permute-done.27 = bf16[2,576,128]{2,1,0:T(8,128)(2,1)S(1)} collective-permute-done((bf16[2,576,128]{2,1,0:T(8,128)(2,1)S(1)}, bf16[2,576,128]{2,1,0:T(8,128)(2,1)S(1)}, u32[]{:S(2)}, u32[]{:S(2)}) %collective-permute-start.27) | collective-permute-done | bytes 294944 | tf_op jit(solution)/shard_map/ppermute | solution.py:33
  163.6 3.6 %collective-permute-done.30 = bf16[576,128]{1,0:T(8,128)(2,1)S(1)} collective-permute-done((bf16[576,128]{1,0:T(8,128)(2,1)S(1)}, bf16[576,128]{1,0:T(8,128)(2,1)S(1)}, u32[]{:S(2)}, u32[]{:S(2)}) %collective-permute-start.30) | collective-permute-done | bytes 147488 | tf_op jit(solution)/shard_map/ppermute | solution.py:33
  168.5 1.4 copy.24
  (90 shorter events, 22.5 us)
Async XLA Ops:
  4.9 16.5 %collective-permute-start.2 = (bf16[4,576,128]{2,1,0:T(8,128)(2,1)}, bf16[4,576,128]{2,1,0:T(8,128)(2,1)S(1)}, u32[]{:S(2)}, u32[]{:S(2)}) collective-permute-start(bf16[4,576,128]{2,1,0:T(8,128)(2,1)} %get-tuple-element.59), channel_id=1, source_target_pairs={{0,4},{4,0},{8,12},{12,8},{16,20},{20,16},{24,28},{28,24},{1,5},{5... | collective-permute-start | bytes 1769480 | tf_op jit(solution)/shard_map/ppermute | solution.py:33
  7.9 13.5 %collective-permute-start.4 = (bf16[4,576,128]{2,1,0:T(8,128)(2,1)S(1)}, bf16[4,576,128]{2,1,0:T(8,128)(2,1)S(1)}, u32[]{:S(2)}, u32[]{:S(2)}) collective-permute-start(bf16[4,576,128]{2,1,0:T(8,128)(2,1)S(1)} %get-tuple-element.58.refs_0_), channel_id=1, source_target_pairs={{0,1},{1,0},{2,3},{3,2},{4,5},{5,4},{6,7},{7,6},{8,9},{9,8},{10,11... | collective-permute-start | bytes 1769480 | tf_op jit(solution)/shard_map/ppermute | solution.py:33
  7.9 15.7 %collective-permute-start.3 = (bf16[4,576,128]{2,1,0:T(8,128)(2,1)S(1)}, bf16[4,576,128]{2,1,0:T(8,128)(2,1)S(1)}, u32[]{:S(2)}, u32[]{:S(2)}) collective-permute-start(bf16[4,576,128]{2,1,0:T(8,128)(2,1)S(1)} %get-tuple-element.58.refs_0_), channel_id=1, source_target_pairs={{0,2},{1,3},{2,0},{3,1},{4,6},{5,7},{6,4},{7,5},{8,10},{9,11},{10,... | collective-permute-start | bytes 1769480 | tf_op jit(solution)/shard_map/ppermute | solution.py:33
  9.4 28.0 %collective-permute-start = (bf16[576,512]{1,0:T(8,128)(2,1)S(1)}, bf16[576,512]{1,0:T(8,128)(2,1)S(1)}, u32[]{:S(2)}, u32[]{:S(2)}) collective-permute-start(bf16[576,512]{1,0:T(8,128)(2,1)S(1)} %copy-done.1), channel_id=1, source_target_pairs={{0,8},{4,12},{8,0},{12,4},{16,24},{20,28},{24,16},{28,20},{1,9},{5... | collective-permute-start | bytes 1769480 | tf_op jit(solution)/shard_map/ppermute | solution.py:33
  10.9 28.9 %collective-permute-start.1 = (bf16[576,512]{1,0:T(8,128)(2,1)S(1)}, bf16[576,512]{1,0:T(8,128)(2,1)}, u32[]{:S(2)}, u32[]{:S(2)}) collective-permute-start(bf16[576,512]{1,0:T(8,128)(2,1)S(1)} %copy-done.1), channel_id=1, source_target_pairs={{0,16},{4,20},{8,24},{12,28},{16,0},{20,4},{24,8},{28,12},{1,17},{... | collective-permute-start | bytes 1769480 | tf_op jit(solution)/shard_map/ppermute | solution.py:33
  23.6 16.2 %collective-permute-start.6 = (bf16[4,576,128]{2,1,0:T(8,128)(2,1)S(1)}, bf16[4,576,128]{2,1,0:T(8,128)(2,1)S(1)}, u32[]{:S(2)}, u32[]{:S(2)}) collective-permute-start(bf16[4,576,128]{2,1,0:T(8,128)(2,1)S(1)} %collective-permute-done.2.refs_4_), channel_id=1, source_target_pairs={{0,1},{1,0},{2,3},{3,2},{4,5},{5,4},{6,7},{7,6},{8,9},{9,8},{10,11... | collective-permute-start | bytes 1769480 | tf_op jit(solution)/shard_map/ppermute | solution.py:33
  23.6 16.2 %collective-permute-start.5 = (bf16[512,512]{1,0:T(8,128)(2,1)S(1)}, bf16[512,512]{1,0:T(8,128)(2,1)S(1)}, u32[]{:S(2)}, u32[]{:S(2)}) collective-permute-start(bf16[512,512]{1,0:T(8,128)(2,1)S(1)} %bitcast.65), channel_id=1, source_target_pairs={{0,4},{4,0},{8,12},{12,8},{16,20},{20,16},{24,28},{28,24},{1,5},{5... | collective-permute-start | bytes 1572872 | tf_op jit(solution)/shard_map/ppermute | solution.py:33
  23.9 16.0 %collective-permute-start.7 = (bf16[4,576,128]{2,1,0:T(8,128)(2,1)S(1)}, bf16[4,576,128]{2,1,0:T(8,128)(2,1)S(1)}, u32[]{:S(2)}, u32[]{:S(2)}) collective-permute-start(bf16[4,576,128]{2,1,0:T(8,128)(2,1)S(1)} %collective-permute-done.2.refs_4_), channel_id=1, source_target_pairs={{0,2},{1,3},{2,0},{3,1},{4,6},{5,7},{6,4},{7,5},{8,10},{9,11},{10,... | collective-permute-start | bytes 1769480 | tf_op jit(solution)/shard_map/ppermute | solution.py:33
  39.8 2.0 %collective-permute-start.8 = (bf16[4,576,128]{2,1,0:T(8,128)(2,1)S(1)}, bf16[4,576,128]{2,1,0:T(8,128)(2,1)S(1)}, u32[]{:S(2)}, u32[]{:S(2)}) collective-permute-start(bf16[4,576,128]{2,1,0:T(8,128)(2,1)S(1)} %collective-permute-done.3.refs_1_), channel_id=1, source_target_pairs={{0,1},{1,0},{2,3},{3,2},{4,5},{5,4},{6,7},{7,6},{8,9},{9,8},{10,11... | collective-permute-start | bytes 1769480 | tf_op jit(solution)/shard_map/ppermute | solution.py:33
  41.8 2.0 %collective-permute-start.9 = (bf16[4,576,128]{2,1,0:T(8,128)(2,1)S(1)}, bf16[4,576,128]{2,1,0:T(8,128)(2,1)S(1)}, u32[]{:S(2)}, u32[]{:S(2)}) collective-permute-start(bf16[4,576,128]{2,1,0:T(8,128)(2,1)S(1)} %collective-permute-done.7.refs_5_), channel_id=1, source_target_pairs={{0,1},{1,0},{2,3},{3,2},{4,5},{5,4},{6,7},{7,6},{8,9},{9,8},{10,11... | collective-permute-start | bytes 1769480 | tf_op jit(solution)/shard_map/ppermute | solution.py:33
  44.8 16.2 %collective-permute-start.10 = (bf16[576,512]{1,0:T(8,128)(2,1)S(1)}, bf16[576,512]{1,0:T(8,128)(2,1)S(1)}, u32[]{:S(2)}, u32[]{:S(2)}) collective-permute-start(bf16[576,512]{1,0:T(8,128)(2,1)S(1)} %gradient_part.6), channel_id=1, source_target_pairs={{0,8},{4,12},{8,0},{12,4},{16,24},{20,28},{24,16},{28,20},{1,9},{5... | collective-permute-start | bytes 1769480 | tf_op jit(solution)/shard_map/ppermute | solution.py:33
  45.3 38.8 %collective-permute-start.14 = (bf16[576,512]{1,0:T(8,128)(2,1)}, bf16[576,512]{1,0:T(8,128)(2,1)S(1)}, u32[]{:S(2)}, u32[]{:S(2)}) collective-permute-start(bf16[576,512]{1,0:T(8,128)(2,1)} %collective-permute-done.1), channel_id=1, source_target_pairs={{0,8},{4,12},{8,0},{12,4},{16,24},{20,28},{24,16},{28,20},{1,9},{5... | collective-permute-start | bytes 1769480 | tf_op jit(solution)/shard_map/ppermute | solution.py:33
  61.2 29.4 %collective-permute-start.11 = (bf16[576,512]{1,0:T(8,128)(2,1)S(1)}, bf16[576,512]{1,0:T(8,128)(2,1)S(1)}, u32[]{:S(2)}, u32[]{:S(2)}) collective-permute-start(bf16[576,512]{1,0:T(8,128)(2,1)S(1)} %add_convert_fusion.4), channel_id=1, source_target_pairs={{0,16},{4,20},{8,24},{12,28},{16,0},{20,4},{24,8},{28,12},{1,17},{... | collective-permute-start | bytes 1769480 | tf_op jit(solution)/shard_map/ppermute | solution.py:33
  62.2 35.9 %collective-permute-start.12 = (bf16[576,512]{1,0:T(8,128)(2,1)S(1)}, bf16[576,512]{1,0:T(8,128)(2,1)S(1)}, u32[]{:S(2)}, u32[]{:S(2)}) collective-permute-start(bf16[576,512]{1,0:T(8,128)(2,1)S(1)} %gradient_part.7), channel_id=1, source_target_pairs={{0,8},{4,12},{8,0},{12,4},{16,24},{20,28},{24,16},{28,20},{1,9},{5... | collective-permute-start | bytes 1769480 | tf_op jit(solution)/shard_map/ppermute | solution.py:33
  64.4 26.2 %collective-permute-start.13 = (bf16[512,512]{1,0:T(8,128)(2,1)S(1)}, bf16[512,512]{1,0:T(8,128)(2,1)S(1)}, u32[]{:S(2)}, u32[]{:S(2)}) collective-permute-start(bf16[512,512]{1,0:T(8,128)(2,1)S(1)} %bitcast.70), channel_id=1, source_target_pairs={{0,4},{4,0},{8,12},{12,8},{16,20},{20,16},{24,28},{28,24},{1,5},{5... | collective-permute-start | bytes 1572872 | tf_op jit(solution)/shard_map/ppermute | solution.py:33
  85.4 12.7 %copy-start.2 = (f32[576,512]{1,0:T(8,128)S(1)}, f32[576,512]{1,0:T(8,128)}, u32[]{:S(2)}) copy-start(f32[576,512]{1,0:T(8,128)} %param.13) | copy-start | bytes 3538948
  101.5 3.7 %collective-permute-start.17 = (bf16[2,2,576,128]{3,2,1,0:T(8,128)(2,1)S(1)}, bf16[2,2,576,128]{3,2,1,0:T(8,128)(2,1)S(1)}, u32[]{:S(2)}, u32[]{:S(2)}) collective-permute-start(bf16[2,2,576,128]{3,2,1,0:T(8,128)(2,1)S(1)} %get-tuple-element.83), channel_id=1, source_target_pairs={{0,1},{1,0},{2,3},{3,2},{4,5},{5,4},{6,7},{7,6},{8,9},{9,8},{10,11... | collective-permute-start | bytes 1769480 | tf_op jit(solution)/shard_map/ppermute | solution.py:33
  101.6 29.3 %collective-permute-start.16 = (bf16[576,512]{1,0:T(8,128)(2,1)S(1)}, bf16[576,512]{1,0:T(8,128)(2,1)S(1)}, u32[]{:S(2)}, u32[]{:S(2)}) collective-permute-start(bf16[576,512]{1,0:T(8,128)(2,1)S(1)} %get-tuple-element.110.block), channel_id=1, source_target_pairs={{0,16},{4,20},{8,24},{12,28},{16,0},{20,4},{24,8},{28,12},{1,17},{... | collective-permute-start | bytes 1769480 | tf_op jit(solution)/shard_map/ppermute | solution.py:33
  103.0 28.0 %collective-permute-start.15 = (bf16[576,512]{1,0:T(8,128)(2,1)S(1)}, bf16[576,512]{1,0:T(8,128)(2,1)S(1)}, u32[]{:S(2)}, u32[]{:S(2)}) collective-permute-start(bf16[576,512]{1,0:T(8,128)(2,1)S(1)} %get-tuple-element.110.block), channel_id=1, source_target_pairs={{0,8},{4,12},{8,0},{12,4},{16,24},{20,28},{24,16},{28,20},{1,9},{5... | collective-permute-start | bytes 1769480 | tf_op jit(solution)/shard_map/ppermute | solution.py:33
  104.7 26.3 %collective-permute-start.19 = (bf16[512,512]{1,0:T(8,128)(2,1)S(1)}, bf16[512,512]{1,0:T(8,128)(2,1)S(1)}, u32[]{:S(2)}, u32[]{:S(2)}) collective-permute-start(bf16[512,512]{1,0:T(8,128)(2,1)S(1)} %get-tuple-element.87), channel_id=1, source_target_pairs={{0,4},{4,0},{8,12},{12,8},{16,20},{20,16},{24,28},{28,24},{1,5},{5... | collective-permute-start | bytes 1572872 | tf_op jit(solution)/shard_map/ppermute | solution.py:33
  105.4 25.6 %collective-permute-start.18 = (bf16[2,576,128]{2,1,0:T(8,128)(2,1)S(1)}, bf16[2,576,128]{2,1,0:T(8,128)(2,1)S(1)}, u32[]{:S(2)}, u32[]{:S(2)}) collective-permute-start(bf16[2,576,128]{2,1,0:T(8,128)(2,1)S(1)} %get-tuple-element.123), channel_id=1, source_target_pairs={{0,2},{1,3},{2,0},{3,1},{4,6},{5,7},{6,4},{7,5},{8,10},{9,11},{10,... | collective-permute-start | bytes 884744 | tf_op jit(solution)/shard_map/ppermute | solution.py:33
  131.8 2.1 %collective-permute-start.21 = (bf16[2,2,576,128]{3,2,1,0:T(8,128)(2,1)S(1)}, bf16[2,2,576,128]{3,2,1,0:T(8,128)(2,1)S(1)}, u32[]{:S(2)}, u32[]{:S(2)}) collective-permute-start(bf16[2,2,576,128]{3,2,1,0:T(8,128)(2,1)S(1)} %get-tuple-element.91), channel_id=1, source_target_pairs={{0,1},{1,0},{2,3},{3,2},{4,5},{5,4},{6,7},{7,6},{8,9},{9,8},{10,11... | collective-permute-start | bytes 1769480 | tf_op jit(solution)/shard_map/ppermute | solution.py:33
  131.9 15.7 %collective-permute-start.20 = (bf16[576,512]{1,0:T(8,128)(2,1)S(1)}, bf16[576,512]{1,0:T(8,128)(2,1)S(1)}, u32[]{:S(2)}, u32[]{:S(2)}) collective-permute-start(bf16[576,512]{1,0:T(8,128)(2,1)S(1)} %collective-permute-done.16.block), channel_id=1, source_target_pairs={{0,8},{4,12},{8,0},{12,4},{16,24},{20,28},{24,16},{28,20},{1,9},{5... | collective-permute-start | bytes 1769480 | tf_op jit(solution)/shard_map/ppermute | solution.py:33
  133.1 2.1 %collective-permute-start.22 = (bf16[2,2,576,128]{3,2,1,0:T(8,128)(2,1)S(1)}, bf16[2,2,576,128]{3,2,1,0:T(8,128)(2,1)S(1)}, u32[]{:S(2)}, u32[]{:S(2)}) collective-permute-start(bf16[2,2,576,128]{3,2,1,0:T(8,128)(2,1)S(1)} %get-tuple-element.93), channel_id=1, source_target_pairs={{0,1},{1,0},{2,3},{3,2},{4,5},{5,4},{6,7},{7,6},{8,9},{9,8},{10,11... | collective-permute-start | bytes 1769480 | tf_op jit(solution)/shard_map/ppermute | solution.py:33
  134.1 13.6 %collective-permute-start.23 = (bf16[2,576,128]{2,1,0:T(8,128)(2,1)S(1)}, bf16[2,576,128]{2,1,0:T(8,128)(2,1)S(1)}, u32[]{:S(2)}, u32[]{:S(2)}) collective-permute-start(bf16[2,576,128]{2,1,0:T(8,128)(2,1)S(1)} %get-tuple-element.121), channel_id=1, source_target_pairs={{0,2},{1,3},{2,0},{3,1},{4,6},{5,7},{6,4},{7,5},{8,10},{9,11},{10,... | collective-permute-start | bytes 884744 | tf_op jit(solution)/shard_map/ppermute | solution.py:33
  135.4 14.1 %collective-permute-start.24 = (bf16[2,576,128]{2,1,0:T(8,128)(2,1)S(1)}, bf16[2,576,128]{2,1,0:T(8,128)(2,1)S(1)}, u32[]{:S(2)}, u32[]{:S(2)}) collective-permute-start(bf16[2,576,128]{2,1,0:T(8,128)(2,1)S(1)} %get-tuple-element.119), channel_id=1, source_target_pairs={{0,2},{1,3},{2,0},{3,1},{4,6},{5,7},{6,4},{7,5},{8,10},{9,11},{10,... | collective-permute-start | bytes 884744 | tf_op jit(solution)/shard_map/ppermute | solution.py:33
  136.5 11.2 %collective-permute-start.25 = (bf16[576,128]{1,0:T(8,128)(2,1)S(1)}, bf16[576,128]{1,0:T(8,128)(2,1)S(1)}, u32[]{:S(2)}, u32[]{:S(2)}) collective-permute-start(bf16[576,128]{1,0:T(8,128)(2,1)S(1)} %get-tuple-element.131), channel_id=1, source_target_pairs={{0,4},{4,0},{8,12},{12,8},{16,20},{20,16},{24,28},{28,24},{1,5},{5... | collective-permute-start | bytes 442376 | tf_op jit(solution)/shard_map/ppermute | solution.py:33
  150.4 2.5 %collective-permute-start.26 = (bf16[2,2,576,128]{3,2,1,0:T(8,128)(2,1)S(1)}, bf16[2,2,576,128]{3,2,1,0:T(8,128)(2,1)S(1)}, u32[]{:S(2)}, u32[]{:S(2)}) collective-permute-start(bf16[2,2,576,128]{3,2,1,0:T(8,128)(2,1)S(1)} %get-tuple-element.108), channel_id=1, source_target_pairs={{0,1},{1,0},{2,3},{3,2},{4,5},{5,4},{6,7},{7,6},{8,9},{9,8},{10,11... | collective-permute-start | bytes 1769480 | tf_op jit(solution)/shard_map/ppermute | solution.py:33
  150.6 13.0 %collective-permute-start.29 = (bf16[576,128]{1,0:T(8,128)(2,1)S(1)}, bf16[576,128]{1,0:T(8,128)(2,1)S(1)}, u32[]{:S(2)}, u32[]{:S(2)}) collective-permute-start(bf16[576,128]{1,0:T(8,128)(2,1)S(1)} %get-tuple-element.128), channel_id=1, source_target_pairs={{0,4},{4,0},{8,12},{12,8},{16,20},{20,16},{24,28},{28,24},{1,5},{5... | collective-permute-start | bytes 442376 | tf_op jit(solution)/shard_map/ppermute | solution.py:33
  151.3 12.3 %collective-permute-start.28 = (bf16[576,128]{1,0:T(8,128)(2,1)S(1)}, bf16[576,128]{1,0:T(8,128)(2,1)S(1)}, u32[]{:S(2)}, u32[]{:S(2)}) collective-permute-start(bf16[576,128]{1,0:T(8,128)(2,1)S(1)} %get-tuple-element.126), channel_id=1, source_target_pairs={{0,4},{4,0},{8,12},{12,8},{16,20},{20,16},{24,28},{28,24},{1,5},{5... | collective-permute-start | bytes 442376 | tf_op jit(solution)/shard_map/ppermute | solution.py:33
  153.0 8.9 %collective-permute-start.27 = (bf16[2,576,128]{2,1,0:T(8,128)(2,1)S(1)}, bf16[2,576,128]{2,1,0:T(8,128)(2,1)S(1)}, u32[]{:S(2)}, u32[]{:S(2)}) collective-permute-start(bf16[2,576,128]{2,1,0:T(8,128)(2,1)S(1)} %slice_bitcast_fusion), channel_id=1, source_target_pairs={{0,2},{1,3},{2,0},{3,1},{4,6},{5,7},{6,4},{7,5},{8,10},{9,11},{10,... | collective-permute-start | bytes 884744 | tf_op jit(solution)/shard_map/ppermute | solution.py:33
  162.1 5.2 %collective-permute-start.30 = (bf16[576,128]{1,0:T(8,128)(2,1)S(1)}, bf16[576,128]{1,0:T(8,128)(2,1)S(1)}, u32[]{:S(2)}, u32[]{:S(2)}) collective-permute-start(bf16[576,128]{1,0:T(8,128)(2,1)S(1)} %get-tuple-element.130), channel_id=1, source_target_pairs={{0,4},{4,0},{8,12},{12,8},{16,20},{20,16},{24,28},{28,24},{1,5},{5... | collective-permute-start | bytes 442376 | tf_op jit(solution)/shard_map/ppermute | solution.py:33
  (4 other events, 24.0 us)
